TPU v7x, 32 devices: a whole 2x2x4 slice. The times are simulated.
32 devices in a mesh: wide: 8 (over z, y), narrow: 4 (over x, core).
Axes of the slice: x: 2, y: 2, z: 4, core: 2. Of those that a mesh axis runs over, the one named last changes fastest.
Arguments:
- tokens: bfloat16 [32, 1600], P('wide'), may hold values from -48 to 48
- source: int32 [32], P('wide'), may hold values from 0 to 31, each once
- lengths: int32 [32], P('wide'), may hold values from 1 to 4096
- cached_key_rows: bfloat16 [32, 1024, 320], P('wide', 'narrow'), may hold values from -160 to 160
- cached_value_rows: bfloat16 [32, 1024, 320], P('wide', 'narrow'), may hold values from -6 to 6
- conv_state: bfloat16 [32, 3, 1600], P('wide', None, 'narrow'), may hold values from -6 to 6
- ssm_state: float32 [32, 16, 1600], P('wide', None, 'narrow'), may hold values from -6 to 6
- norm_gain: float32 [1600], replicated, may hold values from 0.1 to 1.9
- query_key_value_weight: bfloat16 [1600, 2240], P(None, 'narrow'), may hold values from -0.15625 to 0.15625
- w_xz: bfloat16 [1600, 2, 1600], P(None, None, 'narrow'), may hold values from -0.15625 to 0.15625
- conv_weight: float32 [4, 1600], P(None, 'narrow'), may hold values from -3 to 3
- conv_bias: float32 [1600], P('narrow'), may hold values from -3 to 3
- w_xproj: bfloat16 [1600, 132], P('narrow'), may hold values from -0.15625 to 0.15625
- w_dt: bfloat16 [100, 1600], P(None, 'narrow'), may hold values from -0.625 to 0.625
- dt_bias: float32 [1600], P('narrow'), may hold values from -4 to 0.5
- a_log: float32 [16, 1600], P(None, 'narrow'), may hold values from 0 to 2.77
- skip_d: float32 [1600], P('narrow'), may hold values from 0.5 to 2
- w_attn_out: bfloat16 [1600, 1600], P(None, 'narrow'), may hold values from -0.15625 to 0.15625
- w_ssm_out: bfloat16 [1600, 1600], P('narrow'), may hold values from -0.15625 to 0.15625
- gain_attn: float32 [1600], P('narrow'), may hold values from 0.1 to 1.9
- gain_ssm: float32 [1600], P('narrow'), may hold values from 0.1 to 1.9
Outputs:
- out: bfloat16 [32, 1600], P('wide', 'narrow')
- new_kv: bfloat16 [32, 640], P('wide')
- new_conv: bfloat16 [32, 3, 1600], P('wide', None, 'narrow')
- new_ssm: float32 [32, 16, 1600], P('wide', None, 'narrow')
Inputs may be any that keep to these rules, and one draw needn't show every extreme that they name: `source`: each of the 32 requests once.
All inputs are finite; a program needn't handle non-finite values.
Results may differ from a plain program's by a relative error of at most 0.005.
Values may be sent and summed in bfloat16 or wider, within the bound.
No kernel may reach another device: no remote copies, remote signals or barrier semaphores. Data moves between devices by JAX's collectives and lax.ppermute only.
A program may use at most 64 MiB of HBM per device.

v0:
```python
import jax
import jax.numpy as jnp
from jax import lax
from jax.sharding import PartitionSpec as P

MODEL_WIDTH = 1600
QUERY_HEADS = 25
KEY_VALUE_HEADS = 5
HEAD_SIZE = 64
WINDOW_LENGTH = 1024


EPSILON = 1e-06


def shards(
    tokens,
    source,
    lengths,
    cached_key_rows,
    cached_value_rows,
    conv_state,
    ssm_state,
    norm_gain,
    query_key_value_weight,
    w_xz,
    conv_weight,
    conv_bias,
    w_xproj,
    w_dt,
    dt_bias,
    a_log,
    skip_d,
    w_attn_out,
    w_ssm_out,
    gain_attn,
    gain_ssm,
):
    query_groups = QUERY_HEADS // KEY_VALUE_HEADS
    query_total_width = QUERY_HEADS * HEAD_SIZE
    key_value_width = KEY_VALUE_HEADS * HEAD_SIZE
    score_factor_scale = HEAD_SIZE ** (-0.5)
    local_row_count = tokens.shape[0]
    col_width = MODEL_WIDTH // lax.axis_size("narrow")
    col_start = lax.axis_index("narrow") * col_width
    arrived = lax.all_gather(tokens, "wide", axis=0, tiled=True)
    routed_full = jnp.take(arrived, source, axis=0).astype(jnp.float32)
    row_scale = lax.rsqrt(jnp.mean(routed_full * routed_full, axis=1) + EPSILON)
    normed = (routed_full * row_scale[:, None] * norm_gain).astype(jnp.bfloat16)
    routed_cols = lax.dynamic_slice_in_dim(routed_full, col_start, col_width, 1)
    head_part = jnp.dot(normed, query_key_value_weight, preferred_element_type=jnp.float32).astype(
        jnp.bfloat16
    )
    every_head = lax.all_gather(head_part, "narrow", axis=1, tiled=True)
    new_kv = every_head[:, query_total_width:]
    inner_weights = w_xz.reshape(w_xz.shape[0], -1)
    both_parts = jnp.dot(normed, inner_weights, preferred_element_type=jnp.float32).reshape(
        local_row_count, 2, -1
    )
    channel_in = both_parts[:, 0]
    gate_part = both_parts[:, 1]
    conv_out = (
        conv_bias
        + jnp.sum(conv_weight[:-1][None] * conv_state.astype(jnp.float32), axis=1)
        + conv_weight[-1] * channel_in
    )
    conv_act = jax.nn.silu(conv_out)
    new_conv = jnp.concatenate(
        [conv_state[:, 1:], channel_in.astype(jnp.bfloat16)[:, None]], axis=1
    )
    state_inputs = lax.psum(
        jnp.dot(conv_act.astype(jnp.bfloat16), w_xproj, preferred_element_type=jnp.float32),
        "narrow",
    )
    rank_width = w_dt.shape[0]
    state_width = (state_inputs.shape[1] - rank_width) // 2
    step_low = state_inputs[:, :rank_width]
    input_map = state_inputs[:, rank_width : rank_width + state_width]
    output_map = state_inputs[:, rank_width + state_width :]
    step_size = jax.nn.softplus(
        jnp.dot(step_low.astype(jnp.bfloat16), w_dt, preferred_element_type=jnp.float32) + dt_bias
    )
    decay_rate = jnp.exp(-step_size[:, None, :] * jnp.exp(a_log)[None])
    new_ssm = (
        decay_rate * ssm_state
        + step_size[:, None, :] * input_map[:, :, None] * conv_act[:, None, :]
    )
    state_out = jnp.sum(output_map[:, :, None] * new_ssm, axis=1) + skip_d * conv_act
    ssm_heads = (state_out * jax.nn.silu(gate_part)).astype(jnp.bfloat16)
    request_slot_count = cached_key_rows.shape[1]
    slot_index = lax.axis_index("narrow") * request_slot_count + lax.iota(
        jnp.int32, request_slot_count
    )
    length_col = lengths[:, None]
    live_slots = (slot_index[None] < length_col) & jnp.logical_not(
        (length_col >= WINDOW_LENGTH) & (slot_index[None] == length_col % WINDOW_LENGTH)
    )
    live_mask = live_slots[:, None, None, :]
    query_rows = every_head[:, :query_total_width].reshape(
        local_row_count, KEY_VALUE_HEADS, query_groups, HEAD_SIZE
    )
    current_key = every_head[:, query_total_width : query_total_width + key_value_width].reshape(
        local_row_count, KEY_VALUE_HEADS, HEAD_SIZE
    )
    current_value = every_head[:, query_total_width + key_value_width :].reshape(
        local_row_count, KEY_VALUE_HEADS, HEAD_SIZE
    )
    window_keys = cached_key_rows.reshape(
        local_row_count, request_slot_count, KEY_VALUE_HEADS, HEAD_SIZE
    )
    window_values = cached_value_rows.reshape(
        local_row_count, request_slot_count, KEY_VALUE_HEADS, HEAD_SIZE
    )
    score_all = (
        jnp.einsum("rgjd,rtgd->rgjt", query_rows, window_keys, preferred_element_type=jnp.float32)
        * score_factor_scale
    )
    current_score = (
        jnp.einsum("rgjd,rgd->rgj", query_rows, current_key, preferred_element_type=jnp.float32)
        * score_factor_scale
    )
    local_top = jnp.maximum(
        jnp.max(jnp.where(live_mask, score_all, -jnp.inf), axis=3), current_score
    )
    score_top = lax.pmax(local_top, "narrow")
    weights = jnp.where(live_mask, jnp.exp(score_all - score_top[..., None]), 0.0).astype(
        jnp.bfloat16
    )
    current_weight = jnp.exp(current_score - score_top).astype(jnp.bfloat16).astype(jnp.float32)
    weighted_numer = jnp.einsum(
        "rgjt,rtgd->rgjd", weights, window_values, preferred_element_type=jnp.float32
    ).reshape(local_row_count, query_total_width)
    denominator = jnp.sum(weights.astype(jnp.float32), axis=3).reshape(local_row_count, QUERY_HEADS)
    own_numer = (
        current_weight[..., None] * current_value.astype(jnp.float32)[:, :, None, :]
    ).reshape(local_row_count, query_total_width)
    own_denom = current_weight.reshape(local_row_count, QUERY_HEADS)
    summed_num, summed_den = lax.psum((weighted_numer, denominator), "narrow")
    total_num = summed_num + own_numer
    total_den = summed_den + own_denom
    attn_heads = (
        (total_num.reshape(local_row_count, QUERY_HEADS, HEAD_SIZE) / total_den[..., None])
        .reshape(local_row_count, query_total_width)
        .astype(jnp.bfloat16)
    )
    y_attn = jnp.dot(attn_heads, w_attn_out, preferred_element_type=jnp.float32)
    state_partial = jnp.dot(ssm_heads, w_ssm_out, preferred_element_type=jnp.float32)
    y_ssm = lax.psum_scatter(state_partial, "narrow", scatter_dimension=1, tiled=True)
    branch_sums = lax.psum(
        (jnp.sum(y_attn * y_attn, axis=1), jnp.sum(y_ssm * y_ssm, axis=1)), "narrow"
    )
    attn_scale = lax.rsqrt(branch_sums[0] / MODEL_WIDTH + EPSILON)
    state_scale = lax.rsqrt(branch_sums[1] / MODEL_WIDTH + EPSILON)
    mixed = 0.5 * (
        y_attn * attn_scale[:, None] * gain_attn + y_ssm * state_scale[:, None] * gain_ssm
    )
    out = (routed_cols + mixed).astype(jnp.bfloat16)
    return (out, new_kv, new_conv, new_ssm)


def solution(mesh):
    placed = (
        P("wide", None),
        P("wide"),
        P("wide"),
        P("wide", "narrow", None),
        P("wide", "narrow", None),
        P("wide", None, "narrow"),
        P("wide", None, "narrow"),
        P(),
        P(None, "narrow"),
        P(None, None, "narrow"),
        P(None, "narrow"),
        P("narrow"),
        P("narrow", None),
        P(None, "narrow"),
        P("narrow"),
        P(None, "narrow"),
        P("narrow"),
        P(None, "narrow"),
        P("narrow", None),
        P("narrow"),
        P("narrow"),
    )
    return jax.shard_map(
        shards,
        mesh=mesh,
        in_specs=placed,
        out_specs=(
            P("wide", "narrow"),
            P("wide", None),
            P("wide", None, "narrow"),
            P("wide", None, "narrow"),
        ),
        check_vma=False,
    )
```

profile of v0, /device:TPU:0, one launch (start us, length us, event | category | flops | bytes accessed | tf_op | source)
XLA Modules:
  0.0 131.3 jit_solution(17624521330117421058)
XLA Ops:
  7.3 0.8 compare_and_fusion
  8.1 0.7 compare_select_fusion.1
  8.7 1.2 broadcast_compare_fusion
  9.9 1.2 and_select_fusion
  11.1 32.6 %all-gather = bf16[8,4,1600]{2,1,0:T(4,128)(2,1)S(1)} all-gather(bf16[1,4,1600]{2,1,0:T(4,128)(2,1)} %bitcast.85), channel_id=1, replica_groups=mesh['wide'=8,'narrow'=4] {'wide'}, dimensions={0}, use_global_device_ids=true | all-gather | bytes 115200 | tf_op jit(solution)/shard_map/all_gather | solution.py:46
  44.5 2.1 %fusion.2 = bf16[1,560,4]{1,2,0:T(4,128)(2,1)S(1)} fusion(bf16[1600,560]{0,1:T(8,128)(2,1)} %param.29, f32[1600]{0:T(1024)} %param.28, f32[4]{0:T(128)S(1)} %add_rsqrt_fusion.2, bf16[4,1600]{1,0:T(4,128)(2,1)S(1)} %gather_fusion, pred[4]{0:T(512)(128)(4,1)S(1)} %compare_and_fusion), kind=kOutput, calls=%fused_computation.7 | convolution fusion | flops 7202240 | bytes 1815700 | tf_op jit(solution)/shard_map/dot_general | solution.py:51
  46.7 5.3 %all-gather.1 = bf16[4,560,4]{1,2,0:T(4,128)(2,1)S(1)} all-gather(bf16[1,560,4]{1,2,0:T(4,128)(2,1)S(1)} %fusion.2), channel_id=1, replica_groups=mesh['wide'=8,'narrow'=4] {'narrow'}, dimensions={0}, use_global_device_ids=true | all-gather | bytes 22400 | tf_op jit(solution)/shard_map/all_gather | solution.py:54
  53.9 0.6 exp.30
  54.6 0.7 reshape.203
  55.3 0.8 fusion
  56.2 0.6 fusion.15
  56.8 0.7 fusion.19
  57.5 0.8 reshape.177
  58.3 0.8 fusion.29
  59.2 0.7 not_and_fusion
  60.0 1.4 %select_reduce_fusion = (f32[4,5,5]{2,1,0:T(8,128)S(1)}, f32[4,5,5,256]{3,2,1,0:T(8,128)S(1)}) fusion(pred[4,256]{1,0:T(4,128)(4,1)S(1)} %not_and_fusion, bf16[4,5,5,64]{3,2,1,0:T(8,128)(2,1)S(1)} %reshape.177, bf16[4,256,5,64]{1,3,2,0:T(8,128)(2,1)} %bitcast.77), kind=kOutput, calls=%fused_computation.10 | convolution fusion | flops 3353500 | bytes 771984 | tf_op jit(solution)/shard_map/rgjd,rtgd->rgjt/dot_general | solution.py:115
  61.3 11.4 %pmax.7 = f32[4,5,5]{2,1,0:T(8,128)S(1)} all-reduce(f32[4,5,5]{2,1,0:T(8,128)S(1)} %fusion.5), channel_id=1, replica_groups=mesh['wide'=8,'narrow'=4] {'narrow'}, use_global_device_ids=true, to_apply=%region_2.3 | all-reduce | flops 100 | bytes 800 | tf_op jit(solution)/shard_map/pmax | solution.py:125
  72.7 0.9 convert_reduce_fusion
  73.6 1.7 %fusion.22 = f32[4,5,5,64]{3,2,1,0:T(8,128)} fusion(bf16[4,256,5,64]{1,3,2,0:T(8,128)(2,1)S(1)} %bitcast.76, f32[4,5,5,256]{3,2,1,0:T(8,128)S(1)} %get-tuple-element.16, f32[4,5,5]{2,1,0:T(8,128)S(1)} %pmax.7, pred[4,256]{1,0:T(4,128)(4,1)} %copy-done.12), kind=kOutput, calls=%fused_computation.51 | convolution fusion | flops 3353600 | bytes 784784 | tf_op jit(solution)/shard_map/rgjt,rtgd->rgjd/dot_general | solution.py:130
  75.3 1.0 reshape.181
  76.3 11.0 %all-reduce.1 = (f32[4,132]{1,0:T(4,128)S(1)}, f32[4,25]{1,0:T(4,128)S(1)}, f32[4,1600]{1,0:T(4,128)S(1)}) all-reduce(f32[4,132]{1,0:T(4,128)} %fusion.19, f32[4,25]{1,0:T(4,128)S(1)} %reshape.182, f32[4,1600]{1,0:T(4,128)S(1)} %reshape.181), channel_id=1, replica_groups=mesh['wide'=8,'narrow'=4] {'narrow'}, use_global_device_ids=true, to_apply=%region_9.10 | all-reduce | flops 7028 | bytes 56224 | tf_op jit(solution)/shard_map/psum | solution.py:71
  87.4 1.1 fusion.28
  88.5 1.7 %multiply_reduce_fusion = (f32[4,400]{1,0:T(4,128)S(1)}, f32[4,16,400]{2,1,0:T(8,128)}) fusion(f32[4,16]{1,0:T(4,128)S(1)} %get-tuple-element.14, f32[4,400]{1,0:T(4,128)} %fusion.15, f32[4,16]{1,0:T(4,128)S(1)} %get-tuple-element.13, f32[4,400]{1,0:T(4,128)S(1)} %get-tuple-element.18, f32[4,16,400]{2,1,0:T(8,128)} %param.27, f32[16,400]{1,0:T(8,128)} %exp.30, ...), kind=kLoop, calls=%fused_computation.11 | loop fusion | flops 177600 | bytes 256512 | tf_op jit(solution)/shard_map/reduce_sum | solution.py:88
  90.2 3.1 %convolution_bitcast_fusion = f32[1600,4]{1,0:T(8,128)} fusion(bf16[400,1600]{1,0:T(8,128)(2,1)} %param.39, f32[4,2,400]{2,0,1:T(4,128)} %copy-done.3, f32[4,400]{1,0:T(4,128)S(1)} %get-tuple-element.9, f32[400]{0:T(512)} %param.37, f32[4,400]{1,0:T(4,128)S(1)} %multiply_reduce_fusion.2, f32[400]{0:T(512)S(1)} %bitcast.84, f32[400]{0:T(512)S(1)} %copy-done.11), kind=kOutput, calls=%fused_computation.3 | convolution fusion | flops 5144000 | bytes 1336000
  93.3 0.7 slice.78
  94.6 1.9 %multiply_reduce_fusion.4 = (f32[4]{0:T(128)S(1)}, f32[4,400]{1,0:T(4,128)S(1)}) fusion(bf16[1600,400]{0,1:T(8,128)(2,1)} %param.38, f32[4,1600]{1,0:T(4,128)S(1)} %div.32, f32[4,1600]{1,0:T(4,128)S(1)} %get-tuple-element.8, f32[4,1600]{1,0:T(4,128)S(1)} %mul.203), kind=kOutput, calls=%fused_computation.41 | convolution fusion | flops 5142396 | bytes 1363216 | tf_op jit(solution)/shard_map/dot_general | solution.py:146
  96.5 0.6 pad_maximum_fusion
  97.1 1.4 %slice.59 = bf16[4,640]{1,0:T(4,128)(2,1)} slice(bf16[4,2240]{1,0:T(4,128)(2,1)} %bitcast.81), slice={[0:4], [1600:2240]} | slice | bytes 10240 | tf_op jit(solution)/shard_map/slice | solution.py:55
  98.5 18.3 %reduce-scatter.4.cloned.1.call-done = f32[400,4]{1,0:T(8,128)} async-done(((f32[1600,4]{1,0:T(8,128)}), f32[400,4]{1,0:T(8,128)}) %reduce-scatter.4.cloned.1.call-update) | async-done | bytes 6416
  116.8 1.0 copy.30
  118.0 5.8 %all-reduce = (f32[4]{0:T(128)S(1)}, f32[4]{0:T(128)S(1)}) all-reduce(f32[4]{0:T(128)S(1)} %multiply_reduce_fusion.3, f32[4]{0:T(128)S(1)} %get-tuple-element.19), channel_id=1, replica_groups=mesh['wide'=8,'narrow'=4] {'narrow'}, use_global_device_ids=true, to_apply=%region_13.14 | all-reduce | flops 8 | bytes 64 | tf_op jit(solution)/shard_map/psum | solution.py:149
  123.8 0.7 add_convert_fusion
  (68 shorter events, 3.8 us)
Async XLA Ops:
  7.2 48.1 %copy-start = (bf16[1600,2,400]{0,2,1:T(8,128)(2,1)S(1)}, bf16[1600,2,400]{0,2,1:T(8,128)(2,1)}, u32[]{:S(2)}) copy-start(bf16[1600,2,400]{0,2,1:T(8,128)(2,1)} %param.30) | copy-start | bytes 7680004
  7.2 48.1 %copy-start.8 = (f32[1600]{0:T(1024)S(1)}, f32[1600]{0:T(1024)}, u32[]{:S(2)}) copy-start(f32[1600]{0:T(1024)} %param.28) | copy-start | bytes 19204
  7.2 46.7 %copy-start.13 = (f32[4,400]{1,0:T(4,128)S(1)}, f32[4,400]{1,0:T(4,128)}, u32[]{:S(2)}) copy-start(f32[4,400]{1,0:T(4,128)} %param.31) | copy-start | bytes 19204
  7.2 46.7 %copy-start.9 = (f32[16,400]{1,0:T(8,128)S(1)}, f32[16,400]{1,0:T(8,128)}, u32[]{:S(2)}) copy-start(f32[16,400]{1,0:T(8,128)} %param.36) | copy-start | bytes 76804
  7.2 109.6 %reduce-scatter.4.cloned.1.call-start = ((), (), s32[]{:S(2)}) async-start(), calls=%async_computation.1 | async-start | bytes 1024000
  8.1 48.0 %copy-start.14 = (pred[4]{0:T(512)(128)(4,1)}, pred[4]{0:T(512)(128)(4,1)S(1)}, u32[]{:S(2)}) copy-start(pred[4]{0:T(512)(128)(4,1)S(1)} %compare_and_fusion) | copy-start | bytes 16
  46.6 9.5 %copy-start.7 = (bf16[4,3,400]{2,0,1:T(4,128)(2,1)S(1)}, bf16[4,3,400]{2,0,1:T(4,128)(2,1)}, u32[]{:S(2)}) copy-start(bf16[4,3,400]{2,0,1:T(4,128)(2,1)} %param.26) | copy-start | bytes 28804
  46.6 9.5 %copy-start.11 = (f32[400]{0:T(512)S(1)}, f32[400]{0:T(512)}, u32[]{:S(2)}) copy-start(f32[400]{0:T(512)} %param.32) | copy-start | bytes 4804
  46.7 10.1 %copy-start.2 = (bf16[400,132]{0,1:T(8,128)(2,1)S(1)}, bf16[400,132]{0,1:T(8,128)(2,1)}, u32[]{:S(2)}) copy-start(bf16[400,132]{0,1:T(8,128)(2,1)} %param.33) | copy-start | bytes 316804
  52.1 2.4 %copy-start.4 = (bf16[2240,4]{0,1:T(4,128)(2,1)}, bf16[2240,4]{0,1:T(4,128)(2,1)S(1)}, u32[]{:S(2)}) copy-start(bf16[2240,4]{0,1:T(4,128)(2,1)S(1)} %reshape.198) | copy-start | bytes 53764
  55.3 3.9 %copy-start.18 = (s32[256]{0:T(256)S(1)}, s32[256]{0:T(256)}, u32[]{:S(2)}) copy-start(s32[256]{0:T(256)} %iota_add_fusion) | copy-start | bytes 3076
  55.3 18.3 %copy-start.1 = (bf16[4,256,320]{1,2,0:T(8,128)(2,1)S(1)}, bf16[4,256,320]{1,2,0:T(8,128)(2,1)}, u32[]{:S(2)}) copy-start(bf16[4,256,320]{1,2,0:T(8,128)(2,1)} %param.25) | copy-start | bytes 1966084
  56.1 3.8 %copy-start.3 = (f32[4,2,400]{2,0,1:T(4,128)}, f32[4,2,400]{2,0,1:T(4,128)S(1)}, u32[]{:S(2)}) copy-start(f32[4,2,400]{2,0,1:T(4,128)S(1)} %fusion) | copy-start | bytes 38404
  59.2 2.1 %copy-start.5 = (f32[4,5,1,5]{3,2,1,0:T(1,128)}, f32[4,5,1,5]{3,2,1,0:T(1,128)S(1)}, u32[]{:S(2)}) copy-start(f32[4,5,1,5]{3,2,1,0:T(1,128)S(1)} %fusion.29) | copy-start | bytes 1204
  59.9 1.4 %copy-start.12 = (pred[4,256]{1,0:T(4,128)(4,1)}, pred[4,256]{1,0:T(4,128)(4,1)S(1)}, u32[]{:S(2)}) copy-start(pred[4,256]{1,0:T(4,128)(4,1)S(1)} %not_and_fusion) | copy-start | bytes 3076
  75.3 18.7 %copy-start.15 = (pred[4]{0:T(512)(128)(4,1)S(1)}, pred[4]{0:T(512)(128)(4,1)}, u32[]{:S(2)}) copy-start(pred[4]{0:T(512)(128)(4,1)} %copy-done.14) | copy-start | bytes 16
  75.3 18.8 %copy-start.6 = (f32[4,5,1,5]{3,2,1,0:T(1,128)S(1)}, f32[4,5,1,5]{3,2,1,0:T(1,128)}, u32[]{:S(2)}) copy-start(f32[4,5,1,5]{3,2,1,0:T(1,128)} %copy-done.5) | copy-start | bytes 1204
  75.3 18.8 %copy-start.10 = (f32[4,320]{1,0:T(4,128)S(1)}, f32[4,320]{1,0:T(4,128)}, u32[]{:S(2)}) copy-start(f32[4,320]{1,0:T(4,128)} %get-tuple-element.11) | copy-start | bytes 15364
  93.2 3.3 %slice-start = ((bf16[4,3,400]{2,0,1:T(4,128)(2,1)}), bf16[4,2,400]{2,0,1:T(4,128)(2,1)S(1)}, s32[]{:S(2)}) async-start(bf16[4,3,400]{2,0,1:T(4,128)(2,1)} %param.26), calls=%async_computation.2 | async-start | bytes 16384 | tf_op jit(solution)/shard_map/slice | solution.py:69
  93.2 30.5 %copy-start.16 = (f32[400]{0:T(512)S(1)}, f32[400]{0:T(512)}, u32[]{:S(2)}) copy-start(f32[400]{0:T(512)} %param.41) | copy-start | bytes 4804
  93.2 30.5 %copy-start.17 = (f32[400]{0:T(512)S(1)}, f32[400]{0:T(512)}, u32[]{:S(2)}) copy-start(f32[400]{0:T(512)} %param.40) | copy-start | bytes 4804
Sparse Core Ops, SparseCore 0:
  93.4 23.4 reduce-scatter.3
where the time goes:
time: 132 us; the launch traced here: 131 us
  blocking collectives  66 us (50%)
  waiting for transfers between devices  18.4 us (14%)
  between operations  14.3 us (11%)
  matrix products  13.6 us (10%)
  other arithmetic  10.8 us (8%)
  local copies, waits for them, and re-layouts  8.26 us (6%)
    all_gather x1, blocking collectives, shards(): arrived = lax.all_gather(tokens, 'wide', axis=0, tiled=True)  32.6 us
    unnamed x2, waiting for transfers between devices  18.4 us
    pmax x1, blocking collectives, shards(): score_top = lax.pmax(local_top, 'narrow')  11.4 us
    psum x1, blocking collectives, shards(): lax.psum(jnp.dot(conv_act.astype(jnp.bfloat16), w_xproj, preferred_elemen...  11 us
    psum x1, blocking collectives, shards(): lax.psum((jnp.sum(y_attn * y_attn, axis=1), jnp.sum(y_ssm * y_ssm, axis=1...  5.76 us
    all_gather x1, blocking collectives, shards(): every_head = lax.all_gather(head_part, 'narrow', axis=1, tiled=True)  5.32 us
    unnamed x1, matrix products  3.06 us
  transfers between devices with their start and end apart: 1, of which 1 were waited for; matrix products, arithmetic and copies ran while one was open for 4% of the time, Pallas kernels for 0%

commit v1 on v0

v1 whole, which is shorter than its diff:
```python
import jax
import jax.numpy as jnp
from jax import lax
from jax.sharding import PartitionSpec as P

MODEL_WIDTH = 1600
QUERY_HEADS = 25
KEY_VALUE_HEADS = 5
HEAD_SIZE = 64
WINDOW_LENGTH = 1024


EPSILON = 1e-06


def exchange(part, axis):
    size = lax.axis_size(axis)
    me = lax.axis_index(axis)
    pieces = [part] + [
        lax.ppermute(part, axis, [(i, (i + step) % size) for i in range(size)])
        for step in range(1, size)
    ]
    stacked = jnp.stack(pieces)
    return jnp.take(stacked, (me - jnp.arange(size)) % size, axis=0, mode="clip")


def exchange_sum(part, axis):
    size = lax.axis_size(axis)
    total = part
    for step in range(1, size):
        total = total + lax.ppermute(part, axis, [(i, (i + step) % size) for i in range(size)])
    return total


def shards(
    tokens,
    source,
    lengths,
    cached_key_rows,
    cached_value_rows,
    conv_state,
    ssm_state,
    norm_gain,
    query_key_value_weight,
    w_xz,
    conv_weight,
    conv_bias,
    w_xproj,
    w_dt,
    dt_bias,
    a_log,
    skip_d,
    w_attn_out,
    w_ssm_out,
    gain_attn,
    gain_ssm,
):
    query_groups = QUERY_HEADS // KEY_VALUE_HEADS
    query_total_width = QUERY_HEADS * HEAD_SIZE
    key_value_width = KEY_VALUE_HEADS * HEAD_SIZE
    score_factor_scale = HEAD_SIZE ** (-0.5)
    rows = tokens.shape[0]
    wide = lax.axis_size("wide")
    narrow = lax.axis_size("narrow")
    me = lax.axis_index("narrow")
    col_width = MODEL_WIDTH // narrow
    col_start = me * col_width

    arrived = lax.all_to_all(jnp.broadcast_to(tokens[None], (wide,) + tokens.shape), "wide", 0, 0)
    arrived = arrived.reshape(wide * rows, MODEL_WIDTH)
    routed_full = jnp.take(arrived, source, axis=0, mode="clip").astype(jnp.float32)
    row_scale = lax.rsqrt(jnp.mean(routed_full * routed_full, axis=1) + EPSILON)
    normed = (routed_full * row_scale[:, None] * norm_gain).astype(jnp.bfloat16)
    routed_cols = lax.dynamic_slice_in_dim(routed_full, col_start, col_width, 1)
    head_part = jnp.dot(normed, query_key_value_weight, preferred_element_type=jnp.float32).astype(
        jnp.bfloat16
    )
    inner_weights = w_xz.reshape(w_xz.shape[0], -1)
    both_parts = jnp.dot(normed, inner_weights, preferred_element_type=jnp.float32).reshape(
        rows, 2, -1
    )
    channel_in = both_parts[:, 0]
    gate_part = both_parts[:, 1]
    conv_out = (
        conv_bias
        + jnp.sum(conv_weight[:-1][None] * conv_state.astype(jnp.float32), axis=1)
        + conv_weight[-1] * channel_in
    )
    conv_act = jax.nn.silu(conv_out)
    new_conv = jnp.concatenate(
        [conv_state[:, 1:], channel_in.astype(jnp.bfloat16)[:, None]], axis=1
    )
    state_part = jnp.dot(conv_act.astype(jnp.bfloat16), w_xproj, preferred_element_type=jnp.float32)

    head_width = head_part.shape[1]
    first = exchange(jnp.concatenate([head_part.astype(jnp.float32), state_part], axis=1), "narrow")
    every_head = (
        first[:, :, :head_width].transpose(1, 0, 2).reshape(rows, -1).astype(jnp.bfloat16)
    )
    new_kv = every_head[:, query_total_width:]
    state_inputs = jnp.sum(first[:, :, head_width:], axis=0)

    rank_width = w_dt.shape[0]
    state_width = (state_inputs.shape[1] - rank_width) // 2
    step_low = state_inputs[:, :rank_width]
    input_map = state_inputs[:, rank_width : rank_width + state_width]
    output_map = state_inputs[:, rank_width + state_width :]
    step_size = jax.nn.softplus(
        jnp.dot(step_low.astype(jnp.bfloat16), w_dt, preferred_element_type=jnp.float32) + dt_bias
    )
    decay_rate = jnp.exp(-step_size[:, None, :] * jnp.exp(a_log)[None])
    new_ssm = (
        decay_rate * ssm_state
        + step_size[:, None, :] * input_map[:, :, None] * conv_act[:, None, :]
    )
    state_out = jnp.sum(output_map[:, :, None] * new_ssm, axis=1) + skip_d * conv_act
    ssm_heads = (state_out * jax.nn.silu(gate_part)).astype(jnp.bfloat16)
    state_partial = jnp.dot(ssm_heads, w_ssm_out, preferred_element_type=jnp.float32)

    request_slot_count = cached_key_rows.shape[1]
    slot_index = me * request_slot_count + lax.iota(jnp.int32, request_slot_count)
    length_col = lengths[:, None]
    live_slots = (slot_index[None] < length_col) & jnp.logical_not(
        (length_col >= WINDOW_LENGTH) & (slot_index[None] == length_col % WINDOW_LENGTH)
    )
    live_mask = live_slots[:, None, None, :]
    query_rows = every_head[:, :query_total_width].reshape(
        rows, KEY_VALUE_HEADS, query_groups, HEAD_SIZE
    )
    current_key = every_head[:, query_total_width : query_total_width + key_value_width].reshape(
        rows, KEY_VALUE_HEADS, HEAD_SIZE
    )
    current_value = every_head[:, query_total_width + key_value_width :].reshape(
        rows, KEY_VALUE_HEADS, HEAD_SIZE
    )
    window_keys = cached_key_rows.reshape(rows, request_slot_count, KEY_VALUE_HEADS, HEAD_SIZE)
    window_values = cached_value_rows.reshape(rows, request_slot_count, KEY_VALUE_HEADS, HEAD_SIZE)
    score_all = (
        jnp.einsum("rgjd,rtgd->rgjt", query_rows, window_keys, preferred_element_type=jnp.float32)
        * score_factor_scale
    )
    current_score = (
        jnp.einsum("rgjd,rgd->rgj", query_rows, current_key, preferred_element_type=jnp.float32)
        * score_factor_scale
    )
    local_top = jnp.maximum(
        jnp.max(jnp.where(live_mask, score_all, -jnp.inf), axis=3), current_score
    )
    weights = jnp.where(live_mask, jnp.exp(score_all - local_top[..., None]), 0.0).astype(
        jnp.bfloat16
    )
    numer = jnp.einsum(
        "rgjt,rtgd->rgjd", weights, window_values, preferred_element_type=jnp.float32
    ).reshape(rows, query_total_width)
    denom = jnp.sum(weights.astype(jnp.float32), axis=3).reshape(rows, QUERY_HEADS)

    second = exchange(
        jnp.concatenate([numer, state_partial, local_top.reshape(rows, -1), denom], axis=1),
        "narrow",
    )
    numers = second[:, :, :query_total_width]
    y_ssm = jnp.sum(second[:, :, query_total_width : query_total_width + MODEL_WIDTH], axis=0)
    stats = second[:, :, query_total_width + MODEL_WIDTH :]
    tops, denoms = stats[:, :, :QUERY_HEADS], stats[:, :, QUERY_HEADS:]
    top = jnp.max(tops, axis=0)
    factor = jnp.exp(tops - top[None])
    own = jnp.exp(current_score.reshape(rows, -1) - top).astype(jnp.bfloat16).astype(jnp.float32)
    total_den = jnp.sum(factor * denoms, axis=0) + own
    total_num = jnp.sum(
        factor[..., None] * numers.reshape(narrow, rows, QUERY_HEADS, HEAD_SIZE), axis=0
    ) + own[..., None] * jnp.repeat(current_value.astype(jnp.float32), query_groups, axis=1)
    attn_heads = (
        (total_num / total_den[..., None]).reshape(rows, query_total_width).astype(jnp.bfloat16)
    )
    y_attn = jnp.dot(attn_heads, w_attn_out, preferred_element_type=jnp.float32)

    attn_square = exchange_sum(jnp.sum(y_attn * y_attn, axis=1), "narrow")
    attn_scale = lax.rsqrt(attn_square / MODEL_WIDTH + EPSILON)
    state_scale = lax.rsqrt(jnp.mean(y_ssm * y_ssm, axis=1) + EPSILON)
    y_ssm_cols = lax.dynamic_slice_in_dim(y_ssm, col_start, col_width, 1)
    mixed = 0.5 * (
        y_attn * attn_scale[:, None] * gain_attn + y_ssm_cols * state_scale[:, None] * gain_ssm
    )
    out = (routed_cols + mixed).astype(jnp.bfloat16)
    return (out, new_kv, new_conv, new_ssm)


def solution(mesh):
    placed = (
        P("wide", None),
        P("wide"),
        P("wide"),
        P("wide", "narrow", None),
        P("wide", "narrow", None),
        P("wide", None, "narrow"),
        P("wide", None, "narrow"),
        P(),
        P(None, "narrow"),
        P(None, None, "narrow"),
        P(None, "narrow"),
        P("narrow"),
        P("narrow", None),
        P(None, "narrow"),
        P("narrow"),
        P(None, "narrow"),
        P("narrow"),
        P(None, "narrow"),
        P("narrow", None),
        P("narrow"),
        P("narrow"),
    )
    return jax.shard_map(
        shards,
        mesh=mesh,
        in_specs=placed,
        out_specs=(
            P("wide", "narrow"),
            P("wide", None),
            P("wide", None, "narrow"),
            P("wide", None, "narrow"),
        ),
        check_vma=False,
    )
```

time: 132 us -> 53.1 us (0.40)
  blocking collectives: 66 us -> 0 us
  between operations: 14.3 us -> 0.96 us
  starting transfers between devices: 0.04 us -> 12.7 us
  waiting for transfers between devices: 18.4 us -> 5.8 us
  matrix products: 13.6 us -> 10.2 us
  local copies, waits for them, and re-layouts: 8.26 us -> 11.4 us
    all_gather x2 -> x0, blocking collectives: 37.9 us -> none  [the longest x1 32.6 us: shards(): arrived = lax.all_gather(tokens, 'wide', axis=0, tiled=True)]
    unnamed x2 -> x0, waiting for transfers between devices: 18.4 us -> none
    psum x2 -> x0, blocking collectives: 16.8 us -> none  [the longest x1 11 us: shards(): lax.psum(jnp.dot(conv_act.astype(jnp.bfloat16), w_xproj, preferred_elemen...]
    pmax x1 -> x0, blocking collectives: 11.4 us -> none  [shards(): score_top = lax.pmax(local_top, 'narrow')]
    all_to_all x0 -> x1, starting transfers between devices: none -> 7.28 us  [shards(): lax.all_to_all(jnp.broadcast_to(tokens[None], (wide,) + tokens.shape), 'w...]
    ppermute x0 -> x9, starting transfers between devices: none -> 5.42 us  [the longest x3 2.74 us: exchange_sum(): lax.ppermute(part, axis, [(i, (i + step) % size) for i in range(size)])]
    ppermute x0 -> x9, waiting for transfers between devices: none -> 4.78 us  [the longest x3 2.82 us: exchange_sum(): lax.ppermute(part, axis, [(i, (i + step) % size) for i in range(size)])]
    unnamed x1 -> x0, matrix products: 3.06 us -> none
  transfers between devices with their start and end apart: 1 -> 10, of which waited for: 1 -> 7; matrix products, arithmetic and copies ran while one was open for 4% -> 21% of each run, Pallas kernels for 0% -> 0%
where the time goes in v1:
time: 53.1 us; the launch traced here: 52.2 us
  starting transfers between devices  12.7 us (24%)
  local copies, waits for them, and re-layouts  11.4 us (21%)
  other arithmetic  11.2 us (21%)
  matrix products  10.2 us (19%)
  waiting for transfers between devices  5.8 us (11%)
  between operations  0.96 us (2%)
    all_to_all x1, starting transfers between devices, shards(): lax.all_to_all(jnp.broadcast_to(tokens[None], (wide,) + tokens.shape), 'w...  7.28 us
    ppermute x3, waiting for transfers between devices, exchange_sum(): lax.ppermute(part, axis, [(i, (i + step) % size) for i in range(size)])  2.82 us
    ppermute x3, starting transfers between devices, exchange_sum(): lax.ppermute(part, axis, [(i, (i + step) % size) for i in range(size)])  2.74 us
    ppermute x6, starting transfers between devices, exchange(): lax.ppermute(part, axis, [(i, (i + step) % size) for i in range(size)])  2.68 us
    ppermute x6, waiting for transfers between devices, exchange(): lax.ppermute(part, axis, [(i, (i + step) % size) for i in range(size)])  1.96 us
    dot_general x1, matrix products, shards(): y_attn = jnp.dot(attn_heads, w_attn_out, preferred_element_type=jnp.float32)  1.91 us
    dot_general x1, matrix products, shards(): jnp.dot(ssm_heads, w_ssm_out, preferred_element_type=jnp.float32)  1.67 us
    reduce_sum x1, other arithmetic, shards(): jnp.sum(output_map[:, :, None] * new_ssm, axis=1) + skip_d * conv_act  1.66 us
  transfers between devices with their start and end apart: 10, of which 7 were waited for; matrix products, arithmetic and copies ran while one was open for 21% of the time, Pallas kernels for 0%

profile of v1, /device:TPU:0, one launch (start us, length us, event | category | flops | bytes accessed | tf_op | source)
XLA Modules:
  0.0 52.2 jit_solution(14178097464727945523)
XLA Ops:
  0.7 1.5 %broadcast_in_dim.25 = bf16[8,4,1600]{2,1,0:T(4,128)(2,1)} broadcast(bf16[4,1600]{1,0:T(4,128)(2,1)} %param.21), dimensions={1,2} | broadcast | bytes 115200 | tf_op jit(solution)/shard_map/broadcast_in_dim | solution.py:69
  2.2 7.3 %all-to-all-start = ((bf16[8,4,1600]{2,1,0:T(4,128)(2,1)}), bf16[8,4,1600]{2,1,0:T(4,128)(2,1)S(1)}, u32[]{:S(2)}, u32[]{:S(2)}) async-start(bf16[8,4,1600]{2,1,0:T(4,128)(2,1)} %broadcast_in_dim.25), calls=%async_computation | async-start | bytes 212992 | tf_op jit(solution)/shard_map/all_to_all | solution.py:69
  10.1 0.7 %and_select_fusion.1 = s32[4]{0:T(128)S(1)} fusion(s32[4]{0:T(128)} %param.23), kind=kLoop, calls=%fused_computation.69 | loop fusion | flops 44 | bytes 32 | tf_op jit(solution)/shard_map/jit(remainder)/select_n | solution.py:124
  10.8 0.7 %slice.60 = f32[1,400]{1,0:T(1,128)S(1)} slice(f32[4,400]{1,0:T(4,128)} %param.31), slice={[3:4], [0:400]} | slice | bytes 3200 | tf_op jit(solution)/shard_map/slice | solution.py:87
  11.5 0.7 %multiply_reduce_fusion.3 = f32[4,400]{1,0:T(4,128)S(1)} fusion(bf16[4,3,400]{2,0,1:T(4,128)(2,1)} %param.26, f32[3,400]{1,0:T(4,128)} %bitcast.79), kind=kLoop, calls=%fused_computation.25 | loop fusion | flops 12800 | bytes 20800 | tf_op jit(solution)/shard_map/reduce_sum | solution.py:86
  12.3 0.7 %pad_clamp_fusion.1 = s32[1024]{0:T(1024)S(1)} fusion(s32[4]{0:T(128)} %param.22), kind=kLoop, calls=%fused_computation.54 | loop fusion | flops 1024 | bytes 4112 | tf_op jit(solution)/shard_map/jit(_take)/gather | solution.py:71
  12.9 1.4 %exp.39 = f32[16,400]{1,0:T(8,128)} exponential(f32[16,400]{1,0:T(8,128)} %param.36) | non-fusion elementwise | bytes 51200 | tf_op jit(solution)/shard_map/exp | solution.py:111
  14.3 1.3 %not_and_fusion = pred[4,256]{1,0:T(4,128)(4,1)} fusion(s32[256]{0:T(256)S(1)} %iota_add_fusion, pred[4]{0:T(512)(128)(4,1)S(1)} %broadcast_compare_fusion, s32[4]{0:T(128)S(1)} %and_select_fusion.1, s32[4]{0:T(128)} %param.23), kind=kLoop, calls=%fused_computation.59 | loop fusion | flops 5120 | bytes 2084 | tf_op jit(solution)/shard_map/and | solution.py:123
  15.6 1.0 %all-to-all-done = bf16[8,4,1600]{2,1,0:T(4,128)(2,1)S(1)} async-done(((bf16[8,4,1600]{2,1,0:T(4,128)(2,1)}), bf16[8,4,1600]{2,1,0:T(4,128)(2,1)S(1)}, u32[]{:S(2)}, u32[]{:S(2)}) %all-to-all-start) | async-done | bytes 102432 | tf_op jit(solution)/shard_map/all_to_all | solution.py:69
  17.5 1.6 %fusion = f32[4,2,400]{2,0,1:T(4,128)S(1)} fusion(bf16[1600,2,400]{0,2,1:T(8,128)(2,1)S(1)} %copy-done, f32[1600]{0:T(1024)} %param.28, f32[4]{0:T(128)S(1)} %add_rsqrt_fusion.2, bf16[4,1600]{1,0:T(4,128)(2,1)S(1)} %gather_fusion), kind=kOutput, calls=%fused_computation.3 | convolution fusion | flops 10265600 | bytes 2592016 | tf_op jit(solution)/shard_map/dot_general | solution.py:79
  20.0 1.6 %collective-permute-start.1 = (f32[4,692]{1,0:T(4,128)S(1)}, f32[4,692]{1,0:T(4,128)S(1)}, u32[]{:S(2)}, u32[]{:S(2)}) collective-permute-start(f32[4,692]{1,0:T(4,128)S(1)} %pad_maximum_fusion.2), channel_id=1, source_target_pairs={{0,2},{1,3},{2,0},{3,1},{4,6},{5,7},{6,4},{7,5},{8,10},{9,11},{10,... | collective-permute-start | bytes 33224 | tf_op jit(solution)/shard_map/ppermute | solution.py:20
  23.0 0.7 %collective-permute-done.1 = f32[4,692]{1,0:T(4,128)S(1)} collective-permute-done((f32[4,692]{1,0:T(4,128)S(1)}, f32[4,692]{1,0:T(4,128)S(1)}, u32[]{:S(2)}, u32[]{:S(2)}) %collective-permute-start.1) | collective-permute-done | bytes 11104 | tf_op jit(solution)/shard_map/ppermute | solution.py:20
  23.8 0.9 %collective-permute-done = f32[4,692]{1,0:T(4,128)S(1)} collective-permute-done((f32[4,692]{1,0:T(4,128)S(1)}, f32[4,692]{1,0:T(4,128)S(1)}, u32[]{:S(2)}, u32[]{:S(2)}) %collective-permute-start) | collective-permute-done | bytes 11104 | tf_op jit(solution)/shard_map/ppermute | solution.py:20
  26.5 1.4 %select_reduce_fusion = (f32[4,5,5]{2,1,0:T(8,128)S(1)}, f32[4,5,5,256]{3,2,1,0:T(8,128)S(1)}) fusion(pred[4,256]{1,0:T(4,128)(4,1)} %not_and_fusion, bf16[4,5,5,64]{3,2,1,0:T(8,128)(2,1)S(1)} %reshape.245, bf16[4,256,5,64]{1,3,2,0:T(8,128)(2,1)} %bitcast.71), kind=kOutput, calls=%fused_computation.12 | convolution fusion | flops 3353500 | bytes 771984 | tf_op jit(solution)/shard_map/rgjd,rtgd->rgjt/dot_general | solution.py:139
  28.5 0.7 %reshape.250 = f32[4,25]{1,0:T(4,128)} reshape(f32[4,5,5]{2,1,0:T(8,128)S(1)} %get-tuple-element.15) | data formatting | bytes 800 | tf_op jit(solution)/shard_map/reshape | solution.py:158
  29.1 0.8 %convert_reduce_fusion = f32[4,5,5]{2,1,0:T(8,128)S(1)} fusion(f32[4,5,5,256]{3,2,1,0:T(8,128)S(1)} %get-tuple-element.19, f32[4,5,5]{2,1,0:T(8,128)S(1)} %get-tuple-element.15, pred[4,256]{1,0:T(4,128)(4,1)} %not_and_fusion), kind=kLoop, calls=%fused_computation.10 | loop fusion | flops 127900 | bytes 104224 | tf_op jit(solution)/shard_map/reduce_sum | solution.py:155
  30.0 1.6 %fusion.21 = f32[4,5,5,64]{3,2,1,0:T(8,128)} fusion(bf16[4,256,5,64]{1,3,2,0:T(8,128)(2,1)S(1)} %bitcast.70, f32[4,5,5,256]{3,2,1,0:T(8,128)S(1)} %get-tuple-element.19, f32[4,5,5]{2,1,0:T(8,128)S(1)} %get-tuple-element.15, pred[4,256]{1,0:T(4,128)(4,1)} %not_and_fusion), kind=kOutput, calls=%fused_computation.60 | convolution fusion | flops 3353600 | bytes 784784 | tf_op jit(solution)/shard_map/rgjt,rtgd->rgjd/dot_general | solution.py:152
  31.7 1.0 %reshape.249 = f32[4,1600]{1,0:T(4,128)S(1)} reshape(f32[4,5,5,64]{3,2,1,0:T(8,128)} %fusion.21) | data formatting | bytes 51200 | tf_op jit(solution)/shard_map/reshape | solution.py:154
  32.8 1.1 %fusion.32 = (f32[4,400]{1,0:T(4,128)S(1)}, f32[4,400]{1,0:T(4,128)S(1)}) fusion(f32[400]{0:T(512)} %param.35, bf16[100,400]{0,1:T(8,128)(2,1)} %param.34, f32[4,132]{1,0:T(4,128)S(1)} %slice_reduce_fusion.1), kind=kOutput, calls=%fused_computation.84 | convolution fusion | flops 332800 | bytes 95424 | tf_op jit(solution)/shard_map/dot_general | solution.py:109
  33.9 1.7 %multiply_reduce_fusion = (f32[4,400]{1,0:T(4,128)S(1)}, f32[4,16,400]{2,1,0:T(8,128)}) fusion(f32[4,16]{1,0:T(4,128)S(1)} %get-tuple-element.17, f32[4,400]{1,0:T(4,128)} %fusion.13, f32[4,16]{1,0:T(4,128)S(1)} %get-tuple-element.16, f32[4,400]{1,0:T(4,128)S(1)} %get-tuple-element.21, f32[4,16,400]{2,1,0:T(8,128)} %param.27, f32[16,400]{1,0:T(8,128)} %exp.39, ...), kind=kLoop, calls=%fused_computation.13 | loop fusion | flops 177600 | bytes 256512 | tf_op jit(solution)/shard_map/reduce_sum | solution.py:116
  35.5 1.7 %fusion.15 = f32[4,1600]{1,0:T(4,128)S(1)} fusion(bf16[400,1600]{1,0:T(8,128)(2,1)} %param.39, f32[4,2,400]{2,0,1:T(4,128)} %copy-done.4, f32[4,400]{1,0:T(4,128)S(1)} %get-tuple-element.10, f32[400]{0:T(512)} %param.37, f32[4,400]{1,0:T(4,128)S(1)} %multiply_reduce_fusion.3, f32[400]{0:T(512)S(1)} %bitcast.78, f32[400]{0:T(512)} %param.32), kind=kOutput, calls=%fused_computation.52 | convolution fusion | flops 5144000 | bytes 1336000 | tf_op jit(solution)/shard_map/dot_general | solution.py:118
  37.4 0.7 %collective-permute-start.4 = (f32[4,3250]{1,0:T(4,128)S(1)}, f32[4,3250]{1,0:T(4,128)S(1)}, u32[]{:S(2)}, u32[]{:S(2)}) collective-permute-start(f32[4,3250]{1,0:T(4,128)S(1)} %concatenate.10), channel_id=1, source_target_pairs={{0,2},{1,3},{2,0},{3,1},{4,6},{5,7},{6,4},{7,5},{8,10},{9,11},{10,... | collective-permute-start | bytes 156008 | tf_op jit(solution)/shard_map/ppermute | solution.py:20
  38.3 1.3 %pad_maximum_fusion.3 = bf16[4,3,400]{2,0,1:T(4,128)(2,1)} fusion(bf16[4,1,400]{2,0,1:T(4,128)(2,1)} %slice.129, bf16[4,2,400]{2,0,1:T(4,128)(2,1)S(1)} %slice-done), kind=kLoop, calls=%fused_computation.33 | loop fusion | flops 4800 | bytes 19200 | tf_op jit(solution)/shard_map/concatenate | solution.py:90
  39.6 1.4 %slice.97 = bf16[4,640]{1,0:T(4,128)(2,1)} slice(bf16[4,2240]{1,0:T(4,128)(2,1)} %copy-done.5), slice={[0:4], [1600:2240]} | slice | bytes 10240 | tf_op jit(solution)/shard_map/slice | solution.py:100
  41.0 0.8 %reshape.254 = f32[4,5,64]{2,1,0:T(8,128)S(1)} reshape(f32[4,320]{1,0:T(4,128)} %get-tuple-element.12) | data formatting | bytes 10240 | tf_op jit(solution)/shard_map/convert_element_type | solution.py:171
  42.3 0.8 %gather_fusion.2 = f32[4,4,3250]{2,1,0:T(4,128)S(1)} fusion(f32[4,4,3250]{2,1,0:T(4,128)S(1)} %pad_maximum_fusion, s32[1024]{0:T(1024)} %copy-done.10), kind=kCustom, calls=%fused_computation.2 | custom fusion | bytes 416016 | tf_op jit(solution)/shard_map/jit(_take)/gather | solution.py:24
  43.9 1.9 %multiply_reduce_fusion.4 = (f32[4]{0:T(128)S(1)}, f32[4,400]{1,0:T(4,128)S(1)}) fusion(bf16[1600,400]{0,1:T(8,128)(2,1)} %param.38, f32[4,1600]{1,0:T(4,128)S(1)} %div.35, f32[4,1600]{1,0:T(4,128)S(1)} %get-tuple-element.4, f32[4,1600]{1,0:T(4,128)S(1)} %mul.237, f32[4,1600]{1,0:T(4,128)S(1)} %reshape.253), kind=kOutput, calls=%fused_computation.46 | convolution fusion | flops 5148796 | bytes 1388816 | tf_op jit(solution)/shard_map/dot_general | solution.py:175
  45.8 1.4 %collective-permute-start.8 = (f32[4]{0:T(128)S(1)}, f32[4]{0:T(128)S(1)}, u32[]{:S(2)}, u32[]{:S(2)}) collective-permute-start(f32[4]{0:T(128)S(1)} %get-tuple-element.22), channel_id=1, source_target_pairs={{0,3},{1,0},{2,1},{3,2},{4,7},{5,4},{6,5},{7,6},{8,11},{9,8},{10,9... | collective-permute-start | bytes 56 | tf_op jit(solution)/shard_map/ppermute | solution.py:31
  47.2 1.4 %collective-permute-start.7 = (f32[4]{0:T(128)S(1)}, f32[4]{0:T(128)S(1)}, u32[]{:S(2)}, u32[]{:S(2)}) collective-permute-start(f32[4]{0:T(128)S(1)} %get-tuple-element.22), channel_id=1, source_target_pairs={{0,2},{1,3},{2,0},{3,1},{4,6},{5,7},{6,4},{7,5},{8,10},{9,11},{10,... | collective-permute-start | bytes 56 | tf_op jit(solution)/shard_map/ppermute | solution.py:31
  48.7 2.0 %collective-permute-done.7 = f32[4]{0:T(128)S(1)} collective-permute-done((f32[4]{0:T(128)S(1)}, f32[4]{0:T(128)S(1)}, u32[]{:S(2)}, u32[]{:S(2)}) %collective-permute-start.7) | collective-permute-done | bytes 48 | tf_op jit(solution)/shard_map/ppermute | solution.py:31
  50.8 0.8 %collective-permute-done.6 = f32[4]{0:T(128)S(1)} collective-permute-done((f32[4]{0:T(128)S(1)}, f32[4]{0:T(128)S(1)}, u32[]{:S(2)}, u32[]{:S(2)}) %collective-permute-start.6) | collective-permute-done | bytes 48 | tf_op jit(solution)/shard_map/ppermute | solution.py:31
  51.6 0.7 %add_convert_fusion = bf16[4,400]{1,0:T(4,128)(2,1)} fusion(f32[4,1600]{1,0:T(4,128)S(1)} %get-tuple-element.5, s32[]{:T(128)S(6)} %select_n.38, f32[4,400]{1,0:T(4,128)S(1)} %get-tuple-element.23, f32[4,1600]{1,0:T(4,128)S(1)} %convert_element_type.71, f32[400]{0:T(512)S(1)} %copy-done.11, f32[4]{0:T(128)S(1)} %add_rsqrt_fusion, f32[400]{0:T(512)S(1)} %copy-done.12, ...), kind=kLoop, calls=%fused_computation.45 | loop fusion | flops 12800 | bytes 25636 | tf_op jit(solution)/shard_map/convert_element_type | solution.py:184
  (85 shorter events, 8.1 us)
Async XLA Ops:
  0.6 16.8 %copy-start = (bf16[1600,2,400]{0,2,1:T(8,128)(2,1)S(1)}, bf16[1600,2,400]{0,2,1:T(8,128)(2,1)}, u32[]{:S(2)}) copy-start(bf16[1600,2,400]{0,2,1:T(8,128)(2,1)} %param.30) | copy-start | bytes 7680004
  0.6 18.4 %copy-start.7 = (f32[1600]{0:T(1024)S(1)}, f32[1600]{0:T(1024)}, u32[]{:S(2)}) copy-start(f32[1600]{0:T(1024)} %param.28) | copy-start | bytes 19204
  2.2 14.5 %all-to-all-start = ((bf16[8,4,1600]{2,1,0:T(4,128)(2,1)}), bf16[8,4,1600]{2,1,0:T(4,128)(2,1)S(1)}, u32[]{:S(2)}, u32[]{:S(2)}) async-start(bf16[8,4,1600]{2,1,0:T(4,128)(2,1)} %broadcast_in_dim.25), calls=%async_computation | async-start | bytes 212992 | tf_op jit(solution)/shard_map/all_to_all | solution.py:69
  12.9 11.8 %copy-start.10 = (s32[1024]{0:T(1024)}, s32[1024]{0:T(1024)S(1)}, u32[]{:S(2)}) copy-start(s32[1024]{0:T(1024)S(1)} %pad_clamp_fusion) | copy-start | bytes 12292
  17.3 1.8 %copy-start.1 = (bf16[1600,560]{0,1:T(8,128)(2,1)S(1)}, bf16[1600,560]{0,1:T(8,128)(2,1)}, u32[]{:S(2)}) copy-start(bf16[1600,560]{0,1:T(8,128)(2,1)} %param.29) | copy-start | bytes 5376004
  17.4 2.3 %copy-start.3 = (bf16[400,132]{0,1:T(8,128)(2,1)S(1)}, bf16[400,132]{0,1:T(8,128)(2,1)}, u32[]{:S(2)}) copy-start(bf16[400,132]{0,1:T(8,128)(2,1)} %param.33) | copy-start | bytes 316804
  17.4 2.3 %copy-start.8 = (f32[400]{0:T(512)S(1)}, f32[400]{0:T(512)}, u32[]{:S(2)}) copy-start(f32[400]{0:T(512)} %param.32) | copy-start | bytes 4804
  19.1 5.6 %copy-start.4 = (f32[4,2,400]{2,0,1:T(4,128)}, f32[4,2,400]{2,0,1:T(4,128)S(1)}, u32[]{:S(2)}) copy-start(f32[4,2,400]{2,0,1:T(4,128)S(1)} %fusion) | copy-start | bytes 38404
  19.1 10.9 %copy-start.2 = (bf16[4,256,320]{1,2,0:T(8,128)(2,1)S(1)}, bf16[4,256,320]{1,2,0:T(8,128)(2,1)}, u32[]{:S(2)}) copy-start(bf16[4,256,320]{1,2,0:T(8,128)(2,1)} %param.25) | copy-start | bytes 1966084
  20.0 3.0 %collective-permute-start.2 = (f32[4,692]{1,0:T(4,128)S(1)}, f32[4,692]{1,0:T(4,128)S(1)}, u32[]{:S(2)}, u32[]{:S(2)}) collective-permute-start(f32[4,692]{1,0:T(4,128)S(1)} %pad_maximum_fusion.2), channel_id=1, source_target_pairs={{0,3},{1,0},{2,1},{3,2},{4,7},{5,4},{6,5},{7,6},{8,11},{9,8},{10,9... | collective-permute-start | bytes 33224 | tf_op jit(solution)/shard_map/ppermute | solution.py:20
  20.0 3.8 %collective-permute-start.1 = (f32[4,692]{1,0:T(4,128)S(1)}, f32[4,692]{1,0:T(4,128)S(1)}, u32[]{:S(2)}, u32[]{:S(2)}) collective-permute-start(f32[4,692]{1,0:T(4,128)S(1)} %pad_maximum_fusion.2), channel_id=1, source_target_pairs={{0,2},{1,3},{2,0},{3,1},{4,6},{5,7},{6,4},{7,5},{8,10},{9,11},{10,... | collective-permute-start | bytes 33224 | tf_op jit(solution)/shard_map/ppermute | solution.py:20
  21.6 3.1 %collective-permute-start = (f32[4,692]{1,0:T(4,128)S(1)}, f32[4,692]{1,0:T(4,128)S(1)}, u32[]{:S(2)}, u32[]{:S(2)}) collective-permute-start(f32[4,692]{1,0:T(4,128)S(1)} %pad_maximum_fusion.2), channel_id=1, source_target_pairs={{0,1},{1,2},{2,3},{3,0},{4,5},{5,6},{6,7},{7,4},{8,9},{9,10},{10,1... | collective-permute-start | bytes 33224 | tf_op jit(solution)/shard_map/ppermute | solution.py:20
  25.4 1.0 %copy-start.5 = (bf16[4,2240]{1,0:T(4,128)(2,1)}, bf16[4,2240]{1,0:T(4,128)(2,1)S(1)}, u32[]{:S(2)}) copy-start(bf16[4,2240]{1,0:T(4,128)(2,1)S(1)} %convert_element_type.78) | copy-start | bytes 53764
  27.9 10.4 %slice-start = ((bf16[4,3,400]{2,0,1:T(4,128)(2,1)}), bf16[4,2,400]{2,0,1:T(4,128)(2,1)S(1)}, s32[]{:S(2)}) async-start(bf16[4,3,400]{2,0,1:T(4,128)(2,1)} %param.26), calls=%async_computation.1 | async-start | bytes 16384 | tf_op jit(solution)/shard_map/slice | solution.py:91
  31.6 5.5 %copy-start.9 = (f32[4,25]{1,0:T(4,128)S(1)}, f32[4,25]{1,0:T(4,128)}, u32[]{:S(2)}) copy-start(f32[4,25]{1,0:T(4,128)} %reshape.250) | copy-start | bytes 1204
  31.7 9.3 %copy-start.6 = (f32[4,5,5]{2,1,0:T(8,128)S(1)}, f32[4,5,5]{2,1,0:T(8,128)}, u32[]{:S(2)}) copy-start(f32[4,5,5]{2,1,0:T(8,128)} %get-tuple-element.14) | copy-start | bytes 1204
  37.3 4.6 %collective-permute-start.5 = (f32[4,3250]{1,0:T(4,128)S(1)}, f32[4,3250]{1,0:T(4,128)S(1)}, u32[]{:S(2)}, u32[]{:S(2)}) collective-permute-start(f32[4,3250]{1,0:T(4,128)S(1)} %concatenate.10), channel_id=1, source_target_pairs={{0,3},{1,0},{2,1},{3,2},{4,7},{5,4},{6,5},{7,6},{8,11},{9,8},{10,9... | collective-permute-start | bytes 156008 | tf_op jit(solution)/shard_map/ppermute | solution.py:20
  37.4 4.7 %collective-permute-start.4 = (f32[4,3250]{1,0:T(4,128)S(1)}, f32[4,3250]{1,0:T(4,128)S(1)}, u32[]{:S(2)}, u32[]{:S(2)}) collective-permute-start(f32[4,3250]{1,0:T(4,128)S(1)} %concatenate.10), channel_id=1, source_target_pairs={{0,2},{1,3},{2,0},{3,1},{4,6},{5,7},{6,4},{7,5},{8,10},{9,11},{10,... | collective-permute-start | bytes 156008 | tf_op jit(solution)/shard_map/ppermute | solution.py:20
  38.1 4.1 %collective-permute-start.3 = (f32[4,3250]{1,0:T(4,128)S(1)}, f32[4,3250]{1,0:T(4,128)S(1)}, u32[]{:S(2)}, u32[]{:S(2)}) collective-permute-start(f32[4,3250]{1,0:T(4,128)S(1)} %concatenate.10), channel_id=1, source_target_pairs={{0,1},{1,2},{2,3},{3,0},{4,5},{5,6},{6,7},{7,4},{8,9},{9,10},{10,1... | collective-permute-start | bytes 156008 | tf_op jit(solution)/shard_map/ppermute | solution.py:20
  42.2 9.3 %copy-start.11 = (f32[400]{0:T(512)S(1)}, f32[400]{0:T(512)}, u32[]{:S(2)}) copy-start(f32[400]{0:T(512)} %param.41) | copy-start | bytes 4804
  42.2 9.4 %copy-start.12 = (f32[400]{0:T(512)S(1)}, f32[400]{0:T(512)}, u32[]{:S(2)}) copy-start(f32[400]{0:T(512)} %param.40) | copy-start | bytes 4804
  45.8 2.9 %collective-permute-start.8 = (f32[4]{0:T(128)S(1)}, f32[4]{0:T(128)S(1)}, u32[]{:S(2)}, u32[]{:S(2)}) collective-permute-start(f32[4]{0:T(128)S(1)} %get-tuple-element.22), channel_id=1, source_target_pairs={{0,3},{1,0},{2,1},{3,2},{4,7},{5,4},{6,5},{7,6},{8,11},{9,8},{10,9... | collective-permute-start | bytes 56 | tf_op jit(solution)/shard_map/ppermute | solution.py:31
  47.2 3.5 %collective-permute-start.7 = (f32[4]{0:T(128)S(1)}, f32[4]{0:T(128)S(1)}, u32[]{:S(2)}, u32[]{:S(2)}) collective-permute-start(f32[4]{0:T(128)S(1)} %get-tuple-element.22), channel_id=1, source_target_pairs={{0,2},{1,3},{2,0},{3,1},{4,6},{5,7},{6,4},{7,5},{8,10},{9,11},{10,... | collective-permute-start | bytes 56 | tf_op jit(solution)/shard_map/ppermute | solution.py:31
  48.6 3.0 %collective-permute-start.6 = (f32[4]{0:T(128)S(1)}, f32[4]{0:T(128)S(1)}, u32[]{:S(2)}, u32[]{:S(2)}) collective-permute-start(f32[4]{0:T(128)S(1)} %get-tuple-element.22), channel_id=1, source_target_pairs={{0,1},{1,2},{2,3},{3,0},{4,5},{5,6},{6,7},{7,4},{8,9},{9,10},{10,1... | collective-permute-start | bytes 56 | tf_op jit(solution)/shard_map/ppermute | solution.py:31

commit v2 on v0

v2 whole, which is shorter than its diff:
```python
import functools
import jax
import jax.numpy as jnp
from jax import lax
from jax.experimental import pallas as pl
from jax.experimental.pallas import tpu as pltpu
from jax.sharding import PartitionSpec as P

MODEL_WIDTH = 1600
QUERY_HEADS = 25
KEY_VALUE_HEADS = 5
HEAD_SIZE = 64
WINDOW_LENGTH = 1024
GROUP = QUERY_HEADS // KEY_VALUE_HEADS
QUERY_WIDTH = QUERY_HEADS * HEAD_SIZE
KEY_VALUE_WIDTH = KEY_VALUE_HEADS * HEAD_SIZE


EPSILON = 1e-06

NT = (((1,), (1,)), ((), ()))
F32 = jnp.float32
BF16 = jnp.bfloat16


def dot_nt(a, b):
    return lax.dot_general(a, b, NT, preferred_element_type=F32)


def sigmoid(v):
    return 1.0 / (1.0 + jnp.exp(-v))


def exchange(part, axis):
    size = lax.axis_size(axis)
    return [part] + [
        lax.ppermute(part, axis, [(i, (i + step) % size) for i in range(size)])
        for step in range(1, size)
    ]


def gather_xor(part, axis):
    size = lax.axis_size(axis)
    assert size & (size - 1) == 0
    digits = size.bit_length() - 1
    blocks = [part[None]]
    done = 0
    while done < digits:
        held = blocks[0] if len(blocks) == 1 else jnp.concatenate(blocks)
        wide = 1 if (digits - done) % 2 else 2
        blocks = [held] + [
            lax.ppermute(held, axis, [(i, i ^ (step << done)) for i in range(size)])
            for step in range(1, 1 << wide)
        ]
        done += wide
    return blocks


def stack_pieces(me, pieces, held):
    size = len(pieces)
    for step, piece in enumerate(pieces):
        held[lax.rem(me - step + size, size)] = piece[...]


def prepare(place_ref, source_ref, *refs, count):
    rows = source_ref.shape[0]
    given, (chosen_ref, base_ref, new_conv_ref, *kept), (conv_w, conv_b, conv_rows, sems) = (
        refs[: count + 3], refs[count + 3 : -4], refs[-4:])
    large, small = given[:count], given[count:]
    copies = [
        pltpu.make_async_copy(origin, to, sems.at[i])
        for i, (origin, to) in enumerate(zip((*small, *large), (conv_w, conv_b, conv_rows, *kept)))
    ]
    for copy in copies:
        copy.start()
    slots = chosen_ref.shape[1]
    row_id = lax.broadcasted_iota(jnp.int32, (8, slots), 0)
    wanted = jnp.full((8, slots), -1, jnp.int32)
    for r in range(rows):
        origin = lax.bitwise_xor(lax.div(source_ref[r], rows), place_ref[0])
        wanted = jnp.where(row_id == r, origin * rows + lax.rem(source_ref[r], rows), wanted)
    chosen = lax.broadcasted_iota(jnp.int32, (8, slots), 1) == wanted
    chosen_ref[...] = jnp.where(chosen, 1.0, 0.0)
    for copy in copies[:3]:
        copy.wait()
    taps = conv_rows.shape[0]
    base = conv_b[...]
    for tap in range(taps):
        base = base + conv_w[tap : tap + 1] * conv_rows[tap].astype(F32)
    base_ref[:rows] = base
    base_ref[rows:] = jnp.broadcast_to(conv_w[taps:], base.shape)
    for tap in range(taps - 1):
        new_conv_ref[tap] = conv_rows[tap + 1]
    new_conv_ref[taps - 1] = jnp.zeros_like(conv_rows[0])
    for copy in copies[3:]:
        copy.wait()


def project_in(me_ref, *refs, size):
    arrived_refs = refs[:size]
    (chosen_ref, base_ref, old_conv_ref, gain_ref, heads_w_ref, xz_w_ref, xproj_ref, part_ref,
     act_ref, gate_ref, new_conv_ref, cols_ref, blocks) = refs[size:]
    rows, cols = cols_ref.shape
    arrived = jnp.concatenate(
        [ref[i].astype(F32) for ref in arrived_refs for i in range(ref.shape[0])], axis=0
    ).astype(BF16)
    routed = jnp.dot(chosen_ref[...].astype(BF16), arrived, preferred_element_type=F32)
    for block in range(blocks.shape[0]):
        blocks[block] = routed[:rows, block * cols : (block + 1) * cols]
    cols_ref[...] = blocks[me_ref[0]]
    scale = lax.rsqrt(jnp.mean(routed * routed, axis=1, keepdims=True) + EPSILON)
    normed = (routed * scale * gain_ref[...]).astype(BF16)
    heads = dot_nt(normed, heads_w_ref[...])[:rows].astype(BF16).astype(F32)
    channel_in = dot_nt(normed, xz_w_ref[0])[:rows]
    gate = dot_nt(normed, xz_w_ref[1])[:rows]
    taps = old_conv_ref.shape[0]
    conv_out = base_ref[:rows] + base_ref[rows:] * channel_in
    act = conv_out * sigmoid(conv_out)
    for tap in range(taps - 1):
        new_conv_ref[tap] = old_conv_ref[tap]
    new_conv_ref[taps - 1] = channel_in.astype(BF16)
    act_ref[...] = act
    gate_ref[...] = gate * sigmoid(gate)
    state = dot_nt(act.astype(BF16), xproj_ref[...])
    part_ref[...] = jnp.concatenate([heads, state], axis=1)


def mix(
    me_ref, lengths_ref, *refs, size, head_width,
):
    pieces = refs[:size]
    (keys_ref, values_ref, act_ref, gate_ref, dt_w_ref, dt_b_ref, a_log_ref, ssm_ref, skip_ref,
     out_w_ref, part_ref, new_ssm_ref, new_kv_ref, held) = refs[size:]
    me = me_ref[0]
    stack_pieces(me, pieces, held)
    rows = held.shape[1]
    heads = jnp.concatenate([held[i][:, :head_width] for i in range(size)], axis=1)
    state = held[0][:, head_width:]
    for i in range(1, size):
        state = state + held[i][:, head_width:]
    new_kv_ref[...] = heads[:, QUERY_WIDTH:].astype(BF16)

    rank = dt_w_ref.shape[1]
    depth = a_log_ref.shape[0]
    step = dot_nt(state[:, :rank].astype(BF16), dt_w_ref[...]) + dt_b_ref[...]
    step = jnp.maximum(step, 0.0) + jnp.log1p(jnp.exp(-jnp.abs(step)))
    act = act_ref[...]
    rates = jnp.exp(a_log_ref[...])
    maps = jnp.concatenate(
        [state[:, rank:], jnp.zeros((rows, 128 - 2 * depth), F32)], axis=1
    )
    maps = jnp.concatenate([maps, jnp.zeros((8 - rows, 128), F32)], axis=0).T
    outs = []
    for r in range(rows):
        step_row = step[r : r + 1]
        fresh = jnp.exp(-step_row * rates) * ssm_ref[r] + maps[:depth, r : r + 1] * (
            step_row * act[r : r + 1]
        )
        new_ssm_ref[r] = fresh
        outs.append(jnp.sum(maps[depth : 2 * depth, r : r + 1] * fresh, axis=0, keepdims=True))
    state_out = jnp.concatenate(outs, axis=0) + skip_ref[...] * act
    ssm_heads = (state_out * gate_ref[...]).astype(BF16)
    y_part = jnp.dot(ssm_heads, out_w_ref[...], preferred_element_type=F32)

    span = keys_ref.shape[2]
    tall = jnp.concatenate([heads, jnp.zeros((8 - rows, heads.shape[1]), F32)], axis=0)
    row_id = lax.broadcasted_iota(jnp.int32, (8, span), 0)
    slot = lax.broadcasted_iota(jnp.int32, (8, span), 1) + me * span
    length = jnp.zeros((8, span), jnp.int32)
    hole = jnp.zeros((8, span), jnp.int32)
    for r in range(rows):
        count = lengths_ref[r]
        length = jnp.where(row_id == r, count, length)
        hole = jnp.where(
            row_id == r, jnp.where(count >= WINDOW_LENGTH, lax.rem(count, WINDOW_LENGTH), -1), hole
        )
    live = (slot < length) & (slot != hole)
    live = jnp.concatenate([live.astype(F32)] * GROUP, axis=0) > 0.0
    tile_row = lax.rem(lax.broadcasted_iota(jnp.int32, (8 * GROUP, 1), 0), 8)
    own_here = jnp.where(me == 0, 1.0, 0.0)
    numers, tops, totals = [], [], []
    for g in range(KEY_VALUE_HEADS):
        at = QUERY_WIDTH + g * HEAD_SIZE
        new_key = tall[:, at : at + HEAD_SIZE]
        new_value = tall[:, at + KEY_VALUE_WIDTH : at + KEY_VALUE_WIDTH + HEAD_SIZE]
        queries = jnp.concatenate(
            [
                tall[:, j * HEAD_SIZE : (j + 1) * HEAD_SIZE]
                for j in range(g * GROUP, (g + 1) * GROUP)
            ],
            axis=0,
        ) * (HEAD_SIZE ** -0.5)
        own = jnp.sum(queries * jnp.concatenate([new_key] * GROUP, axis=0), axis=1, keepdims=True)
        packed = queries.astype(BF16)
        score = jnp.zeros((8 * GROUP, span), F32)
        for r in range(rows):
            one = jnp.dot(
                packed,
                keys_ref[r, g * HEAD_SIZE : (g + 1) * HEAD_SIZE, :],
                preferred_element_type=F32,
            )
            score = jnp.where(tile_row == r, one, score)
        top = jnp.maximum(
            jnp.max(jnp.where(live, score, -jnp.inf), axis=1, keepdims=True), own
        )
        weight = jnp.where(live, jnp.exp(score - top), 0.0).astype(BF16)
        own_weight = jnp.exp(own - top).astype(BF16).astype(F32) * own_here
        total = jnp.sum(weight.astype(F32), axis=1, keepdims=True) + own_weight
        numer = jnp.zeros((8 * GROUP, HEAD_SIZE), F32)
        for r in range(rows):
            one = dot_nt(weight, values_ref[r, g * HEAD_SIZE : (g + 1) * HEAD_SIZE, :])
            numer = jnp.where(tile_row == r, one, numer)
        numer = numer + own_weight * jnp.concatenate([new_value] * GROUP, axis=0)
        for j in range(GROUP):
            numers.append(numer[8 * j : 8 * j + 8])
            tops.append(top[8 * j : 8 * j + 8])
            totals.append(total[8 * j : 8 * j + 8])
    line = jnp.concatenate(numers + tops + totals, axis=1)[:rows]
    part_ref[:, : line.shape[1]] = line
    part_ref[:, line.shape[1] :] = y_part


def project_out(
    me_ref, *refs, size,
):
    pieces = refs[:size]
    (spread_ref, w_ref, cols_ref, gain_ref, y_ref, base_ref, square_ref, blocks) = refs[size:]
    rows = cols_ref.shape[0]
    cols = cols_ref.shape[1]
    lows = QUERY_WIDTH
    tops = [p[:, lows : lows + QUERY_HEADS] for p in pieces]
    totals = [p[:, lows + QUERY_HEADS : lows + 2 * QUERY_HEADS] for p in pieces]
    top = functools.reduce(jnp.maximum, tops)
    factors = [jnp.exp(t - top) for t in tops]
    total = functools.reduce(jnp.add, [f * t for f, t in zip(factors, totals)])
    factors = jnp.concatenate([f / total for f in factors], axis=0)
    high = factors.astype(BF16)
    low = (factors - high.astype(F32)).astype(BF16)
    spread = jnp.dot(high, spread_ref[...], preferred_element_type=F32) + jnp.dot(
        low, spread_ref[...], preferred_element_type=F32
    )
    merged = functools.reduce(
        jnp.add,
        [spread[i * rows : (i + 1) * rows] * p[:, :QUERY_WIDTH] for i, p in enumerate(pieces)],
    )
    y_attn = dot_nt(merged.astype(BF16), w_ref[...])
    y_ref[...] = y_attn
    square_ref[...] = jnp.broadcast_to(
        jnp.sum(y_attn * y_attn, axis=1, keepdims=True), square_ref.shape
    )
    lows = lows + 2 * QUERY_HEADS
    y_ssm = functools.reduce(jnp.add, [p[:, lows : lows + MODEL_WIDTH] for p in pieces])
    scale = lax.rsqrt(jnp.mean(y_ssm * y_ssm, axis=1, keepdims=True) + EPSILON)
    for block in range(blocks.shape[0]):
        blocks[block] = y_ssm[:, block * cols : (block + 1) * cols]
    base_ref[...] = cols_ref[...] + 0.5 * (blocks[me_ref[0]] * scale * gain_ref[...])


def finish(*refs, size):
    squares = refs[:size]
    y_ref, base_ref, gain_ref, out_ref = refs[size:]
    square = functools.reduce(jnp.add, [s[:, :1] for s in squares])
    scale = lax.rsqrt(square / MODEL_WIDTH + EPSILON)
    out_ref[...] = (base_ref[...] + 0.5 * (y_ref[...] * scale * gain_ref[...])).astype(BF16)


SMEM = pl.BlockSpec(memory_space=pltpu.SMEM)
VMEM = pl.BlockSpec(memory_space=pltpu.VMEM)


def call(body, scalars, blocks, outs, scratch=()):
    return pl.pallas_call(
        body,
        in_specs=[SMEM] * len(scalars) + [VMEM] * len(blocks),
        out_specs=[VMEM] * len(outs),
        out_shape=outs,
        scratch_shapes=scratch,
        compiler_params=pltpu.CompilerParams(vmem_limit_bytes=16 * 1024 * 1024),
    )(*scalars, *blocks)


def shards(
    tokens,
    source,
    lengths,
    cached_key_rows,
    cached_value_rows,
    conv_state,
    ssm_state,
    norm_gain,
    query_key_value_weight,
    w_xz,
    conv_weight,
    conv_bias,
    w_xproj,
    w_dt,
    dt_bias,
    a_log,
    skip_d,
    w_attn_out,
    w_ssm_out,
    gain_attn,
    gain_ssm,
):
    rows = tokens.shape[0]
    narrow = lax.axis_size("narrow")
    me = lax.axis_index("narrow").astype(jnp.int32).reshape(1)
    cols = MODEL_WIDTH // narrow
    head_width = query_key_value_weight.shape[1]
    shape = jax.ShapeDtypeStruct

    place = lax.axis_index("wide").astype(jnp.int32).reshape(1)
    arrived = gather_xor(tokens, "wide")

    large = (
        norm_gain[None], query_key_value_weight.T, w_xz.transpose(1, 2, 0), w_xproj.T,
    )
    small = (conv_weight, conv_bias[None], conv_state.transpose(1, 0, 2))
    slots = rows * lax.axis_size("wide")
    anywhere = pl.BlockSpec(memory_space=pl.ANY)
    prepared = pl.pallas_call(
        functools.partial(prepare, count=len(large)),
        in_specs=[SMEM] * 2 + [anywhere] * (len(large) + len(small)),
        out_specs=[VMEM] * (3 + len(large)),
        out_shape=[
            pltpu.VMEM((8, slots), F32),
            pltpu.VMEM((2 * rows, cols), F32),
            pltpu.VMEM(small[2].shape, BF16),
            *(pltpu.VMEM(a.shape, a.dtype) for a in large),
        ],
        scratch_shapes=[pltpu.VMEM(a.shape, a.dtype) for a in small]
        + [pltpu.SemaphoreType.DMA((len(large) + len(small),))],
        compiler_params=pltpu.CompilerParams(vmem_limit_bytes=4 * 1024 * 1024),
        cost_estimate=pl.CostEstimate(
            flops=0, transcendentals=0, bytes_accessed=2 * sum(a.size * a.dtype.itemsize for a in large)
        ),
    )(place, source, *(pltpu.with_memory_space_constraint(a, pltpu.HBM) for a in large + small))
    part_width = head_width + w_xproj.shape[1]
    part, act, gate, new_conv, routed_cols = call(
        functools.partial(project_in, size=len(arrived)),
        (me,),
        (*arrived, *prepared),
        (
            shape((rows, part_width), F32),
            shape((rows, cols), F32),
            shape((rows, cols), F32),
            shape((conv_state.shape[1], rows, cols), BF16),
            shape((rows, cols), F32),
        ),
        (pltpu.VMEM((narrow, rows, cols), F32),),
    )
    pieces = exchange(part, "narrow")
    second_width = QUERY_WIDTH + 2 * QUERY_HEADS + MODEL_WIDTH
    part, new_ssm, new_kv = call(
        functools.partial(mix, size=narrow, head_width=head_width),
        (me, lengths),
        (
            *pieces,
            cached_key_rows.transpose(0, 2, 1),
            cached_value_rows.transpose(0, 2, 1),
            act,
            gate,
            w_dt.T,
            dt_bias[None],
            a_log,
            ssm_state,
            skip_d[None],
            w_ssm_out,
        ),
        (
            shape((rows, second_width), F32),
            shape(ssm_state.shape, F32),
            shape((rows, 2 * KEY_VALUE_WIDTH), BF16),
        ),
        (pltpu.VMEM((narrow, rows, part_width), F32),),
    )
    pieces = exchange(part, "narrow")
    spread = (
        lax.broadcasted_iota(jnp.int32, (QUERY_HEADS, QUERY_WIDTH), 1) // HEAD_SIZE
        == lax.broadcasted_iota(jnp.int32, (QUERY_HEADS, QUERY_WIDTH), 0)
    ).astype(BF16)
    y_attn, base, square = call(
        functools.partial(project_out, size=narrow),
        (me,),
        (*pieces, spread, w_attn_out.T, routed_cols, gain_ssm[None]),
        (
            shape((rows, cols), F32),
            shape((rows, cols), F32),
            shape((rows, 128), F32),
        ),
        (pltpu.VMEM((narrow, rows, cols), F32),),
    )
    squares = exchange(square, "narrow")
    (out,) = call(
        functools.partial(finish, size=narrow),
        (),
        (*squares, y_attn, base, gain_attn[None]),
        (shape((rows, cols), BF16),),
    )
    return (out, new_kv, new_conv.transpose(1, 0, 2), new_ssm)


def solution(mesh):
    placed = (
        P("wide", None),
        P("wide"),
        P("wide"),
        P("wide", "narrow", None),
        P("wide", "narrow", None),
        P("wide", None, "narrow"),
        P("wide", None, "narrow"),
        P(),
        P(None, "narrow"),
        P(None, None, "narrow"),
        P(None, "narrow"),
        P("narrow"),
        P("narrow", None),
        P(None, "narrow"),
        P("narrow"),
        P(None, "narrow"),
        P("narrow"),
        P(None, "narrow"),
        P("narrow", None),
        P("narrow"),
        P("narrow"),
    )
    return jax.shard_map(
        shards,
        mesh=mesh,
        in_specs=placed,
        out_specs=(
            P("wide", "narrow"),
            P("wide", None),
            P("wide", None, "narrow"),
            P("wide", None, "narrow"),
        ),
        check_vma=False,
    )
```

time: 132 us -> 37.4 us (0.28)
  blocking collectives: 66 us -> 0 us
  starting transfers between devices: 0.04 us -> 16 us
  matrix products: 13.6 us -> 0 us
  between operations: 14.3 us -> 0.78 us
  waiting for transfers between devices: 18.4 us -> 7.69 us
  other arithmetic: 10.8 us -> 0.77 us
  Pallas kernels: 0 us -> 9.63 us
  local copies, waits for them, and re-layouts: 8.26 us -> 2.01 us
    all_gather x2 -> x0, blocking collectives: 37.9 us -> none  [the longest x1 32.6 us: shards(): arrived = lax.all_gather(tokens, 'wide', axis=0, tiled=True)]
    unnamed x2 -> x0, waiting for transfers between devices: 18.4 us -> none
    psum x2 -> x0, blocking collectives: 16.8 us -> none  [the longest x1 11 us: shards(): lax.psum(jnp.dot(conv_act.astype(jnp.bfloat16), w_xproj, preferred_elemen...]
    ppermute x0 -> x13, starting transfers between devices: none -> 16 us  [the longest x9 8.24 us: exchange(): lax.ppermute(part, axis, [(i, (i + step) % size) for i in range(size)])]
    pmax x1 -> x0, blocking collectives: 11.4 us -> none  [shards(): score_top = lax.pmax(local_top, 'narrow')]
    dot_general x8 -> x0, matrix products: 10.5 us -> none  [the longest x1 2.11 us: shards(): jnp.dot(normed, query_key_value_weight, preferred_element_type=jnp.float32)]
    pallas_call x0 -> x5, Pallas kernels: none -> 9.63 us  [the longest x4 6.65 us: call(): pl.pallas_call(body, in_specs=[SMEM] * len(scalars) + [VMEM] * len(blocks...]
    ppermute x0 -> x13, waiting for transfers between devices: none -> 7.69 us  [the longest x9 5.11 us: exchange(): lax.ppermute(part, axis, [(i, (i + step) % size) for i in range(size)])]
  transfers between devices with their start and end apart: 1 -> 13, of which waited for: 1 -> 9; matrix products, arithmetic and copies ran while one was open for 4% -> 4% of each run, Pallas kernels for 0% -> 8%
where the time goes in v2:
time: 37.4 us; the launch traced here: 36.9 us
  starting transfers between devices  16 us (43%)
  Pallas kernels  9.63 us (26%)
  waiting for transfers between devices  7.69 us (21%)
  local copies, waits for them, and re-layouts  2.01 us (5%)
  between operations  0.78 us (2%)
  other arithmetic  0.77 us (2%)
    ppermute x9, starting transfers between devices, exchange(): lax.ppermute(part, axis, [(i, (i + step) % size) for i in range(size)])  8.24 us
    ppermute x4, starting transfers between devices, gather_xor(): lax.ppermute(held, axis, [(i, i ^ step << done) for i in range(size)])  7.77 us
    pallas_call x4, Pallas kernels, call(): pl.pallas_call(body, in_specs=[SMEM] * len(scalars) + [VMEM] * len(blocks...  6.65 us
    ppermute x9, waiting for transfers between devices, exchange(): lax.ppermute(part, axis, [(i, (i + step) % size) for i in range(size)])  5.11 us
    pallas_call x1, Pallas kernels, shards(): pl.pallas_call(functools.partial(prepare, count=len(large)), in_specs=[SM...  2.98 us
    ppermute x4, waiting for transfers between devices, gather_xor(): lax.ppermute(held, axis, [(i, i ^ step << done) for i in range(size)])  2.58 us
    broadcast_in_dim x1, local copies, waits for them, and re-layouts, shards(): norm_gain[None]  1.29 us
  transfers between devices with their start and end apart: 13, of which 9 were waited for; matrix products, arithmetic and copies ran while one was open for 4% of the time, Pallas kernels for 8%

profile of v2, /device:TPU:0, one launch (start us, length us, event | category | flops | bytes accessed | tf_op | source)
XLA Modules:
  0.0 36.9 jit_solution(5626466169339492603)
XLA Ops:
  0.6 3.0 %collective-permute-start = (bf16[1,4,1600]{2,1,0:T(4,128)(2,1)}, bf16[1,4,1600]{2,1,0:T(4,128)(2,1)S(1)}, u32[]{:S(2)}, u32[]{:S(2)}) collective-permute-start(bf16[1,4,1600]{2,1,0:T(4,128)(2,1)} %bitcast.28), channel_id=1, source_target_pairs={{0,4},{4,0},{8,12},{12,8},{16,20},{20,16},{24,28},{28,24},{1,5},{5... | collective-permute-start | bytes 38408 | tf_op jit(solution)/shard_map/ppermute | solution.py:52
  3.7 1.9 %collective-permute-done = bf16[1,4,1600]{2,1,0:T(4,128)(2,1)S(1)} collective-permute-done((bf16[1,4,1600]{2,1,0:T(4,128)(2,1)}, bf16[1,4,1600]{2,1,0:T(4,128)(2,1)S(1)}, u32[]{:S(2)}, u32[]{:S(2)}) %collective-permute-start) | collective-permute-done | bytes 12832 | tf_op jit(solution)/shard_map/ppermute | solution.py:52
  5.6 0.7 %pad_maximum_fusion.refs_0_ = bf16[2,4,1600]{2,1,0:T(4,128)(2,1)S(1)} fusion(bf16[1,4,1600]{2,1,0:T(4,128)(2,1)S(1)} %collective-permute-done, bf16[1,4,1600]{2,1,0:T(4,128)(2,1)} %bitcast.29), kind=kLoop, calls=%fused_computation.2 | loop fusion | flops 12800 | bytes 51200 | tf_op jit(solution)/shard_map/concatenate | solution.py:49
  6.3 2.1 %collective-permute-start.1 = (bf16[2,4,1600]{2,1,0:T(4,128)(2,1)S(1)}, bf16[2,4,1600]{2,1,0:T(4,128)(2,1)S(1)}, u32[]{:S(2)}, u32[]{:S(2)}) collective-permute-start(bf16[2,4,1600]{2,1,0:T(4,128)(2,1)S(1)} %pad_maximum_fusion.refs_0_), channel_id=1, source_target_pairs={{0,8},{4,12},{8,0},{12,4},{16,24},{20,28},{24,16},{28,20},{1,9},{5... | collective-permute-start | bytes 76808 | tf_op jit(solution)/shard_map/ppermute | solution.py:52
  8.4 2.6 %collective-permute-start.2 = (bf16[2,4,1600]{2,1,0:T(4,128)(2,1)S(1)}, bf16[2,4,1600]{2,1,0:T(4,128)(2,1)S(1)}, u32[]{:S(2)}, u32[]{:S(2)}) collective-permute-start(bf16[2,4,1600]{2,1,0:T(4,128)(2,1)S(1)} %pad_maximum_fusion.refs_0_), channel_id=1, source_target_pairs={{0,16},{4,20},{8,24},{12,28},{16,0},{20,4},{24,8},{28,12},{1,17},{... | collective-permute-start | bytes 76808 | tf_op jit(solution)/shard_map/ppermute | solution.py:52
  11.0 1.3 %broadcast_in_dim.22.refs_0_ = f32[1,1600]{1,0:T(1,128)} reshape(f32[1600]{0:T(1024)} %param.28) | data formatting | bytes 12800 | tf_op jit(solution)/shard_map/broadcast_in_dim | solution.py:316
  12.3 0.7 %copy-done.12 = s32[4]{0:T(128)S(1)} copy-done((s32[4]{0:T(128)S(1)}, s32[4]{0:T(128)}, u32[]{:S(2)}) %copy-start.12) | copy-done | bytes 40
  13.0 3.0 %shard_map.228 = (f32[8,32]{1,0:T(8,128)S(1)}, f32[8,400]{1,0:T(8,128)S(1)}, bf16[3,4,400]{2,1,0:T(4,128)(2,1)S(1)}, f32[1,1600]{1,0:T(1,128)S(1)}, bf16[560,160...) custom-call(s32[1]{0:T(128)} %bitcast.2.place_ref, s32[4]{0:T(128)S(1)} %copy-done.12, ...), custom_call_target="tpu_custom_call" | custom-call | bytes 8928000 | tf_op jit(solution)/shard_map/pallas_call | solution.py:321
  16.0 0.7 %collective-permute-done.3.refs_3_ = bf16[2,4,1600]{2,1,0:T(4,128)(2,1)S(1)} collective-permute-done((bf16[2,4,1600]{2,1,0:T(4,128)(2,1)S(1)}, bf16[2,4,1600]{2,1,0:T(4,128)(2,1)S(1)}, u32[]{:S(2)}, u32[]{:S(2)}) %collective-permute-start.3) | collective-permute-done | bytes 25632 | tf_op jit(solution)/shard_map/ppermute | solution.py:52
  16.7 0.0 copy-start.5
  16.7 0.0 copy-start.10
  16.7 0.0 copy-start.11
  16.7 2.0 %shard_map.229 = (f32[4,692]{1,0:T(4,128)S(1)}, f32[4,400]{1,0:T(4,128)S(1)}, f32[4,400]{1,0:T(4,128)S(1)}, bf16[3,4,400]{2,1,0:T(4,128)(2,1)}, f32[4,400]{1,0:T(4,128)S(1)}) custom-call(s32[1]{0:T(128)} %bitcast.me_ref, bf16[2,4,1600]{2,1,0:T(4,128)(2,1)S(1)} %pad_maximum_fusion.refs_0_, bf16[2,4,1600]{2,1,0:T(4,128)(2,1)S(1)} %collective-permute-done.1.refs_1_, ...), custom_call_target="tpu_custom_call" | custom-call | tf_op jit(solution)/shard_map/pallas_call | solution.py:272
  18.7 1.5 %collective-permute-start.5 = (f32[4,692]{1,0:T(4,128)S(1)}, f32[4,692]{1,0:T(4,128)S(1)}, u32[]{:S(2)}, u32[]{:S(2)}) collective-permute-start(f32[4,692]{1,0:T(4,128)S(1)} %get-tuple-element.29.refs_0_), channel_id=1, source_target_pairs={{0,2},{1,3},{2,0},{3,1},{4,6},{5,7},{6,4},{7,5},{8,10},{9,11},{10,... | collective-permute-start | bytes 33224 | tf_op jit(solution)/shard_map/ppermute | solution.py:37
  20.2 1.4 %collective-permute-start.6 = (f32[4,692]{1,0:T(4,128)S(1)}, f32[4,692]{1,0:T(4,128)S(1)}, u32[]{:S(2)}, u32[]{:S(2)}) collective-permute-start(f32[4,692]{1,0:T(4,128)S(1)} %get-tuple-element.29.refs_0_), channel_id=1, source_target_pairs={{0,3},{1,0},{2,1},{3,2},{4,7},{5,4},{6,5},{7,6},{8,11},{9,8},{10,9... | collective-permute-start | bytes 33224 | tf_op jit(solution)/shard_map/ppermute | solution.py:37
  21.7 0.2 collective-permute-done.4.refs_1_
  21.8 0.6 %collective-permute-done.5.refs_2_ = f32[4,692]{1,0:T(4,128)S(1)} collective-permute-done((f32[4,692]{1,0:T(4,128)S(1)}, f32[4,692]{1,0:T(4,128)S(1)}, u32[]{:S(2)}, u32[]{:S(2)}) %collective-permute-start.5) | collective-permute-done | bytes 11104 | tf_op jit(solution)/shard_map/ppermute | solution.py:37
  22.5 0.6 %collective-permute-done.6.refs_3_ = f32[4,692]{1,0:T(4,128)S(1)} collective-permute-done((f32[4,692]{1,0:T(4,128)S(1)}, f32[4,692]{1,0:T(4,128)S(1)}, u32[]{:S(2)}, u32[]{:S(2)}) %collective-permute-start.6) | collective-permute-done | bytes 11104 | tf_op jit(solution)/shard_map/ppermute | solution.py:37
  23.2 3.2 %shard_map.230 = (f32[4,3250]{1,0:T(4,128)S(1)}, f32[4,16,400]{2,1,0:T(8,128)}, bf16[4,640]{1,0:T(4,128)(2,1)}) custom-call(s32[1]{0:T(128)} %bitcast.me_ref, s32[4]{0:T(128)S(1)} %copy-done.11, f32[4,692]{1,0:T(4,128)S(1)} %get-tuple-element.29.refs_0_, f32[4,692]{1,0:T(4,128)S(1)} %collective-permute-done.4.refs_1_, ...), custom_call_target="tpu_custom_call" | custom-call | tf_op jit(solution)/shard_map/pallas_call | solution.py:272
  26.4 0.6 %collective-permute-start.7 = (f32[4,3250]{1,0:T(4,128)S(1)}, f32[4,3250]{1,0:T(4,128)S(1)}, u32[]{:S(2)}, u32[]{:S(2)}) collective-permute-start(f32[4,3250]{1,0:T(4,128)S(1)} %get-tuple-element.32.refs_0_), channel_id=1, source_target_pairs={{0,1},{1,2},{2,3},{3,0},{4,5},{5,6},{6,7},{7,4},{8,9},{9,10},{10,1... | collective-permute-start | bytes 156008 | tf_op jit(solution)/shard_map/ppermute | solution.py:37
  27.0 1.5 %collective-permute-start.8 = (f32[4,3250]{1,0:T(4,128)S(1)}, f32[4,3250]{1,0:T(4,128)S(1)}, u32[]{:S(2)}, u32[]{:S(2)}) collective-permute-start(f32[4,3250]{1,0:T(4,128)S(1)} %get-tuple-element.32.refs_0_), channel_id=1, source_target_pairs={{0,2},{1,3},{2,0},{3,1},{4,6},{5,7},{6,4},{7,5},{8,10},{9,11},{10,... | collective-permute-start | bytes 156008 | tf_op jit(solution)/shard_map/ppermute | solution.py:37
  28.5 0.2 collective-permute-start.9
  28.7 1.2 %collective-permute-done.7.refs_1_ = f32[4,3250]{1,0:T(4,128)S(1)} collective-permute-done((f32[4,3250]{1,0:T(4,128)S(1)}, f32[4,3250]{1,0:T(4,128)S(1)}, u32[]{:S(2)}, u32[]{:S(2)}) %collective-permute-start.7) | collective-permute-done | bytes 52032 | tf_op jit(solution)/shard_map/ppermute | solution.py:37
  29.9 1.2 %collective-permute-done.8.refs_2_ = f32[4,3250]{1,0:T(4,128)S(1)} collective-permute-done((f32[4,3250]{1,0:T(4,128)S(1)}, f32[4,3250]{1,0:T(4,128)S(1)}, u32[]{:S(2)}, u32[]{:S(2)}) %collective-permute-start.8) | collective-permute-done | bytes 52032 | tf_op jit(solution)/shard_map/ppermute | solution.py:37
  31.2 0.8 %shard_map.231 = (f32[4,400]{1,0:T(4,128)S(1)}, f32[4,400]{1,0:T(4,128)S(1)}, f32[4,128]{1,0:T(4,128)S(1)}) custom-call(s32[1]{0:T(128)} %bitcast.me_ref, f32[4,3250]{1,0:T(4,128)S(1)} %get-tuple-element.32.refs_0_, f32[4,3250]{1,0:T(4,128)S(1)} %collective-permute-done.7.refs_1_, f32[4,3250]{1,0:T(4,128)S(1)} %collective-permute-done.8.refs_2_, ...), custom_call_target="tpu_custom_call" | custom-call | tf_op jit(solution)/shard_map/pallas_call | solution.py:272
  31.9 0.6 %collective-permute-start.10 = (f32[4,128]{1,0:T(4,128)S(1)}, f32[4,128]{1,0:T(4,128)S(1)}, u32[]{:S(2)}, u32[]{:S(2)}) collective-permute-start(f32[4,128]{1,0:T(4,128)S(1)} %get-tuple-element.34.refs_0_), channel_id=1, source_target_pairs={{0,1},{1,2},{2,3},{3,0},{4,5},{5,6},{6,7},{7,4},{8,9},{9,10},{10,1... | collective-permute-start | bytes 6152 | tf_op jit(solution)/shard_map/ppermute | solution.py:37
  32.6 1.2 %collective-permute-start.11 = (f32[4,128]{1,0:T(4,128)S(1)}, f32[4,128]{1,0:T(4,128)S(1)}, u32[]{:S(2)}, u32[]{:S(2)}) collective-permute-start(f32[4,128]{1,0:T(4,128)S(1)} %get-tuple-element.34.refs_0_), channel_id=1, source_target_pairs={{0,2},{1,3},{2,0},{3,1},{4,6},{5,7},{6,4},{7,5},{8,10},{9,11},{10,... | collective-permute-start | bytes 6152 | tf_op jit(solution)/shard_map/ppermute | solution.py:37
  33.8 1.1 %collective-permute-start.12 = (f32[4,128]{1,0:T(4,128)S(1)}, f32[4,128]{1,0:T(4,128)S(1)}, u32[]{:S(2)}, u32[]{:S(2)}) collective-permute-start(f32[4,128]{1,0:T(4,128)S(1)} %get-tuple-element.34.refs_0_), channel_id=1, source_target_pairs={{0,3},{1,0},{2,1},{3,2},{4,7},{5,4},{6,5},{7,6},{8,11},{9,8},{10,9... | collective-permute-start | bytes 6152 | tf_op jit(solution)/shard_map/ppermute | solution.py:37
  34.9 0.1 collective-permute-done.10.refs_1_
  35.0 1.2 %collective-permute-done.11.refs_2_ = f32[4,128]{1,0:T(4,128)S(1)} collective-permute-done((f32[4,128]{1,0:T(4,128)S(1)}, f32[4,128]{1,0:T(4,128)S(1)}, u32[]{:S(2)}, u32[]{:S(2)}) %collective-permute-start.11) | collective-permute-done | bytes 2080 | tf_op jit(solution)/shard_map/ppermute | solution.py:37
  36.2 0.0 collective-permute-done.12.refs_3_
  36.2 0.7 %shard_map.232 = bf16[4,400]{1,0:T(4,128)(2,1)} custom-call(f32[4,128]{1,0:T(4,128)S(1)} %get-tuple-element.34.refs_0_, f32[4,128]{1,0:T(4,128)S(1)} %collective-permute-done.10.refs_1_, f32[4,128]{1,0:T(4,128)S(1)} %collective-permute-done.11.refs_2_, f32[4,128]{1,0:T(4,128)S(1)} %collective-permute-done.12.refs_3_, ...), custom_call_target="tpu_custom_call" | custom-call | tf_op jit(solution)/shard_map/pallas_call | solution.py:272
  (30 shorter events, 0.1 us)
Async XLA Ops:
  0.6 4.9 %collective-permute-start = (bf16[1,4,1600]{2,1,0:T(4,128)(2,1)}, bf16[1,4,1600]{2,1,0:T(4,128)(2,1)S(1)}, u32[]{:S(2)}, u32[]{:S(2)}) collective-permute-start(bf16[1,4,1600]{2,1,0:T(4,128)(2,1)} %bitcast.28), channel_id=1, source_target_pairs={{0,4},{4,0},{8,12},{12,8},{16,20},{20,16},{24,28},{28,24},{1,5},{5... | collective-permute-start | bytes 38408 | tf_op jit(solution)/shard_map/ppermute | solution.py:52
  6.3 9.7 %collective-permute-start.1 = (bf16[2,4,1600]{2,1,0:T(4,128)(2,1)S(1)}, bf16[2,4,1600]{2,1,0:T(4,128)(2,1)S(1)}, u32[]{:S(2)}, u32[]{:S(2)}) collective-permute-start(bf16[2,4,1600]{2,1,0:T(4,128)(2,1)S(1)} %pad_maximum_fusion.refs_0_), channel_id=1, source_target_pairs={{0,8},{4,12},{8,0},{12,4},{16,24},{20,28},{24,16},{28,20},{1,9},{5... | collective-permute-start | bytes 76808 | tf_op jit(solution)/shard_map/ppermute | solution.py:52
  8.4 7.5 %collective-permute-start.2 = (bf16[2,4,1600]{2,1,0:T(4,128)(2,1)S(1)}, bf16[2,4,1600]{2,1,0:T(4,128)(2,1)S(1)}, u32[]{:S(2)}, u32[]{:S(2)}) collective-permute-start(bf16[2,4,1600]{2,1,0:T(4,128)(2,1)S(1)} %pad_maximum_fusion.refs_0_), channel_id=1, source_target_pairs={{0,16},{4,20},{8,24},{12,28},{16,0},{20,4},{24,8},{28,12},{1,17},{... | collective-permute-start | bytes 76808 | tf_op jit(solution)/shard_map/ppermute | solution.py:52
  11.0 5.6 %collective-permute-start.3 = (bf16[2,4,1600]{2,1,0:T(4,128)(2,1)S(1)}, bf16[2,4,1600]{2,1,0:T(4,128)(2,1)S(1)}, u32[]{:S(2)}, u32[]{:S(2)}) collective-permute-start(bf16[2,4,1600]{2,1,0:T(4,128)(2,1)S(1)} %pad_maximum_fusion.refs_0_), channel_id=1, source_target_pairs={{0,24},{4,28},{8,16},{12,20},{16,8},{20,12},{24,0},{28,4},{1,25},{... | collective-permute-start | bytes 76808 | tf_op jit(solution)/shard_map/ppermute | solution.py:52
  12.3 0.7 %copy-start.12 = (s32[4]{0:T(128)S(1)}, s32[4]{0:T(128)}, u32[]{:S(2)}) copy-start(s32[4]{0:T(128)} %source_ref.1) | copy-start | bytes 52
  16.7 6.4 %copy-start.1 = (bf16[400,1600]{1,0:T(8,128)(2,1)S(1)}, bf16[400,1600]{1,0:T(8,128)(2,1)}, u32[]{:S(2)}) copy-start(bf16[400,1600]{1,0:T(8,128)(2,1)} %refs_13_.1) | copy-start | bytes 3840004
  16.7 6.4 %copy-start.2 = (bf16[4,256,320]{1,2,0:T(8,128)(2,1)S(1)}, bf16[4,256,320]{1,2,0:T(8,128)(2,1)}, u32[]{:S(2)}) copy-start(bf16[4,256,320]{1,2,0:T(8,128)(2,1)} %param.24) | copy-start | bytes 1966084
  16.7 6.4 %copy-start.3 = (bf16[4,256,320]{1,2,0:T(8,128)(2,1)S(1)}, bf16[4,256,320]{1,2,0:T(8,128)(2,1)}, u32[]{:S(2)}) copy-start(bf16[4,256,320]{1,2,0:T(8,128)(2,1)} %param.25) | copy-start | bytes 1966084
  16.7 6.4 %copy-start.4 = (f32[4,16,400]{2,1,0:T(8,128)S(1)}, f32[4,16,400]{2,1,0:T(8,128)}, u32[]{:S(2)}) copy-start(f32[4,16,400]{2,1,0:T(8,128)} %refs_11_.1) | copy-start | bytes 307204
  16.7 6.4 %copy-start.5 = (bf16[100,400]{0,1:T(8,128)(2,1)S(1)}, bf16[100,400]{0,1:T(8,128)(2,1)}, u32[]{:S(2)}) copy-start(bf16[100,400]{0,1:T(8,128)(2,1)} %param.34) | copy-start | bytes 240004
  16.7 6.4 %copy-start.6 = (f32[16,400]{1,0:T(8,128)S(1)}, f32[16,400]{1,0:T(8,128)}, u32[]{:S(2)}) copy-start(f32[16,400]{1,0:T(8,128)} %refs_10_.1) | copy-start | bytes 76804
  16.7 6.4 %copy-start.9 = (f32[400]{0:T(512)S(1)}, f32[400]{0:T(512)}, u32[]{:S(2)}) copy-start(f32[400]{0:T(512)} %param.35) | copy-start | bytes 4804
  16.7 6.4 %copy-start.10 = (f32[400]{0:T(512)S(1)}, f32[400]{0:T(512)}, u32[]{:S(2)}) copy-start(f32[400]{0:T(512)} %param.37) | copy-start | bytes 4804
  16.7 6.4 %copy-start.11 = (s32[4]{0:T(128)S(1)}, s32[4]{0:T(128)}, u32[]{:S(2)}) copy-start(s32[4]{0:T(128)} %lengths_ref.1) | copy-start | bytes 52
  18.7 12.4 %copy-start = (bf16[1600,400]{0,1:T(8,128)(2,1)S(1)}, bf16[1600,400]{0,1:T(8,128)(2,1)}, u32[]{:S(2)}) copy-start(bf16[1600,400]{0,1:T(8,128)(2,1)} %param.38) | copy-start | bytes 3840004
  18.7 12.4 %copy-start.7 = (f32[400]{0:T(512)S(1)}, f32[400]{0:T(512)}, u32[]{:S(2)}) copy-start(f32[400]{0:T(512)} %param.41) | copy-start | bytes 4804
  18.7 3.1 %collective-permute-start.4 = (f32[4,692]{1,0:T(4,128)S(1)}, f32[4,692]{1,0:T(4,128)S(1)}, u32[]{:S(2)}, u32[]{:S(2)}) collective-permute-start(f32[4,692]{1,0:T(4,128)S(1)} %get-tuple-element.29.refs_0_), channel_id=1, source_target_pairs={{0,1},{1,2},{2,3},{3,0},{4,5},{5,6},{6,7},{7,4},{8,9},{9,10},{10,1... | collective-permute-start | bytes 33224 | tf_op jit(solution)/shard_map/ppermute | solution.py:37
  18.7 3.7 %collective-permute-start.5 = (f32[4,692]{1,0:T(4,128)S(1)}, f32[4,692]{1,0:T(4,128)S(1)}, u32[]{:S(2)}, u32[]{:S(2)}) collective-permute-start(f32[4,692]{1,0:T(4,128)S(1)} %get-tuple-element.29.refs_0_), channel_id=1, source_target_pairs={{0,2},{1,3},{2,0},{3,1},{4,6},{5,7},{6,4},{7,5},{8,10},{9,11},{10,... | collective-permute-start | bytes 33224 | tf_op jit(solution)/shard_map/ppermute | solution.py:37
  20.2 2.8 %collective-permute-start.6 = (f32[4,692]{1,0:T(4,128)S(1)}, f32[4,692]{1,0:T(4,128)S(1)}, u32[]{:S(2)}, u32[]{:S(2)}) collective-permute-start(f32[4,692]{1,0:T(4,128)S(1)} %get-tuple-element.29.refs_0_), channel_id=1, source_target_pairs={{0,3},{1,0},{2,1},{3,2},{4,7},{5,4},{6,5},{7,6},{8,11},{9,8},{10,9... | collective-permute-start | bytes 33224 | tf_op jit(solution)/shard_map/ppermute | solution.py:37
  23.1 13.1 %copy-start.8 = (f32[400]{0:T(512)S(1)}, f32[400]{0:T(512)}, u32[]{:S(2)}) copy-start(f32[400]{0:T(512)} %param.40) | copy-start | bytes 4804
  26.4 3.6 %collective-permute-start.7 = (f32[4,3250]{1,0:T(4,128)S(1)}, f32[4,3250]{1,0:T(4,128)S(1)}, u32[]{:S(2)}, u32[]{:S(2)}) collective-permute-start(f32[4,3250]{1,0:T(4,128)S(1)} %get-tuple-element.32.refs_0_), channel_id=1, source_target_pairs={{0,1},{1,2},{2,3},{3,0},{4,5},{5,6},{6,7},{7,4},{8,9},{9,10},{10,1... | collective-permute-start | bytes 156008 | tf_op jit(solution)/shard_map/ppermute | solution.py:37
  27.0 4.1 %collective-permute-start.8 = (f32[4,3250]{1,0:T(4,128)S(1)}, f32[4,3250]{1,0:T(4,128)S(1)}, u32[]{:S(2)}, u32[]{:S(2)}) collective-permute-start(f32[4,3250]{1,0:T(4,128)S(1)} %get-tuple-element.32.refs_0_), channel_id=1, source_target_pairs={{0,2},{1,3},{2,0},{3,1},{4,6},{5,7},{6,4},{7,5},{8,10},{9,11},{10,... | collective-permute-start | bytes 156008 | tf_op jit(solution)/shard_map/ppermute | solution.py:37
  28.5 2.7 %collective-permute-start.9 = (f32[4,3250]{1,0:T(4,128)S(1)}, f32[4,3250]{1,0:T(4,128)S(1)}, u32[]{:S(2)}, u32[]{:S(2)}) collective-permute-start(f32[4,3250]{1,0:T(4,128)S(1)} %get-tuple-element.32.refs_0_), channel_id=1, source_target_pairs={{0,3},{1,0},{2,1},{3,2},{4,7},{5,4},{6,5},{7,6},{8,11},{9,8},{10,9... | collective-permute-start | bytes 156008 | tf_op jit(solution)/shard_map/ppermute | solution.py:37
  31.9 3.0 %collective-permute-start.10 = (f32[4,128]{1,0:T(4,128)S(1)}, f32[4,128]{1,0:T(4,128)S(1)}, u32[]{:S(2)}, u32[]{:S(2)}) collective-permute-start(f32[4,128]{1,0:T(4,128)S(1)} %get-tuple-element.34.refs_0_), channel_id=1, source_target_pairs={{0,1},{1,2},{2,3},{3,0},{4,5},{5,6},{6,7},{7,4},{8,9},{9,10},{10,1... | collective-permute-start | bytes 6152 | tf_op jit(solution)/shard_map/ppermute | solution.py:37
  32.6 3.6 %collective-permute-start.11 = (f32[4,128]{1,0:T(4,128)S(1)}, f32[4,128]{1,0:T(4,128)S(1)}, u32[]{:S(2)}, u32[]{:S(2)}) collective-permute-start(f32[4,128]{1,0:T(4,128)S(1)} %get-tuple-element.34.refs_0_), channel_id=1, source_target_pairs={{0,2},{1,3},{2,0},{3,1},{4,6},{5,7},{6,4},{7,5},{8,10},{9,11},{10,... | collective-permute-start | bytes 6152 | tf_op jit(solution)/shard_map/ppermute | solution.py:37
  33.8 2.4 %collective-permute-start.12 = (f32[4,128]{1,0:T(4,128)S(1)}, f32[4,128]{1,0:T(4,128)S(1)}, u32[]{:S(2)}, u32[]{:S(2)}) collective-permute-start(f32[4,128]{1,0:T(4,128)S(1)} %get-tuple-element.34.refs_0_), channel_id=1, source_target_pairs={{0,3},{1,0},{2,1},{3,2},{4,7},{5,4},{6,5},{7,6},{8,11},{9,8},{10,9... | collective-permute-start | bytes 6152 | tf_op jit(solution)/shard_map/ppermute | solution.py:37

commit v3 on v2

--- a/solution.py
+++ b/solution.py
@@ -17,6 +17,7 @@
 
 
 EPSILON = 1e-06
+PARTS = 4
 
 NT = (((1,), (1,)), ((), ()))
 F32 = jnp.float32
@@ -39,21 +40,50 @@
     ]
 
 
-def gather_xor(part, axis):
+def join(*refs):
+    *given, out_ref = refs
+    at = 0
+    for ref in given:
+        if ref.shape[1:] == out_ref.shape[1:]:
+            out_ref[at : at + ref.shape[0]] = ref[...]
+            at += ref.shape[0]
+
+
+def digits_of(size):
+    assert size & (size - 1) == 0
+    rounds, done, total = [], 0, size.bit_length() - 1
+    while done < total:
+        count = 1 if (total - done) % 2 else 2
+        rounds.append((done, count))
+        done += count
+    return rounds
+
+
+def gather_xor(part, axis, beside):
     size = lax.axis_size(axis)
-    assert size & (size - 1) == 0
-    digits = size.bit_length() - 1
     blocks = [part[None]]
-    done = 0
-    while done < digits:
-        held = blocks[0] if len(blocks) == 1 else jnp.concatenate(blocks)
-        wide = 1 if (digits - done) % 2 else 2
+    for place, count in digits_of(size):
+        held = blocks[0]
+        if len(blocks) > 1:
+            entries = sum(b.shape[0] for b in blocks)
+            (held,) = call(
+                join, (), (*blocks, *beside), (jax.ShapeDtypeStruct((entries, *part.shape), part.dtype),)
+            )
+            beside = ()
         blocks = [held] + [
-            lax.ppermute(held, axis, [(i, i ^ (step << done)) for i in range(size)])
-            for step in range(1, 1 << wide)
+            lax.ppermute(held, axis, [(i, i ^ (step << place)) for i in range(size)])
+            for step in range((1 << count) - 1, 0, -1)
         ]
-        done += wide
     return blocks
+
+
+def entry_of(away, size):
+    entry = jnp.int32(0)
+    for place, count in digits_of(size):
+        top = (1 << count) - 1
+        digit = lax.bitwise_and(lax.shift_right_logical(away, place), top)
+        entry = entry + lax.shift_left(lax.bitwise_and(top + 1 - digit, top), place)
+    return entry
 
 
 def stack_pieces(me, pieces, held):
@@ -62,27 +92,49 @@
         held[lax.rem(me - step + size, size)] = piece[...]
 
 
-def prepare(place_ref, source_ref, *refs, count):
-    rows = source_ref.shape[0]
-    given, (chosen_ref, base_ref, new_conv_ref, *kept), (conv_w, conv_b, conv_rows, sems) = (
-        refs[: count + 3], refs[count + 3 : -4], refs[-4:])
-    large, small = given[:count], given[count:]
-    copies = [
-        pltpu.make_async_copy(origin, to, sems.at[i])
-        for i, (origin, to) in enumerate(zip((*small, *large), (conv_w, conv_b, conv_rows, *kept)))
-    ]
+def cut(rows, count):
+    step = -(-rows // (16 * count)) * 16
+    return [(at, min(step, rows - at)) for at in range(0, rows, step)]
+
+
+def copies_of(pairs, sems):
+    copies = []
+    for origin, to in pairs:
+        if len(to.shape) == 2 and to.shape[0] >= 256:
+            ranges = [pl.ds(at, size) for at, size in cut(to.shape[0], PARTS)]
+            copies += [(origin.at[r], to.at[r]) for r in ranges]
+        else:
+            copies.append((origin, to))
+    return [pltpu.make_async_copy(origin, to, sems.at[i]) for i, (origin, to) in enumerate(copies)]
+
+
+def prepare(
+    place_ref, source_ref, gain_ref, conv_w_ref, conv_b_ref, conv_rows_ref, heads_ref, xproj_ref, xz_ref,
+    chosen_ref, base_ref, new_conv_ref, gain_out, heads_out, xproj_out, in_out,
+    source, gain, conv_w, conv_b, conv_rows, sems,
+):
+    rows = source.shape[0]
+    small = (
+        (source_ref, source), (gain_ref, gain), (conv_w_ref, conv_w), (conv_b_ref, conv_b),
+        (conv_rows_ref, conv_rows),
+    )
+    copies = copies_of(
+        small + ((heads_ref, heads_out), (xz_ref.at[0], in_out), (xproj_ref, xproj_out)), sems
+    )
     for copy in copies:
         copy.start()
+    for copy in copies[: len(small)]:
+        copy.wait()
     slots = chosen_ref.shape[1]
     row_id = lax.broadcasted_iota(jnp.int32, (8, slots), 0)
     wanted = jnp.full((8, slots), -1, jnp.int32)
     for r in range(rows):
-        origin = lax.bitwise_xor(lax.div(source_ref[r], rows), place_ref[0])
-        wanted = jnp.where(row_id == r, origin * rows + lax.rem(source_ref[r], rows), wanted)
+        away = lax.bitwise_xor(lax.div(source[r], rows), place_ref[0])
+        entry = entry_of(away, slots // rows)
+        wanted = jnp.where(row_id == r, entry * rows + lax.rem(source[r], rows), wanted)
     chosen = lax.broadcasted_iota(jnp.int32, (8, slots), 1) == wanted
     chosen_ref[...] = jnp.where(chosen, 1.0, 0.0)
-    for copy in copies[:3]:
-        copy.wait()
+    gain_out[...] = gain[...][None]
     taps = conv_rows.shape[0]
     base = conv_b[...]
     for tap in range(taps):
@@ -92,14 +144,22 @@
     for tap in range(taps - 1):
         new_conv_ref[tap] = conv_rows[tap + 1]
     new_conv_ref[taps - 1] = jnp.zeros_like(conv_rows[0])
-    for copy in copies[3:]:
+    for copy in copies[len(small) :]:
+        copy.wait()
+
+
+def bring(after_ref, xz_ref, gate_out, sems):
+    copies = copies_of(((xz_ref.at[1], gate_out),), sems)
+    for copy in copies:
+        copy.start()
+    for copy in copies:
         copy.wait()
 
 
 def project_in(me_ref, *refs, size):
     arrived_refs = refs[:size]
-    (chosen_ref, base_ref, old_conv_ref, gain_ref, heads_w_ref, xz_w_ref, xproj_ref, part_ref,
-     act_ref, gate_ref, new_conv_ref, cols_ref, blocks) = refs[size:]
+    (chosen_ref, base_ref, old_conv_ref, gain_ref, heads_w_ref, xproj_ref, in_w_ref, gate_w_ref,
+     part_ref, act_ref, gate_ref, new_conv_ref, cols_ref, blocks) = refs[size:]
     rows, cols = cols_ref.shape
     arrived = jnp.concatenate(
         [ref[i].astype(F32) for ref in arrived_refs for i in range(ref.shape[0])], axis=0
@@ -111,8 +171,8 @@
     scale = lax.rsqrt(jnp.mean(routed * routed, axis=1, keepdims=True) + EPSILON)
     normed = (routed * scale * gain_ref[...]).astype(BF16)
     heads = dot_nt(normed, heads_w_ref[...])[:rows].astype(BF16).astype(F32)
-    channel_in = dot_nt(normed, xz_w_ref[0])[:rows]
-    gate = dot_nt(normed, xz_w_ref[1])[:rows]
+    channel_in = dot_nt(normed, in_w_ref[...])[:rows]
+    gate = dot_nt(normed, gate_w_ref[...])[:rows]
     taps = old_conv_ref.shape[0]
     conv_out = base_ref[:rows] + base_ref[rows:] * channel_in
     act = conv_out * sigmoid(conv_out)
@@ -125,21 +185,14 @@
     part_ref[...] = jnp.concatenate([heads, state], axis=1)
 
 
-def mix(
-    me_ref, lengths_ref, *refs, size, head_width,
-):
+def state_step(me_ref, *refs, size, head_width):
     pieces = refs[:size]
-    (keys_ref, values_ref, act_ref, gate_ref, dt_w_ref, dt_b_ref, a_log_ref, ssm_ref, skip_ref,
-     out_w_ref, part_ref, new_ssm_ref, new_kv_ref, held) = refs[size:]
-    me = me_ref[0]
-    stack_pieces(me, pieces, held)
-    rows = held.shape[1]
-    heads = jnp.concatenate([held[i][:, :head_width] for i in range(size)], axis=1)
-    state = held[0][:, head_width:]
-    for i in range(1, size):
-        state = state + held[i][:, head_width:]
-    new_kv_ref[...] = heads[:, QUERY_WIDTH:].astype(BF16)
-
+    (act_ref, gate_ref, dt_w_ref, dt_b_ref, a_log_ref, ssm_ref, skip_ref, out_w_ref, part_ref,
+     new_ssm_ref) = refs[size:]
+    state = pieces[0][:, head_width:]
+    for piece in pieces[1:]:
+        state = state + piece[:, head_width:]
+    rows = state.shape[0]
     rank = dt_w_ref.shape[1]
     depth = a_log_ref.shape[0]
     step = dot_nt(state[:, :rank].astype(BF16), dt_w_ref[...]) + dt_b_ref[...]
@@ -160,7 +213,17 @@
         outs.append(jnp.sum(maps[depth : 2 * depth, r : r + 1] * fresh, axis=0, keepdims=True))
     state_out = jnp.concatenate(outs, axis=0) + skip_ref[...] * act
     ssm_heads = (state_out * gate_ref[...]).astype(BF16)
-    y_part = jnp.dot(ssm_heads, out_w_ref[...], preferred_element_type=F32)
+    part_ref[...] = jnp.dot(ssm_heads, out_w_ref[...], preferred_element_type=F32).astype(BF16)
+
+
+def attend(me_ref, lengths_ref, *refs, size, head_width):
+    pieces = refs[:size]
+    (keys_ref, values_ref, part_ref, new_kv_ref, held) = refs[size:]
+    me = me_ref[0]
+    stack_pieces(me, pieces, held)
+    rows = held.shape[1]
+    heads = jnp.concatenate([held[i][:, :head_width] for i in range(size)], axis=1)
+    new_kv_ref[...] = heads[:, QUERY_WIDTH:].astype(BF16)
 
     span = keys_ref.shape[2]
     tall = jnp.concatenate([heads, jnp.zeros((8 - rows, heads.shape[1]), F32)], axis=0)
@@ -215,21 +278,15 @@
             numers.append(numer[8 * j : 8 * j + 8])
             tops.append(top[8 * j : 8 * j + 8])
             totals.append(total[8 * j : 8 * j + 8])
-    line = jnp.concatenate(numers + tops + totals, axis=1)[:rows]
-    part_ref[:, : line.shape[1]] = line
-    part_ref[:, line.shape[1] :] = y_part
-
-
-def project_out(
-    me_ref, *refs, size,
-):
+    part_ref[...] = jnp.concatenate(numers + tops + totals, axis=1)[:rows]
+
+
+def project_out(*refs, size):
     pieces = refs[:size]
-    (spread_ref, w_ref, cols_ref, gain_ref, y_ref, base_ref, square_ref, blocks) = refs[size:]
-    rows = cols_ref.shape[0]
-    cols = cols_ref.shape[1]
-    lows = QUERY_WIDTH
-    tops = [p[:, lows : lows + QUERY_HEADS] for p in pieces]
-    totals = [p[:, lows + QUERY_HEADS : lows + 2 * QUERY_HEADS] for p in pieces]
+    (state_ref, spread_ref, w_ref, y_ref, part_ref) = refs[size:]
+    rows = y_ref.shape[0]
+    tops = [p[:, QUERY_WIDTH : QUERY_WIDTH + QUERY_HEADS] for p in pieces]
+    totals = [p[:, QUERY_WIDTH + QUERY_HEADS :] for p in pieces]
     top = functools.reduce(jnp.maximum, tops)
     factors = [jnp.exp(t - top) for t in tops]
     total = functools.reduce(jnp.add, [f * t for f, t in zip(factors, totals)])
@@ -245,23 +302,33 @@
     )
     y_attn = dot_nt(merged.astype(BF16), w_ref[...])
     y_ref[...] = y_attn
-    square_ref[...] = jnp.broadcast_to(
-        jnp.sum(y_attn * y_attn, axis=1, keepdims=True), square_ref.shape
-    )
-    lows = lows + 2 * QUERY_HEADS
-    y_ssm = functools.reduce(jnp.add, [p[:, lows : lows + MODEL_WIDTH] for p in pieces])
-    scale = lax.rsqrt(jnp.mean(y_ssm * y_ssm, axis=1, keepdims=True) + EPSILON)
+    square = jnp.sum(y_attn * y_attn, axis=1, keepdims=True)
+    high = square.astype(BF16)
+    rest = square - high.astype(F32)
+    low = rest.astype(BF16)
+    lowest = (rest - low.astype(F32)).astype(BF16)
+    part_ref[...] = jnp.concatenate(
+        [state_ref[...], high, low, lowest, jnp.zeros((rows, part_ref.shape[1] - MODEL_WIDTH - 3), BF16)],
+        axis=1,
+    )
+
+
+def finish(me_ref, *refs, size):
+    pieces = refs[:size]
+    y_ref, cols_ref, gain_attn_ref, gain_ssm_ref, out_ref, blocks = refs[size:]
+    cols = out_ref.shape[1]
+    total = functools.reduce(jnp.add, [p[...].astype(F32) for p in pieces])
+    square = jnp.sum(total[:, MODEL_WIDTH : MODEL_WIDTH + 3], axis=1, keepdims=True)
+    attn_scale = lax.rsqrt(square / MODEL_WIDTH + EPSILON)
+    y_ssm = total[:, :MODEL_WIDTH]
+    state_scale = lax.rsqrt(jnp.mean(y_ssm * y_ssm, axis=1, keepdims=True) + EPSILON)
     for block in range(blocks.shape[0]):
         blocks[block] = y_ssm[:, block * cols : (block + 1) * cols]
-    base_ref[...] = cols_ref[...] + 0.5 * (blocks[me_ref[0]] * scale * gain_ref[...])
-
-
-def finish(*refs, size):
-    squares = refs[:size]
-    y_ref, base_ref, gain_ref, out_ref = refs[size:]
-    square = functools.reduce(jnp.add, [s[:, :1] for s in squares])
-    scale = lax.rsqrt(square / MODEL_WIDTH + EPSILON)
-    out_ref[...] = (base_ref[...] + 0.5 * (y_ref[...] * scale * gain_ref[...])).astype(BF16)
+    mixed = 0.5 * (
+        y_ref[...] * attn_scale * gain_attn_ref[...]
+        + blocks[me_ref[0]] * state_scale * gain_ssm_ref[...]
+    )
+    out_ref[...] = (cols_ref[...] + mixed).astype(BF16)
 
 
 SMEM = pl.BlockSpec(memory_space=pltpu.SMEM)
@@ -310,36 +377,44 @@
     shape = jax.ShapeDtypeStruct
 
     place = lax.axis_index("wide").astype(jnp.int32).reshape(1)
-    arrived = gather_xor(tokens, "wide")
-
-    large = (
-        norm_gain[None], query_key_value_weight.T, w_xz.transpose(1, 2, 0), w_xproj.T,
-    )
-    small = (conv_weight, conv_bias[None], conv_state.transpose(1, 0, 2))
+    large = (query_key_value_weight.T, w_xproj.T, w_xz.transpose(1, 2, 0))
+    small = (source, norm_gain, conv_weight, conv_bias[None], conv_state.transpose(1, 0, 2))
     slots = rows * lax.axis_size("wide")
+    half = large[2].shape[1:]
+    pinned = [pltpu.with_memory_space_constraint(a, pltpu.HBM) for a in small + large]
     anywhere = pl.BlockSpec(memory_space=pl.ANY)
     prepared = pl.pallas_call(
-        functools.partial(prepare, count=len(large)),
-        in_specs=[SMEM] * 2 + [anywhere] * (len(large) + len(small)),
-        out_specs=[VMEM] * (3 + len(large)),
+        prepare,
+        in_specs=[SMEM] + [anywhere] * len(pinned),
+        out_specs=[VMEM] * 7,
         out_shape=[
             pltpu.VMEM((8, slots), F32),
             pltpu.VMEM((2 * rows, cols), F32),
-            pltpu.VMEM(small[2].shape, BF16),
-            *(pltpu.VMEM(a.shape, a.dtype) for a in large),
+            pltpu.VMEM(small[4].shape, BF16),
+            pltpu.VMEM((1, MODEL_WIDTH), F32),
+            pltpu.VMEM(large[0].shape, BF16),
+            pltpu.VMEM(large[1].shape, BF16),
+            pltpu.VMEM(half, BF16),
         ],
-        scratch_shapes=[pltpu.VMEM(a.shape, a.dtype) for a in small]
-        + [pltpu.SemaphoreType.DMA((len(large) + len(small),))],
+        scratch_shapes=[pltpu.SMEM(source.shape, jnp.int32)]
+        + [pltpu.VMEM(a.shape, a.dtype) for a in small[1:]]
+        + [pltpu.SemaphoreType.DMA((6 + 2 * (PARTS + 1),))],
         compiler_params=pltpu.CompilerParams(vmem_limit_bytes=4 * 1024 * 1024),
-        cost_estimate=pl.CostEstimate(
-            flops=0, transcendentals=0, bytes_accessed=2 * sum(a.size * a.dtype.itemsize for a in large)
-        ),
-    )(place, source, *(pltpu.with_memory_space_constraint(a, pltpu.HBM) for a in large + small))
+    )(place, *pinned)
+    arrived = gather_xor(tokens, "wide", prepared[:1])
+    (gate_w,) = pl.pallas_call(
+        bring,
+        in_specs=[anywhere] * 2,
+        out_specs=[VMEM],
+        out_shape=[pltpu.VMEM(half, BF16)],
+        scratch_shapes=[pltpu.SemaphoreType.DMA((PARTS + 1,))],
+        compiler_params=pltpu.CompilerParams(vmem_limit_bytes=4 * 1024 * 1024),
+    )(arrived[0], pinned[-1])
     part_width = head_width + w_xproj.shape[1]
     part, act, gate, new_conv, routed_cols = call(
         functools.partial(project_in, size=len(arrived)),
         (me,),
-        (*arrived, *prepared),
+        (*arrived, *prepared, gate_w),
         (
             shape((rows, part_width), F32),
             shape((rows, cols), F32),
@@ -350,52 +425,42 @@
         (pltpu.VMEM((narrow, rows, cols), F32),),
     )
     pieces = exchange(part, "narrow")
-    second_width = QUERY_WIDTH + 2 * QUERY_HEADS + MODEL_WIDTH
-    part, new_ssm, new_kv = call(
-        functools.partial(mix, size=narrow, head_width=head_width),
+    second, new_kv = call(
+        functools.partial(attend, size=narrow, head_width=head_width),
         (me, lengths),
+        (*pieces, cached_key_rows.transpose(0, 2, 1), cached_value_rows.transpose(0, 2, 1)),
         (
-            *pieces,
-            cached_key_rows.transpose(0, 2, 1),
-            cached_value_rows.transpose(0, 2, 1),
-            act,
-            gate,
-            w_dt.T,
-            dt_bias[None],
-            a_log,
-            ssm_state,
-            skip_d[None],
-            w_ssm_out,
-        ),
-        (
-            shape((rows, second_width), F32),
-            shape(ssm_state.shape, F32),
+            shape((rows, QUERY_WIDTH + 2 * QUERY_HEADS), F32),
             shape((rows, 2 * KEY_VALUE_WIDTH), BF16),
         ),
         (pltpu.VMEM((narrow, rows, part_width), F32),),
     )
-    pieces = exchange(part, "narrow")
+    state_part, new_ssm = call(
+        functools.partial(state_step, size=narrow, head_width=head_width),
+        (me,),
+        (
+            *pieces, act, gate, w_dt.T, dt_bias[None], a_log, ssm_state, skip_d[None], w_ssm_out,
+        ),
+        (shape((rows, MODEL_WIDTH), BF16), shape(ssm_state.shape, F32)),
+    )
+    pieces = exchange(second, "narrow")
     spread = (
         lax.broadcasted_iota(jnp.int32, (QUERY_HEADS, QUERY_WIDTH), 1) // HEAD_SIZE
         == lax.broadcasted_iota(jnp.int32, (QUERY_HEADS, QUERY_WIDTH), 0)
     ).astype(BF16)
-    y_attn, base, square = call(
+    y_attn, third = call(
         functools.partial(project_out, size=narrow),
-        (me,),
-        (*pieces, spread, w_attn_out.T, routed_cols, gain_ssm[None]),
-        (
-            shape((rows, cols), F32),
-            shape((rows, cols), F32),
-            shape((rows, 128), F32),
-        ),
-        (pltpu.VMEM((narrow, rows, cols), F32),),
-    )
-    squares = exchange(square, "narrow")
+        (),
+        (*pieces, state_part, spread, w_attn_out.T),
+        (shape((rows, cols), F32), shape((rows, MODEL_WIDTH + 64), BF16)),
+    )
+    pieces = exchange(third, "narrow")
     (out,) = call(
         functools.partial(finish, size=narrow),
-        (),
-        (*squares, y_attn, base, gain_attn[None]),
+        (me,),
+        (*pieces, y_attn, routed_cols, gain_attn[None], gain_ssm[None]),
         (shape((rows, cols), BF16),),
+        (pltpu.VMEM((narrow, rows, cols), F32),),
     )
     return (out, new_kv, new_conv.transpose(1, 0, 2), new_ssm)
 

time: 37.4 us -> 34.4 us (0.920)
  local copies, waits for them, and re-layouts: 2.01 us -> 0.06 us
  Pallas kernels: 9.63 us -> 10.6 us
  waiting for transfers between devices: 7.69 us -> 6.74 us
  other arithmetic: 0.77 us -> 0.04 us
    broadcast_in_dim x1 -> x0, local copies, waits for them, and re-layouts: 1.29 us -> none  [shards(): norm_gain[None]]
    ppermute x9, waiting for transfers between devices: 5.11 us -> 3.95 us  [exchange(): lax.ppermute(part, axis, [(i, (i + step) % size) for i in range(size)])]
    concatenate x1 -> x0, other arithmetic: 0.73 us -> none  [gather_xor(): held = blocks[0] if len(blocks) == 1 else jnp.concatenate(blocks)]
    unnamed x26, local copies, waits for them, and re-layouts: 0.71 us -> 0.06 us
    pallas_call x4 -> x6, Pallas kernels: 6.65 us -> 7.17 us  [call(): pl.pallas_call(body, in_specs=[SMEM] * len(scalars) + [VMEM] * len(blocks...]
    pallas_call x1 -> x2, Pallas kernels: 2.98 us -> 3.39 us  [the longest x1 2.08 us: shards(): pl.pallas_call(prepare, in_specs=[SMEM] + [anywhere] * len(pinned), out_s...]
  transfers between devices with their start and end apart: 13 -> 13, of which waited for: 9 -> 8; matrix products, arithmetic and copies ran while one was open for 4% -> 0% of each run, Pallas kernels for 8% -> 13%
where the time goes in v3:
time: 34.4 us; the launch traced here: 34.2 us
  starting transfers between devices  16 us (47%)
  Pallas kernels  10.6 us (31%)
  waiting for transfers between devices  6.74 us (20%)
  between operations  0.8 us (2%)
    ppermute x9, starting transfers between devices, exchange(): lax.ppermute(part, axis, [(i, (i + step) % size) for i in range(size)])  8.41 us
    ppermute x4, starting transfers between devices, gather_xor(): lax.ppermute(held, axis, [(i, i ^ step << place) for i in range(size)])  7.55 us
    pallas_call x6, Pallas kernels, call(): pl.pallas_call(body, in_specs=[SMEM] * len(scalars) + [VMEM] * len(blocks...  7.17 us
    ppermute x9, waiting for transfers between devices, exchange(): lax.ppermute(part, axis, [(i, (i + step) % size) for i in range(size)])  3.95 us
    ppermute x4, waiting for transfers between devices, gather_xor(): lax.ppermute(held, axis, [(i, i ^ step << place) for i in range(size)])  2.79 us
    pallas_call x1, Pallas kernels, shards(): pl.pallas_call(prepare, in_specs=[SMEM] + [anywhere] * len(pinned), out_s...  2.08 us
    pallas_call x1, Pallas kernels, shards(): pl.pallas_call(bring, in_specs=[anywhere] * 2, out_specs=[VMEM], out_shap...  1.31 us
  transfers between devices with their start and end apart: 13, of which 8 were waited for; matrix products, arithmetic and copies ran while one was open for 0% of the time, Pallas kernels for 13%

profile of v3, /device:TPU:0, one launch (start us, length us, event | category | flops | bytes accessed | tf_op | source)
XLA Modules:
  0.0 34.2 jit_solution(3994274616849325112)
XLA Ops:
  0.6 3.0 %collective-permute-start = (bf16[1,4,1600]{2,1,0:T(4,128)(2,1)}, bf16[1,4,1600]{2,1,0:T(4,128)(2,1)S(1)}, u32[]{:S(2)}, u32[]{:S(2)}) collective-permute-start(bf16[1,4,1600]{2,1,0:T(4,128)(2,1)} %bitcast.21), channel_id=1, source_target_pairs={{0,4},{4,0},{8,12},{12,8},{16,20},{20,16},{24,28},{28,24},{1,5},{5... | collective-permute-start | bytes 38408 | tf_op jit(solution)/shard_map/ppermute | solution.py:74
  3.7 2.1 %shard_map.228 = (f32[8,32]{1,0:T(8,128)S(1)}, f32[8,400]{1,0:T(8,128)S(1)}, bf16[3,4,400]{2,1,0:T(4,128)(2,1)S(1)}, f32[1,1600]{1,0:T(1,128)S(1)}, bf16[560,160...) custom-call(s32[1]{0:T(128)} %bitcast.2.place_ref, s32[4]{0:T(128)} %source_ref.1, ...), custom_call_target="tpu_custom_call" | custom-call | tf_op jit(solution)/shard_map/pallas_call | solution.py:386
  5.8 3.9 %collective-permute-start.1 = (bf16[2,4,1600]{2,1,0:T(4,128)(2,1)S(1)}, bf16[2,4,1600]{2,1,0:T(4,128)(2,1)S(1)}, u32[]{:S(2)}, u32[]{:S(2)}) collective-permute-start(bf16[2,4,1600]{2,1,0:T(4,128)(2,1)S(1)} %shard_map.229.after_ref.refs_0_), channel_id=1, source_target_pairs={{0,24},{4,28},{8,16},{12,20},{16,8},{20,12},{24,0},{28,4},{1,25},{... | collective-permute-start | bytes 76808 | tf_op jit(solution)/shard_map/ppermute | solution.py:74
  9.7 0.6 %collective-permute-start.3 = (bf16[2,4,1600]{2,1,0:T(4,128)(2,1)S(1)}, bf16[2,4,1600]{2,1,0:T(4,128)(2,1)S(1)}, u32[]{:S(2)}, u32[]{:S(2)}) collective-permute-start(bf16[2,4,1600]{2,1,0:T(4,128)(2,1)S(1)} %shard_map.229.after_ref.refs_0_), channel_id=1, source_target_pairs={{0,8},{4,12},{8,0},{12,4},{16,24},{20,28},{24,16},{28,20},{1,9},{5... | collective-permute-start | bytes 76808 | tf_op jit(solution)/shard_map/ppermute | solution.py:74
  10.3 1.3 %shard_map.230.refs_11_ = bf16[400,1600]{1,0:T(8,128)(2,1)S(1)} custom-call(bf16[2,4,1600]{2,1,0:T(4,128)(2,1)S(1)} %shard_map.229.after_ref.refs_0_, bf16[2,400,1600]{2,1,0:T(8,128)(2,1)} %bitcast.28), custom_call_target="tpu_custom_call" | custom-call | tf_op jit(solution)/shard_map/pallas_call | solution.py:405
  11.6 0.1 collective-permute-done.1.refs_1_
  11.8 2.6 %collective-permute-done.2.refs_2_ = bf16[2,4,1600]{2,1,0:T(4,128)(2,1)S(1)} collective-permute-done((bf16[2,4,1600]{2,1,0:T(4,128)(2,1)S(1)}, bf16[2,4,1600]{2,1,0:T(4,128)(2,1)S(1)}, u32[]{:S(2)}, u32[]{:S(2)}) %collective-permute-start.2) | collective-permute-done | bytes 25632 | tf_op jit(solution)/shard_map/ppermute | solution.py:74
  14.4 0.0 copy-start.5
  14.4 2.0 %shard_map.231 = (f32[4,692]{1,0:T(4,128)S(1)}, f32[4,400]{1,0:T(4,128)S(1)}, f32[4,400]{1,0:T(4,128)S(1)}, bf16[3,4,400]{2,1,0:T(4,128)(2,1)}, f32[4,400]{1,0:T(4,128)S(1)}) custom-call(s32[1]{0:T(128)} %bitcast.me_ref, bf16[2,4,1600]{2,1,0:T(4,128)(2,1)S(1)} %shard_map.229.after_ref.refs_0_, bf16[2,4,1600]{2,1,0:T(4,128)(2,1)S(1)} %collective-permute-done.1.refs_1_, ...), custom_call_target="tpu_custom_call" | custom-call | tf_op jit(solution)/shard_map/pallas_call | solution.py:339
  16.4 0.0 copy-start.9
  16.4 0.1 collective-permute-start.4
  16.5 1.6 %collective-permute-start.5 = (f32[4,692]{1,0:T(4,128)S(1)}, f32[4,692]{1,0:T(4,128)S(1)}, u32[]{:S(2)}, u32[]{:S(2)}) collective-permute-start(f32[4,692]{1,0:T(4,128)S(1)} %get-tuple-element.29.refs_0_), channel_id=1, source_target_pairs={{0,2},{1,3},{2,0},{3,1},{4,6},{5,7},{6,4},{7,5},{8,10},{9,11},{10,... | collective-permute-start | bytes 33224 | tf_op jit(solution)/shard_map/ppermute | solution.py:38
  18.1 1.4 %collective-permute-start.6 = (f32[4,692]{1,0:T(4,128)S(1)}, f32[4,692]{1,0:T(4,128)S(1)}, u32[]{:S(2)}, u32[]{:S(2)}) collective-permute-start(f32[4,692]{1,0:T(4,128)S(1)} %get-tuple-element.29.refs_0_), channel_id=1, source_target_pairs={{0,3},{1,0},{2,1},{3,2},{4,7},{5,4},{6,5},{7,6},{8,11},{9,8},{10,9... | collective-permute-start | bytes 33224 | tf_op jit(solution)/shard_map/ppermute | solution.py:38
  19.5 0.2 collective-permute-done.4.refs_1_
  19.6 0.7 %collective-permute-done.5.refs_2_ = f32[4,692]{1,0:T(4,128)S(1)} collective-permute-done((f32[4,692]{1,0:T(4,128)S(1)}, f32[4,692]{1,0:T(4,128)S(1)}, u32[]{:S(2)}, u32[]{:S(2)}) %collective-permute-start.5) | collective-permute-done | bytes 11104 | tf_op jit(solution)/shard_map/ppermute | solution.py:38
  20.3 0.6 %collective-permute-done.6.refs_3_ = f32[4,692]{1,0:T(4,128)S(1)} collective-permute-done((f32[4,692]{1,0:T(4,128)S(1)}, f32[4,692]{1,0:T(4,128)S(1)}, u32[]{:S(2)}, u32[]{:S(2)}) %collective-permute-start.6) | collective-permute-done | bytes 11104 | tf_op jit(solution)/shard_map/ppermute | solution.py:38
  20.9 2.7 %shard_map.232 = (f32[4,1650]{1,0:T(4,128)S(1)}, bf16[4,640]{1,0:T(4,128)(2,1)}) custom-call(s32[1]{0:T(128)} %bitcast.me_ref, s32[4]{0:T(128)S(1)} %copy-done.12, f32[4,692]{1,0:T(4,128)S(1)} %get-tuple-element.29.refs_0_, f32[4,692]{1,0:T(4,128)S(1)} %collective-permute-done.4.refs_1_, f32[4,692]{1,0:T(4,128)S(1)} %collective-permute-done.5.refs_2_, ...), custom_call_target="tpu_custom_call" | custom-call | tf_op jit(solution)/shard_map/pallas_call | solution.py:339
  23.6 0.6 %collective-permute-start.7 = (f32[4,1650]{1,0:T(4,128)S(1)}, f32[4,1650]{1,0:T(4,128)S(1)}, u32[]{:S(2)}, u32[]{:S(2)}) collective-permute-start(f32[4,1650]{1,0:T(4,128)S(1)} %get-tuple-element.30.refs_0_), channel_id=1, source_target_pairs={{0,1},{1,2},{2,3},{3,0},{4,5},{5,6},{6,7},{7,4},{8,9},{9,10},{10,1... | collective-permute-start | bytes 79208 | tf_op jit(solution)/shard_map/ppermute | solution.py:38
  24.2 1.5 %collective-permute-start.8 = (f32[4,1650]{1,0:T(4,128)S(1)}, f32[4,1650]{1,0:T(4,128)S(1)}, u32[]{:S(2)}, u32[]{:S(2)}) collective-permute-start(f32[4,1650]{1,0:T(4,128)S(1)} %get-tuple-element.30.refs_0_), channel_id=1, source_target_pairs={{0,2},{1,3},{2,0},{3,1},{4,6},{5,7},{6,4},{7,5},{8,10},{9,11},{10,... | collective-permute-start | bytes 79208 | tf_op jit(solution)/shard_map/ppermute | solution.py:38
  25.7 0.3 collective-permute-start.9
  26.1 0.0 copy-start.10
  26.1 0.0 copy-start.11
  26.1 0.9 %shard_map.233 = (bf16[4,1600]{1,0:T(4,128)(2,1)S(1)}, f32[4,16,400]{2,1,0:T(8,128)}) custom-call(s32[1]{0:T(128)} %bitcast.me_ref, f32[4,692]{1,0:T(4,128)S(1)} %get-tuple-element.29.refs_0_, f32[4,692]{1,0:T(4,128)S(1)} %collective-permute-done.4.refs_1_, f32[4,692]{1,0:T(4,128)S(1)} %collective-permute-done.5.refs_2_, ...), custom_call_target="tpu_custom_call" | custom-call | tf_op jit(solution)/shard_map/pallas_call | solution.py:339
  27.1 1.0 %collective-permute-done.8.refs_2_ = f32[4,1650]{1,0:T(4,128)S(1)} collective-permute-done((f32[4,1650]{1,0:T(4,128)S(1)}, f32[4,1650]{1,0:T(4,128)S(1)}, u32[]{:S(2)}, u32[]{:S(2)}) %collective-permute-start.8) | collective-permute-done | bytes 26432 | tf_op jit(solution)/shard_map/ppermute | solution.py:38
  28.1 0.0 collective-permute-done.9.refs_3_
  28.1 0.8 %shard_map.234 = (f32[4,400]{1,0:T(4,128)S(1)}, bf16[4,1664]{1,0:T(4,128)(2,1)S(1)}) custom-call(f32[4,1650]{1,0:T(4,128)S(1)} %get-tuple-element.30.refs_0_, f32[4,1650]{1,0:T(4,128)S(1)} %collective-permute-done.7.refs_1_, f32[4,1650]{1,0:T(4,128)S(1)} %collective-permute-done.8.refs_2_, f32[4,1650]{1,0:T(4,128)S(1)} %collective-permute-done.9.refs_3_, ...), custom_call_target="tpu_custom_call" | custom-call | tf_op jit(solution)/shard_map/pallas_call | solution.py:339
  28.9 0.7 %collective-permute-start.10 = (bf16[4,1664]{1,0:T(4,128)(2,1)S(1)}, bf16[4,1664]{1,0:T(4,128)(2,1)S(1)}, u32[]{:S(2)}, u32[]{:S(2)}) collective-permute-start(bf16[4,1664]{1,0:T(4,128)(2,1)S(1)} %get-tuple-element.34.refs_0_), channel_id=1, source_target_pairs={{0,1},{1,2},{2,3},{3,0},{4,5},{5,6},{6,7},{7,4},{8,9},{9,10},{10,1... | collective-permute-start | bytes 39944 | tf_op jit(solution)/shard_map/ppermute | solution.py:38
  29.5 1.0 %collective-permute-start.11 = (bf16[4,1664]{1,0:T(4,128)(2,1)S(1)}, bf16[4,1664]{1,0:T(4,128)(2,1)S(1)}, u32[]{:S(2)}, u32[]{:S(2)}) collective-permute-start(bf16[4,1664]{1,0:T(4,128)(2,1)S(1)} %get-tuple-element.34.refs_0_), channel_id=1, source_target_pairs={{0,2},{1,3},{2,0},{3,1},{4,6},{5,7},{6,4},{7,5},{8,10},{9,11},{10,... | collective-permute-start | bytes 39944 | tf_op jit(solution)/shard_map/ppermute | solution.py:38
  30.5 1.4 %collective-permute-start.12 = (bf16[4,1664]{1,0:T(4,128)(2,1)S(1)}, bf16[4,1664]{1,0:T(4,128)(2,1)S(1)}, u32[]{:S(2)}, u32[]{:S(2)}) collective-permute-start(bf16[4,1664]{1,0:T(4,128)(2,1)S(1)} %get-tuple-element.34.refs_0_), channel_id=1, source_target_pairs={{0,3},{1,0},{2,1},{3,2},{4,7},{5,4},{6,5},{7,6},{8,11},{9,8},{10,9... | collective-permute-start | bytes 39944 | tf_op jit(solution)/shard_map/ppermute | solution.py:38
  31.9 0.2 collective-permute-done.10.refs_1_
  32.0 1.4 %collective-permute-done.11.refs_2_ = bf16[4,1664]{1,0:T(4,128)(2,1)S(1)} collective-permute-done((bf16[4,1664]{1,0:T(4,128)(2,1)S(1)}, bf16[4,1664]{1,0:T(4,128)(2,1)S(1)}, u32[]{:S(2)}, u32[]{:S(2)}) %collective-permute-start.11) | collective-permute-done | bytes 13344 | tf_op jit(solution)/shard_map/ppermute | solution.py:38
  33.4 0.8 %shard_map.235 = bf16[4,400]{1,0:T(4,128)(2,1)} custom-call(s32[1]{0:T(128)} %bitcast.me_ref, bf16[4,1664]{1,0:T(4,128)(2,1)S(1)} %get-tuple-element.34.refs_0_, bf16[4,1664]{1,0:T(4,128)(2,1)S(1)} %collective-permute-done.10.refs_1_, bf16[4,1664]{1,0:T(4,128)(2,1)S(1)} %collective-permute-done.11.refs_2_, ...), custom_call_target="tpu_custom_call" | custom-call | tf_op jit(solution)/shard_map/pallas_call | solution.py:339
  (31 shorter events, 0.1 us)
Async XLA Ops:
  0.6 5.1 %collective-permute-start = (bf16[1,4,1600]{2,1,0:T(4,128)(2,1)}, bf16[1,4,1600]{2,1,0:T(4,128)(2,1)S(1)}, u32[]{:S(2)}, u32[]{:S(2)}) collective-permute-start(bf16[1,4,1600]{2,1,0:T(4,128)(2,1)} %bitcast.21), channel_id=1, source_target_pairs={{0,4},{4,0},{8,12},{12,8},{16,20},{20,16},{24,28},{28,24},{1,5},{5... | collective-permute-start | bytes 38408 | tf_op jit(solution)/shard_map/ppermute | solution.py:74
  3.7 2.1 %copy-start.7 = (bf16[4,1600]{1,0:T(4,128)(2,1)S(1)}, bf16[4,1600]{1,0:T(4,128)(2,1)}, u32[]{:S(2)}) copy-start(bf16[4,1600]{1,0:T(4,128)(2,1)} %param.21) | copy-start | bytes 38404
  5.8 6.0 %collective-permute-start.1 = (bf16[2,4,1600]{2,1,0:T(4,128)(2,1)S(1)}, bf16[2,4,1600]{2,1,0:T(4,128)(2,1)S(1)}, u32[]{:S(2)}, u32[]{:S(2)}) collective-permute-start(bf16[2,4,1600]{2,1,0:T(4,128)(2,1)S(1)} %shard_map.229.after_ref.refs_0_), channel_id=1, source_target_pairs={{0,24},{4,28},{8,16},{12,20},{16,8},{20,12},{24,0},{28,4},{1,25},{... | collective-permute-start | bytes 76808 | tf_op jit(solution)/shard_map/ppermute | solution.py:74
  9.7 4.7 %collective-permute-start.2 = (bf16[2,4,1600]{2,1,0:T(4,128)(2,1)S(1)}, bf16[2,4,1600]{2,1,0:T(4,128)(2,1)S(1)}, u32[]{:S(2)}, u32[]{:S(2)}) collective-permute-start(bf16[2,4,1600]{2,1,0:T(4,128)(2,1)S(1)} %shard_map.229.after_ref.refs_0_), channel_id=1, source_target_pairs={{0,16},{4,20},{8,24},{12,28},{16,0},{20,4},{24,8},{28,12},{1,17},{... | collective-permute-start | bytes 76808 | tf_op jit(solution)/shard_map/ppermute | solution.py:74
  9.7 4.7 %collective-permute-start.3 = (bf16[2,4,1600]{2,1,0:T(4,128)(2,1)S(1)}, bf16[2,4,1600]{2,1,0:T(4,128)(2,1)S(1)}, u32[]{:S(2)}, u32[]{:S(2)}) collective-permute-start(bf16[2,4,1600]{2,1,0:T(4,128)(2,1)S(1)} %shard_map.229.after_ref.refs_0_), channel_id=1, source_target_pairs={{0,8},{4,12},{8,0},{12,4},{16,24},{20,28},{24,16},{28,20},{1,9},{5... | collective-permute-start | bytes 76808 | tf_op jit(solution)/shard_map/ppermute | solution.py:74
  14.4 6.4 %copy-start.2 = (bf16[4,256,320]{1,2,0:T(8,128)(2,1)S(1)}, bf16[4,256,320]{1,2,0:T(8,128)(2,1)}, u32[]{:S(2)}) copy-start(bf16[4,256,320]{1,2,0:T(8,128)(2,1)} %param.24) | copy-start | bytes 1966084
  14.4 6.4 %copy-start.3 = (bf16[4,256,320]{1,2,0:T(8,128)(2,1)S(1)}, bf16[4,256,320]{1,2,0:T(8,128)(2,1)}, u32[]{:S(2)}) copy-start(bf16[4,256,320]{1,2,0:T(8,128)(2,1)} %param.25) | copy-start | bytes 1966084
  14.4 6.4 %copy-start.12 = (s32[4]{0:T(128)S(1)}, s32[4]{0:T(128)}, u32[]{:S(2)}) copy-start(s32[4]{0:T(128)} %lengths_ref.1) | copy-start | bytes 52
  14.4 11.6 %copy-start.5 = (bf16[100,400]{0,1:T(8,128)(2,1)S(1)}, bf16[100,400]{0,1:T(8,128)(2,1)}, u32[]{:S(2)}) copy-start(bf16[100,400]{0,1:T(8,128)(2,1)} %param.34) | copy-start | bytes 240004
  16.4 9.6 %copy-start = (bf16[400,1600]{1,0:T(8,128)(2,1)S(1)}, bf16[400,1600]{1,0:T(8,128)(2,1)}, u32[]{:S(2)}) copy-start(bf16[400,1600]{1,0:T(8,128)(2,1)} %refs_11_.1) | copy-start | bytes 3840004
  16.4 9.6 %copy-start.4 = (f32[4,16,400]{2,1,0:T(8,128)S(1)}, f32[4,16,400]{2,1,0:T(8,128)}, u32[]{:S(2)}) copy-start(f32[4,16,400]{2,1,0:T(8,128)} %refs_9_.1) | copy-start | bytes 307204
  16.4 9.7 %copy-start.6 = (f32[16,400]{1,0:T(8,128)S(1)}, f32[16,400]{1,0:T(8,128)}, u32[]{:S(2)}) copy-start(f32[16,400]{1,0:T(8,128)} %refs_8_.1) | copy-start | bytes 76804
  16.4 9.7 %copy-start.8 = (f32[400]{0:T(512)S(1)}, f32[400]{0:T(512)}, u32[]{:S(2)}) copy-start(f32[400]{0:T(512)} %param.35) | copy-start | bytes 4804
  16.4 9.7 %copy-start.9 = (f32[400]{0:T(512)S(1)}, f32[400]{0:T(512)}, u32[]{:S(2)}) copy-start(f32[400]{0:T(512)} %param.37) | copy-start | bytes 4804
  16.4 3.2 %collective-permute-start.4 = (f32[4,692]{1,0:T(4,128)S(1)}, f32[4,692]{1,0:T(4,128)S(1)}, u32[]{:S(2)}, u32[]{:S(2)}) collective-permute-start(f32[4,692]{1,0:T(4,128)S(1)} %get-tuple-element.29.refs_0_), channel_id=1, source_target_pairs={{0,1},{1,2},{2,3},{3,0},{4,5},{5,6},{6,7},{7,4},{8,9},{9,10},{10,1... | collective-permute-start | bytes 33224 | tf_op jit(solution)/shard_map/ppermute | solution.py:38
  16.5 3.8 %collective-permute-start.5 = (f32[4,692]{1,0:T(4,128)S(1)}, f32[4,692]{1,0:T(4,128)S(1)}, u32[]{:S(2)}, u32[]{:S(2)}) collective-permute-start(f32[4,692]{1,0:T(4,128)S(1)} %get-tuple-element.29.refs_0_), channel_id=1, source_target_pairs={{0,2},{1,3},{2,0},{3,1},{4,6},{5,7},{6,4},{7,5},{8,10},{9,11},{10,... | collective-permute-start | bytes 33224 | tf_op jit(solution)/shard_map/ppermute | solution.py:38
  18.1 2.8 %collective-permute-start.6 = (f32[4,692]{1,0:T(4,128)S(1)}, f32[4,692]{1,0:T(4,128)S(1)}, u32[]{:S(2)}, u32[]{:S(2)}) collective-permute-start(f32[4,692]{1,0:T(4,128)S(1)} %get-tuple-element.29.refs_0_), channel_id=1, source_target_pairs={{0,3},{1,0},{2,1},{3,2},{4,7},{5,4},{6,5},{7,6},{8,11},{9,8},{10,9... | collective-permute-start | bytes 33224 | tf_op jit(solution)/shard_map/ppermute | solution.py:38
  20.9 7.2 %copy-start.1 = (bf16[1600,400]{0,1:T(8,128)(2,1)S(1)}, bf16[1600,400]{0,1:T(8,128)(2,1)}, u32[]{:S(2)}) copy-start(bf16[1600,400]{0,1:T(8,128)(2,1)} %param.38) | copy-start | bytes 3840004
  23.6 3.5 %collective-permute-start.7 = (f32[4,1650]{1,0:T(4,128)S(1)}, f32[4,1650]{1,0:T(4,128)S(1)}, u32[]{:S(2)}, u32[]{:S(2)}) collective-permute-start(f32[4,1650]{1,0:T(4,128)S(1)} %get-tuple-element.30.refs_0_), channel_id=1, source_target_pairs={{0,1},{1,2},{2,3},{3,0},{4,5},{5,6},{6,7},{7,4},{8,9},{9,10},{10,1... | collective-permute-start | bytes 79208 | tf_op jit(solution)/shard_map/ppermute | solution.py:38
  24.2 3.8 %collective-permute-start.8 = (f32[4,1650]{1,0:T(4,128)S(1)}, f32[4,1650]{1,0:T(4,128)S(1)}, u32[]{:S(2)}, u32[]{:S(2)}) collective-permute-start(f32[4,1650]{1,0:T(4,128)S(1)} %get-tuple-element.30.refs_0_), channel_id=1, source_target_pairs={{0,2},{1,3},{2,0},{3,1},{4,6},{5,7},{6,4},{7,5},{8,10},{9,11},{10,... | collective-permute-start | bytes 79208 | tf_op jit(solution)/shard_map/ppermute | solution.py:38
  25.7 2.3 %collective-permute-start.9 = (f32[4,1650]{1,0:T(4,128)S(1)}, f32[4,1650]{1,0:T(4,128)S(1)}, u32[]{:S(2)}, u32[]{:S(2)}) collective-permute-start(f32[4,1650]{1,0:T(4,128)S(1)} %get-tuple-element.30.refs_0_), channel_id=1, source_target_pairs={{0,3},{1,0},{2,1},{3,2},{4,7},{5,4},{6,5},{7,6},{8,11},{9,8},{10,9... | collective-permute-start | bytes 79208 | tf_op jit(solution)/shard_map/ppermute | solution.py:38
  26.1 7.3 %copy-start.10 = (f32[400]{0:T(512)S(1)}, f32[400]{0:T(512)}, u32[]{:S(2)}) copy-start(f32[400]{0:T(512)} %param.40) | copy-start | bytes 4804
  26.1 7.3 %copy-start.11 = (f32[400]{0:T(512)S(1)}, f32[400]{0:T(512)}, u32[]{:S(2)}) copy-start(f32[400]{0:T(512)} %param.41) | copy-start | bytes 4804
  28.9 3.2 %collective-permute-start.10 = (bf16[4,1664]{1,0:T(4,128)(2,1)S(1)}, bf16[4,1664]{1,0:T(4,128)(2,1)S(1)}, u32[]{:S(2)}, u32[]{:S(2)}) collective-permute-start(bf16[4,1664]{1,0:T(4,128)(2,1)S(1)} %get-tuple-element.34.refs_0_), channel_id=1, source_target_pairs={{0,1},{1,2},{2,3},{3,0},{4,5},{5,6},{6,7},{7,4},{8,9},{9,10},{10,1... | collective-permute-start | bytes 39944 | tf_op jit(solution)/shard_map/ppermute | solution.py:38
  29.5 3.8 %collective-permute-start.11 = (bf16[4,1664]{1,0:T(4,128)(2,1)S(1)}, bf16[4,1664]{1,0:T(4,128)(2,1)S(1)}, u32[]{:S(2)}, u32[]{:S(2)}) collective-permute-start(bf16[4,1664]{1,0:T(4,128)(2,1)S(1)} %get-tuple-element.34.refs_0_), channel_id=1, source_target_pairs={{0,2},{1,3},{2,0},{3,1},{4,6},{5,7},{6,4},{7,5},{8,10},{9,11},{10,... | collective-permute-start | bytes 39944 | tf_op jit(solution)/shard_map/ppermute | solution.py:38
  30.5 2.9 %collective-permute-start.12 = (bf16[4,1664]{1,0:T(4,128)(2,1)S(1)}, bf16[4,1664]{1,0:T(4,128)(2,1)S(1)}, u32[]{:S(2)}, u32[]{:S(2)}) collective-permute-start(bf16[4,1664]{1,0:T(4,128)(2,1)S(1)} %get-tuple-element.34.refs_0_), channel_id=1, source_target_pairs={{0,3},{1,0},{2,1},{3,2},{4,7},{5,4},{6,5},{7,6},{8,11},{9,8},{10,9... | collective-permute-start | bytes 39944 | tf_op jit(solution)/shard_map/ppermute | solution.py:38

commit v4 on v3

--- a/solution.py
+++ b/solution.py
@@ -44,9 +44,8 @@
     *given, out_ref = refs
     at = 0
     for ref in given:
-        if ref.shape[1:] == out_ref.shape[1:]:
-            out_ref[at : at + ref.shape[0]] = ref[...]
-            at += ref.shape[0]
+        out_ref[at : at + ref.shape[0]] = ref[...]
+        at += ref.shape[0]
 
 
 def digits_of(size):
@@ -67,7 +66,7 @@
         if len(blocks) > 1:
             entries = sum(b.shape[0] for b in blocks)
             (held,) = call(
-                join, (), (*blocks, *beside), (jax.ShapeDtypeStruct((entries, *part.shape), part.dtype),)
+                join, (), blocks, (jax.ShapeDtypeStruct((entries, *part.shape), part.dtype),), after=beside
             )
             beside = ()
         blocks = [held] + [
@@ -78,11 +77,12 @@
 
 
 def entry_of(away, size):
-    entry = jnp.int32(0)
+    entry, done = jnp.int32(0), 0
     for place, count in digits_of(size):
         top = (1 << count) - 1
         digit = lax.bitwise_and(lax.shift_right_logical(away, place), top)
-        entry = entry + lax.shift_left(lax.bitwise_and(top + 1 - digit, top), place)
+        entry = entry + lax.shift_left(lax.bitwise_and(top + 1 - digit, top), done)
+        done += count
     return entry
 
 
@@ -158,8 +158,8 @@
 
 def project_in(me_ref, *refs, size):
     arrived_refs = refs[:size]
-    (chosen_ref, base_ref, old_conv_ref, gain_ref, heads_w_ref, xproj_ref, in_w_ref, gate_w_ref,
-     part_ref, act_ref, gate_ref, new_conv_ref, cols_ref, blocks) = refs[size:]
+    (chosen_ref, base_ref, old_conv_ref, gain_ref, heads_w_ref, xproj_ref, in_w_ref, part_ref,
+     act_ref, normed_ref, new_conv_ref, cols_ref, blocks) = refs[size:]
     rows, cols = cols_ref.shape
     arrived = jnp.concatenate(
         [ref[i].astype(F32) for ref in arrived_refs for i in range(ref.shape[0])], axis=0
@@ -170,9 +170,9 @@
     cols_ref[...] = blocks[me_ref[0]]
     scale = lax.rsqrt(jnp.mean(routed * routed, axis=1, keepdims=True) + EPSILON)
     normed = (routed * scale * gain_ref[...]).astype(BF16)
+    normed_ref[...] = normed
+    channel_in = dot_nt(normed, in_w_ref[...])[:rows]
     heads = dot_nt(normed, heads_w_ref[...])[:rows].astype(BF16).astype(F32)
-    channel_in = dot_nt(normed, in_w_ref[...])[:rows]
-    gate = dot_nt(normed, gate_w_ref[...])[:rows]
     taps = old_conv_ref.shape[0]
     conv_out = base_ref[:rows] + base_ref[rows:] * channel_in
     act = conv_out * sigmoid(conv_out)
@@ -180,9 +180,13 @@
         new_conv_ref[tap] = old_conv_ref[tap]
     new_conv_ref[taps - 1] = channel_in.astype(BF16)
     act_ref[...] = act
-    gate_ref[...] = gate * sigmoid(gate)
     state = dot_nt(act.astype(BF16), xproj_ref[...])
     part_ref[...] = jnp.concatenate([heads, state], axis=1)
+
+
+def project_gate(normed_ref, gate_w_ref, gate_ref):
+    gate = dot_nt(normed_ref[...], gate_w_ref[...])[: gate_ref.shape[0]]
+    gate_ref[...] = gate * sigmoid(gate)
 
 
 def state_step(me_ref, *refs, size, head_width):
@@ -224,9 +228,51 @@
     rows = held.shape[1]
     heads = jnp.concatenate([held[i][:, :head_width] for i in range(size)], axis=1)
     new_kv_ref[...] = heads[:, QUERY_WIDTH:].astype(BF16)
+    tall = jnp.concatenate([heads, jnp.zeros((8 - rows, heads.shape[1]), F32)], axis=0)
+    tall = jnp.concatenate([tall, jnp.zeros((8, -tall.shape[1] % 128), F32)], axis=1)
+    lane = lax.broadcasted_iota(jnp.int32, (8, 128), 1)
+    row = lax.broadcasted_iota(jnp.int32, (8, 128), 0)
+    first = lane < HEAD_SIZE
+
+    turned = {}
+
+    def twice(at):
+        tile = at // 128
+        if tile not in turned:
+            line = tall[:, tile * 128 : tile * 128 + 128]
+            turned[tile] = (line, pltpu.roll(line, HEAD_SIZE, 1))
+        line, other = turned[tile]
+        return jnp.where(first, line, other) if at % 128 == 0 else jnp.where(first, other, line)
+
+    blocks = -(-rows // 2)
+    own_block = [
+        jnp.where(row == jnp.where(first, 2 * i, 2 * i + 1), 1.0, 0.0) for i in range(blocks)
+    ]
+    half = jnp.where(first, HEAD_SIZE ** -0.5, 0.0)
+    groups = range(KEY_VALUE_HEADS)
+    queries = [[twice(j * HEAD_SIZE) for j in range(g * GROUP, (g + 1) * GROUP)] for g in groups]
+    scores = []
+    for g in groups:
+        spread = jnp.concatenate(
+            [
+                jnp.concatenate([q * (HEAD_SIZE ** -0.5) * mask for mask in own_block], axis=1)
+                for q in queries[g]
+            ],
+            axis=0,
+        ).astype(BF16)
+        keys = jnp.concatenate(
+            [keys_ref[r, g * HEAD_SIZE : (g + 1) * HEAD_SIZE, :] for r in range(rows)], axis=0
+        )
+        scores.append(jnp.dot(spread, keys, preferred_element_type=F32))
+    new_keys = [twice(QUERY_WIDTH + g * HEAD_SIZE) * half for g in groups]
+    own = [
+        jnp.sum(
+            jnp.concatenate([q * new_keys[g] for q in queries[g]], axis=0), axis=1, keepdims=True
+        )
+        for g in groups
+    ]
 
     span = keys_ref.shape[2]
-    tall = jnp.concatenate([heads, jnp.zeros((8 - rows, heads.shape[1]), F32)], axis=0)
     row_id = lax.broadcasted_iota(jnp.int32, (8, span), 0)
     slot = lax.broadcasted_iota(jnp.int32, (8, span), 1) + me * span
     length = jnp.zeros((8, span), jnp.int32)
@@ -237,56 +283,72 @@
         hole = jnp.where(
             row_id == r, jnp.where(count >= WINDOW_LENGTH, lax.rem(count, WINDOW_LENGTH), -1), hole
         )
-    live = (slot < length) & (slot != hole)
-    live = jnp.concatenate([live.astype(F32)] * GROUP, axis=0) > 0.0
-    tile_row = lax.rem(lax.broadcasted_iota(jnp.int32, (8 * GROUP, 1), 0), 8)
+    live = jnp.where((slot < length) & (slot != hole), 1.0, 0.0)
+    live = jnp.concatenate([live] * GROUP, axis=0) > 0.0
+    tops = [
+        jnp.maximum(
+            jnp.max(jnp.where(live, scores[g], -jnp.inf), axis=1, keepdims=True), own[g]
+        )
+        for g in groups
+    ]
+    weights = [
+        jnp.where(live, jnp.exp(scores[g] - tops[g]), 0.0).astype(BF16) for g in groups
+    ]
     own_here = jnp.where(me == 0, 1.0, 0.0)
-    numers, tops, totals = [], [], []
-    for g in range(KEY_VALUE_HEADS):
-        at = QUERY_WIDTH + g * HEAD_SIZE
-        new_key = tall[:, at : at + HEAD_SIZE]
-        new_value = tall[:, at + KEY_VALUE_WIDTH : at + KEY_VALUE_WIDTH + HEAD_SIZE]
-        queries = jnp.concatenate(
-            [
-                tall[:, j * HEAD_SIZE : (j + 1) * HEAD_SIZE]
-                for j in range(g * GROUP, (g + 1) * GROUP)
-            ],
-            axis=0,
-        ) * (HEAD_SIZE ** -0.5)
-        own = jnp.sum(queries * jnp.concatenate([new_key] * GROUP, axis=0), axis=1, keepdims=True)
-        packed = queries.astype(BF16)
-        score = jnp.zeros((8 * GROUP, span), F32)
-        for r in range(rows):
-            one = jnp.dot(
-                packed,
-                keys_ref[r, g * HEAD_SIZE : (g + 1) * HEAD_SIZE, :],
-                preferred_element_type=F32,
+    own_weights = [
+        jnp.exp(own[g] - tops[g]).astype(BF16).astype(F32) * own_here for g in groups
+    ]
+    products = []
+    for g in groups:
+        values = jnp.concatenate(
+            [values_ref[r, g * HEAD_SIZE : (g + 1) * HEAD_SIZE, :] for r in range(rows)], axis=0
+        )
+        products.append(dot_nt(weights[g], values))
+    totals = [
+        jnp.sum(weights[g].astype(F32), axis=1, keepdims=True) + own_weights[g] for g in groups
+    ]
+    stats = jnp.zeros((8, 128), F32)
+    numers = []
+    for g in groups:
+        new_value = twice(QUERY_WIDTH + KEY_VALUE_WIDTH + g * HEAD_SIZE)
+        for k in range(GROUP):
+            j = g * GROUP + k
+            at = slice(8 * k, 8 * k + 8)
+            folded = products[g][at, :128] * own_block[0]
+            for i in range(1, blocks):
+                folded = folded + products[g][at, 128 * i : 128 * i + 128] * own_block[i]
+            numers.append(
+                folded + pltpu.roll(folded, HEAD_SIZE, 1) + own_weights[g][at] * new_value
             )
-            score = jnp.where(tile_row == r, one, score)
-        top = jnp.maximum(
-            jnp.max(jnp.where(live, score, -jnp.inf), axis=1, keepdims=True), own
-        )
-        weight = jnp.where(live, jnp.exp(score - top), 0.0).astype(BF16)
-        own_weight = jnp.exp(own - top).astype(BF16).astype(F32) * own_here
-        total = jnp.sum(weight.astype(F32), axis=1, keepdims=True) + own_weight
-        numer = jnp.zeros((8 * GROUP, HEAD_SIZE), F32)
-        for r in range(rows):
-            one = dot_nt(weight, values_ref[r, g * HEAD_SIZE : (g + 1) * HEAD_SIZE, :])
-            numer = jnp.where(tile_row == r, one, numer)
-        numer = numer + own_weight * jnp.concatenate([new_value] * GROUP, axis=0)
-        for j in range(GROUP):
-            numers.append(numer[8 * j : 8 * j + 8])
-            tops.append(top[8 * j : 8 * j + 8])
-            totals.append(total[8 * j : 8 * j + 8])
-    part_ref[...] = jnp.concatenate(numers + tops + totals, axis=1)[:rows]
+            stats = jnp.where(lane == j, tops[g][at], stats)
+            stats = jnp.where(lane == QUERY_HEADS + j, totals[g][at], stats)
+    lines = [
+        jnp.where(first, numers[j], numers[j + 1]) for j in range(0, QUERY_HEADS - 1, 2)
+    ]
+    high = stats.astype(BF16).astype(F32)
+    middle = (stats - high).astype(BF16).astype(F32)
+    low = stats - high - middle
+    lines.append(jnp.where(first, numers[-1], pltpu.roll(high, HEAD_SIZE, 1)))
+    lines.append(jnp.where(first, middle, pltpu.roll(low, HEAD_SIZE, 1)))
+    part_ref[...] = jnp.concatenate(lines, axis=1)[:rows].astype(BF16)
 
 
 def project_out(*refs, size):
     pieces = refs[:size]
     (state_ref, spread_ref, w_ref, y_ref, part_ref) = refs[size:]
     rows = y_ref.shape[0]
-    tops = [p[:, QUERY_WIDTH : QUERY_WIDTH + QUERY_HEADS] for p in pieces]
-    totals = [p[:, QUERY_WIDTH + QUERY_HEADS :] for p in pieces]
+    stats = [
+        functools.reduce(
+            jnp.add,
+            [
+                p[:, QUERY_WIDTH + i * HEAD_SIZE : QUERY_WIDTH + (i + 1) * HEAD_SIZE].astype(F32)
+                for i in range(3)
+            ],
+        )
+        for p in pieces
+    ]
+    tops = [t[:, :QUERY_HEADS] for t in stats]
+    totals = [t[:, QUERY_HEADS : 2 * QUERY_HEADS] for t in stats]
     top = functools.reduce(jnp.maximum, tops)
     factors = [jnp.exp(t - top) for t in tops]
     total = functools.reduce(jnp.add, [f * t for f, t in zip(factors, totals)])
@@ -298,7 +360,7 @@
     )
     merged = functools.reduce(
         jnp.add,
-        [spread[i * rows : (i + 1) * rows] * p[:, :QUERY_WIDTH] for i, p in enumerate(pieces)],
+        [spread[i * rows : (i + 1) * rows] * p[:, :QUERY_WIDTH].astype(F32) for i, p in enumerate(pieces)],
     )
     y_attn = dot_nt(merged.astype(BF16), w_ref[...])
     y_ref[...] = y_attn
@@ -335,15 +397,20 @@
 VMEM = pl.BlockSpec(memory_space=pltpu.VMEM)
 
 
-def call(body, scalars, blocks, outs, scratch=()):
+def call(body, scalars, blocks, outs, scratch=(), after=()):
+    def run(*refs):
+        body(*refs[len(after) :])
+
     return pl.pallas_call(
-        body,
-        in_specs=[SMEM] * len(scalars) + [VMEM] * len(blocks),
+        run,
+        in_specs=[pl.BlockSpec(memory_space=pl.ANY)] * len(after)
+        + [SMEM] * len(scalars)
+        + [VMEM] * len(blocks),
         out_specs=[VMEM] * len(outs),
         out_shape=outs,
         scratch_shapes=scratch,
         compiler_params=pltpu.CompilerParams(vmem_limit_bytes=16 * 1024 * 1024),
-    )(*scalars, *blocks)
+    )(*after, *scalars, *blocks)
 
 
 def shards(
@@ -411,29 +478,32 @@
         compiler_params=pltpu.CompilerParams(vmem_limit_bytes=4 * 1024 * 1024),
     )(arrived[0], pinned[-1])
     part_width = head_width + w_xproj.shape[1]
-    part, act, gate, new_conv, routed_cols = call(
+    part, act, normed, new_conv, routed_cols = call(
         functools.partial(project_in, size=len(arrived)),
         (me,),
-        (*arrived, *prepared, gate_w),
+        (*arrived, *prepared),
         (
             shape((rows, part_width), F32),
             shape((rows, cols), F32),
-            shape((rows, cols), F32),
+            shape((8, MODEL_WIDTH), BF16),
             shape((conv_state.shape[1], rows, cols), BF16),
             shape((rows, cols), F32),
         ),
         (pltpu.VMEM((narrow, rows, cols), F32),),
+        after=(gate_w,),
     )
     pieces = exchange(part, "narrow")
+    (gate,) = call(project_gate, (), (normed, gate_w), (shape((rows, cols), F32),))
     second, new_kv = call(
         functools.partial(attend, size=narrow, head_width=head_width),
         (me, lengths),
         (*pieces, cached_key_rows.transpose(0, 2, 1), cached_value_rows.transpose(0, 2, 1)),
         (
-            shape((rows, QUERY_WIDTH + 2 * QUERY_HEADS), F32),
+            shape((rows, QUERY_WIDTH + 3 * HEAD_SIZE), BF16),
             shape((rows, 2 * KEY_VALUE_WIDTH), BF16),
         ),
         (pltpu.VMEM((narrow, rows, part_width), F32),),
+        after=(gate,),
     )
     state_part, new_ssm = call(
         functools.partial(state_step, size=narrow, head_width=head_width),

time: 34.4 us -> 33 us (0.959)
  Pallas kernels: 10.6 us -> 9.92 us
  waiting for transfers between devices: 6.74 us -> 6.07 us
    ppermute x9, waiting for transfers between devices: 3.95 us -> 3.28 us  [exchange(): lax.ppermute(part, axis, [(i, (i + step) % size) for i in range(size)])]
    pallas_call x6 -> x7, Pallas kernels: 7.17 us -> 6.52 us  [call(): pl.pallas_call(run, in_specs=[pl.BlockSpec(memory_space=pl.ANY)] * len(af...]
  transfers between devices with their start and end apart: 13 -> 13, of which waited for: 8 -> 7; matrix products, arithmetic and copies ran while one was open for 0% -> 0% of each run, Pallas kernels for 13% -> 15%
where the time goes in v4:
time: 33 us; the launch traced here: 32.8 us
  starting transfers between devices  15.9 us (48%)
  Pallas kernels  9.92 us (30%)
  waiting for transfers between devices  6.07 us (18%)
  between operations  0.82 us (2%)
    ppermute x9, starting transfers between devices, exchange(): lax.ppermute(part, axis, [(i, (i + step) % size) for i in range(size)])  8.33 us
    ppermute x4, starting transfers between devices, gather_xor(): lax.ppermute(held, axis, [(i, i ^ step << place) for i in range(size)])  7.55 us
    pallas_call x7, Pallas kernels, call(): pl.pallas_call(run, in_specs=[pl.BlockSpec(memory_space=pl.ANY)] * len(af...  6.52 us
    ppermute x9, waiting for transfers between devices, exchange(): lax.ppermute(part, axis, [(i, (i + step) % size) for i in range(size)])  3.28 us
    ppermute x4, waiting for transfers between devices, gather_xor(): lax.ppermute(held, axis, [(i, i ^ step << place) for i in range(size)])  2.79 us
    pallas_call x1, Pallas kernels, shards(): pl.pallas_call(prepare, in_specs=[SMEM] + [anywhere] * len(pinned), out_s...  2.08 us
    pallas_call x1, Pallas kernels, shards(): pl.pallas_call(bring, in_specs=[anywhere] * 2, out_specs=[VMEM], out_shap...  1.31 us
  transfers between devices with their start and end apart: 13, of which 7 were waited for; matrix products, arithmetic and copies ran while one was open for 0% of the time, Pallas kernels for 15%

profile of v4, /device:TPU:0, one launch (start us, length us, event | category | flops | bytes accessed | tf_op | source)
XLA Modules:
  0.0 32.8 jit_solution(3768206499156627133)
XLA Ops:
  0.6 3.0 %collective-permute-start = (bf16[1,4,1600]{2,1,0:T(4,128)(2,1)}, bf16[1,4,1600]{2,1,0:T(4,128)(2,1)S(1)}, u32[]{:S(2)}, u32[]{:S(2)}) collective-permute-start(bf16[1,4,1600]{2,1,0:T(4,128)(2,1)} %bitcast.21), channel_id=1, source_target_pairs={{0,4},{4,0},{8,12},{12,8},{16,20},{20,16},{24,28},{28,24},{1,5},{5... | collective-permute-start | bytes 38408 | tf_op jit(solution)/shard_map/ppermute | solution.py:73
  3.7 2.1 %shard_map.228 = (f32[8,32]{1,0:T(8,128)S(1)}, f32[8,400]{1,0:T(8,128)S(1)}, bf16[3,4,400]{2,1,0:T(4,128)(2,1)S(1)}, f32[1,1600]{1,0:T(1,128)S(1)}, bf16[560,160...) custom-call(s32[1]{0:T(128)} %bitcast.1.place_ref, s32[4]{0:T(128)} %source_ref.1, ...), custom_call_target="tpu_custom_call" | custom-call | tf_op jit(solution)/shard_map/pallas_call | solution.py:453
  5.8 3.9 %collective-permute-start.1 = (bf16[2,4,1600]{2,1,0:T(4,128)(2,1)S(1)}, bf16[2,4,1600]{2,1,0:T(4,128)(2,1)S(1)}, u32[]{:S(2)}, u32[]{:S(2)}) collective-permute-start(bf16[2,4,1600]{2,1,0:T(4,128)(2,1)S(1)} %shard_map.229.after_ref.refs_2_), channel_id=1, source_target_pairs={{0,24},{4,28},{8,16},{12,20},{16,8},{20,12},{24,0},{28,4},{1,25},{... | collective-permute-start | bytes 76808 | tf_op jit(solution)/shard_map/ppermute | solution.py:73
  9.7 0.6 %collective-permute-start.3 = (bf16[2,4,1600]{2,1,0:T(4,128)(2,1)S(1)}, bf16[2,4,1600]{2,1,0:T(4,128)(2,1)S(1)}, u32[]{:S(2)}, u32[]{:S(2)}) collective-permute-start(bf16[2,4,1600]{2,1,0:T(4,128)(2,1)S(1)} %shard_map.229.after_ref.refs_2_), channel_id=1, source_target_pairs={{0,8},{4,12},{8,0},{12,4},{16,24},{20,28},{24,16},{28,20},{1,9},{5... | collective-permute-start | bytes 76808 | tf_op jit(solution)/shard_map/ppermute | solution.py:73
  10.3 1.3 %shard_map.230.refs_0_.refs_1_ = bf16[400,1600]{1,0:T(8,128)(2,1)S(1)} custom-call(bf16[2,4,1600]{2,1,0:T(4,128)(2,1)S(1)} %shard_map.229.after_ref.refs_2_, bf16[2,400,1600]{2,1,0:T(8,128)(2,1)} %bitcast.28), custom_call_target="tpu_custom_call" | custom-call | tf_op jit(solution)/shard_map/pallas_call | solution.py:472
  11.6 0.1 collective-permute-done.1.refs_3_
  11.8 2.6 %collective-permute-done.2.refs_4_ = bf16[2,4,1600]{2,1,0:T(4,128)(2,1)S(1)} collective-permute-done((bf16[2,4,1600]{2,1,0:T(4,128)(2,1)S(1)}, bf16[2,4,1600]{2,1,0:T(4,128)(2,1)S(1)}, u32[]{:S(2)}, u32[]{:S(2)}) %collective-permute-start.2) | collective-permute-done | bytes 25632 | tf_op jit(solution)/shard_map/ppermute | solution.py:73
  14.4 1.6 %shard_map.231 = (f32[4,692]{1,0:T(4,128)S(1)}, f32[4,400]{1,0:T(4,128)S(1)}, bf16[8,1600]{1,0:T(8,128)(2,1)S(1)}, bf16[3,4,400]{2,1,0:T(4,128)(2,1)}, f32[4,400]{1,0:T(4,128)S(1)}) custom-call(bf16[400,1600]{1,0:T(8,128)(2,1)S(1)} %shard_map.230.refs_0_.refs_1_, s32[1]{0:T(128)} %bitcast.refs_1_.refs_0_, ...), custom_call_target="tpu_custom_call" | custom-call | tf_op jit(solution)/shard_map/pallas_call | solution.py:404
  16.1 1.6 %collective-permute-start.5 = (f32[4,692]{1,0:T(4,128)S(1)}, f32[4,692]{1,0:T(4,128)S(1)}, u32[]{:S(2)}, u32[]{:S(2)}) collective-permute-start(f32[4,692]{1,0:T(4,128)S(1)} %get-tuple-element.30.refs_3_.refs_1_), channel_id=1, source_target_pairs={{0,2},{1,3},{2,0},{3,1},{4,6},{5,7},{6,4},{7,5},{8,10},{9,11},{10,... | collective-permute-start | bytes 33224 | tf_op jit(solution)/shard_map/ppermute | solution.py:38
  17.6 1.4 %collective-permute-start.6 = (f32[4,692]{1,0:T(4,128)S(1)}, f32[4,692]{1,0:T(4,128)S(1)}, u32[]{:S(2)}, u32[]{:S(2)}) collective-permute-start(f32[4,692]{1,0:T(4,128)S(1)} %get-tuple-element.30.refs_3_.refs_1_), channel_id=1, source_target_pairs={{0,3},{1,0},{2,1},{3,2},{4,7},{5,4},{6,5},{7,6},{8,11},{9,8},{10,9... | collective-permute-start | bytes 33224 | tf_op jit(solution)/shard_map/ppermute | solution.py:38
  19.0 0.0 copy-start.4
  19.0 0.0 copy-start.5
  19.1 0.0 copy-start.8
  19.1 0.0 copy-start.9
  19.1 0.5 %shard_map.232.refs_0_.refs_6_ = f32[4,400]{1,0:T(4,128)S(1)} custom-call(bf16[8,1600]{1,0:T(8,128)(2,1)S(1)} %get-tuple-element.29.refs_0_, bf16[400,1600]{1,0:T(8,128)(2,1)S(1)} %shard_map.230.refs_0_.refs_1_), custom_call_target="tpu_custom_call" | custom-call | tf_op jit(solution)/shard_map/pallas_call | solution.py:404
  19.6 0.3 collective-permute-done.5.refs_5_.refs_3_
  19.8 0.6 %collective-permute-done.6.refs_6_.refs_4_ = f32[4,692]{1,0:T(4,128)S(1)} collective-permute-done((f32[4,692]{1,0:T(4,128)S(1)}, f32[4,692]{1,0:T(4,128)S(1)}, u32[]{:S(2)}, u32[]{:S(2)}) %collective-permute-start.6) | collective-permute-done | bytes 11104 | tf_op jit(solution)/shard_map/ppermute | solution.py:38
  20.4 1.9 %shard_map.233 = (bf16[4,1792]{1,0:T(4,128)(2,1)S(1)}, bf16[4,640]{1,0:T(4,128)(2,1)}) custom-call(f32[4,400]{1,0:T(4,128)S(1)} %shard_map.232.refs_0_.refs_6_, s32[1]{0:T(128)} %bitcast.refs_1_.refs_0_, s32[4]{0:T(128)S(1)} %copy-done.12, f32[4,692]{1,0:T(4,128)S(1)} %get-tuple-element.30.refs_3_.refs_1_, ...), custom_call_target="tpu_custom_call" | custom-call | tf_op jit(solution)/shard_map/pallas_call | solution.py:404
  22.3 0.6 %collective-permute-start.7 = (bf16[4,1792]{1,0:T(4,128)(2,1)S(1)}, bf16[4,1792]{1,0:T(4,128)(2,1)S(1)}, u32[]{:S(2)}, u32[]{:S(2)}) collective-permute-start(bf16[4,1792]{1,0:T(4,128)(2,1)S(1)} %get-tuple-element.31.refs_0_), channel_id=1, source_target_pairs={{0,1},{1,2},{2,3},{3,0},{4,5},{5,6},{6,7},{7,4},{8,9},{9,10},{10,1... | collective-permute-start | bytes 43016 | tf_op jit(solution)/shard_map/ppermute | solution.py:38
  22.9 1.5 %collective-permute-start.8 = (bf16[4,1792]{1,0:T(4,128)(2,1)S(1)}, bf16[4,1792]{1,0:T(4,128)(2,1)S(1)}, u32[]{:S(2)}, u32[]{:S(2)}) collective-permute-start(bf16[4,1792]{1,0:T(4,128)(2,1)S(1)} %get-tuple-element.31.refs_0_), channel_id=1, source_target_pairs={{0,2},{1,3},{2,0},{3,1},{4,6},{5,7},{6,4},{7,5},{8,10},{9,11},{10,... | collective-permute-start | bytes 43016 | tf_op jit(solution)/shard_map/ppermute | solution.py:38
  24.4 0.3 collective-permute-start.9
  24.8 0.0 copy-start.10
  24.8 0.0 copy-start.11
  24.8 0.9 %shard_map.234 = (bf16[4,1600]{1,0:T(4,128)(2,1)S(1)}, f32[4,16,400]{2,1,0:T(8,128)}) custom-call(s32[1]{0:T(128)} %bitcast.refs_1_.refs_0_, f32[4,692]{1,0:T(4,128)S(1)} %get-tuple-element.30.refs_3_.refs_1_, f32[4,692]{1,0:T(4,128)S(1)} %collective-permute-done.4.refs_4_.refs_2_, f32[4,692]{1,0:T(4,128)S(1)} %collective-permute-done.5.refs_5_.refs_3_, ...), custom_call_target="tpu_custom_call" | custom-call | tf_op jit(solution)/shard_map/pallas_call | solution.py:404
  25.8 0.9 %collective-permute-done.8.refs_2_ = bf16[4,1792]{1,0:T(4,128)(2,1)S(1)} collective-permute-done((bf16[4,1792]{1,0:T(4,128)(2,1)S(1)}, bf16[4,1792]{1,0:T(4,128)(2,1)S(1)}, u32[]{:S(2)}, u32[]{:S(2)}) %collective-permute-start.8) | collective-permute-done | bytes 14368 | tf_op jit(solution)/shard_map/ppermute | solution.py:38
  26.7 0.9 %shard_map.235 = (f32[4,400]{1,0:T(4,128)S(1)}, bf16[4,1664]{1,0:T(4,128)(2,1)S(1)}) custom-call(bf16[4,1792]{1,0:T(4,128)(2,1)S(1)} %get-tuple-element.31.refs_0_, bf16[4,1792]{1,0:T(4,128)(2,1)S(1)} %collective-permute-done.7.refs_1_, bf16[4,1792]{1,0:T(4,128)(2,1)S(1)} %collective-permute-done.8.refs_2_, ...), custom_call_target="tpu_custom_call" | custom-call | tf_op jit(solution)/shard_map/pallas_call | solution.py:404
  27.5 0.7 %collective-permute-start.10 = (bf16[4,1664]{1,0:T(4,128)(2,1)S(1)}, bf16[4,1664]{1,0:T(4,128)(2,1)S(1)}, u32[]{:S(2)}, u32[]{:S(2)}) collective-permute-start(bf16[4,1664]{1,0:T(4,128)(2,1)S(1)} %get-tuple-element.34.refs_1_), channel_id=1, source_target_pairs={{0,1},{1,2},{2,3},{3,0},{4,5},{5,6},{6,7},{7,4},{8,9},{9,10},{10,1... | collective-permute-start | bytes 39944 | tf_op jit(solution)/shard_map/ppermute | solution.py:38
  28.2 0.9 %collective-permute-start.11 = (bf16[4,1664]{1,0:T(4,128)(2,1)S(1)}, bf16[4,1664]{1,0:T(4,128)(2,1)S(1)}, u32[]{:S(2)}, u32[]{:S(2)}) collective-permute-start(bf16[4,1664]{1,0:T(4,128)(2,1)S(1)} %get-tuple-element.34.refs_1_), channel_id=1, source_target_pairs={{0,2},{1,3},{2,0},{3,1},{4,6},{5,7},{6,4},{7,5},{8,10},{9,11},{10,... | collective-permute-start | bytes 39944 | tf_op jit(solution)/shard_map/ppermute | solution.py:38
  29.1 1.4 %collective-permute-start.12 = (bf16[4,1664]{1,0:T(4,128)(2,1)S(1)}, bf16[4,1664]{1,0:T(4,128)(2,1)S(1)}, u32[]{:S(2)}, u32[]{:S(2)}) collective-permute-start(bf16[4,1664]{1,0:T(4,128)(2,1)S(1)} %get-tuple-element.34.refs_1_), channel_id=1, source_target_pairs={{0,3},{1,0},{2,1},{3,2},{4,7},{5,4},{6,5},{7,6},{8,11},{9,8},{10,9... | collective-permute-start | bytes 39944 | tf_op jit(solution)/shard_map/ppermute | solution.py:38
  30.5 0.2 collective-permute-done.10.refs_2_
  30.7 1.4 %collective-permute-done.11.refs_3_ = bf16[4,1664]{1,0:T(4,128)(2,1)S(1)} collective-permute-done((bf16[4,1664]{1,0:T(4,128)(2,1)S(1)}, bf16[4,1664]{1,0:T(4,128)(2,1)S(1)}, u32[]{:S(2)}, u32[]{:S(2)}) %collective-permute-start.11) | collective-permute-done | bytes 13344 | tf_op jit(solution)/shard_map/ppermute | solution.py:38
  32.0 0.8 %shard_map.236 = bf16[4,400]{1,0:T(4,128)(2,1)} custom-call(s32[1]{0:T(128)} %bitcast.refs_1_.refs_0_, bf16[4,1664]{1,0:T(4,128)(2,1)S(1)} %get-tuple-element.34.refs_1_, bf16[4,1664]{1,0:T(4,128)(2,1)S(1)} %collective-permute-done.10.refs_2_, bf16[4,1664]{1,0:T(4,128)(2,1)S(1)} %collective-permute-done.11.refs_3_, ...), custom_call_target="tpu_custom_call" | custom-call | tf_op jit(solution)/shard_map/pallas_call | solution.py:404
  (32 shorter events, 0.1 us)
Async XLA Ops:
  0.6 5.1 %collective-permute-start = (bf16[1,4,1600]{2,1,0:T(4,128)(2,1)}, bf16[1,4,1600]{2,1,0:T(4,128)(2,1)S(1)}, u32[]{:S(2)}, u32[]{:S(2)}) collective-permute-start(bf16[1,4,1600]{2,1,0:T(4,128)(2,1)} %bitcast.21), channel_id=1, source_target_pairs={{0,4},{4,0},{8,12},{12,8},{16,20},{20,16},{24,28},{28,24},{1,5},{5... | collective-permute-start | bytes 38408 | tf_op jit(solution)/shard_map/ppermute | solution.py:73
  3.7 2.1 %copy-start.7 = (bf16[4,1600]{1,0:T(4,128)(2,1)S(1)}, bf16[4,1600]{1,0:T(4,128)(2,1)}, u32[]{:S(2)}) copy-start(bf16[4,1600]{1,0:T(4,128)(2,1)} %param.21) | copy-start | bytes 38404
  5.8 6.0 %collective-permute-start.1 = (bf16[2,4,1600]{2,1,0:T(4,128)(2,1)S(1)}, bf16[2,4,1600]{2,1,0:T(4,128)(2,1)S(1)}, u32[]{:S(2)}, u32[]{:S(2)}) collective-permute-start(bf16[2,4,1600]{2,1,0:T(4,128)(2,1)S(1)} %shard_map.229.after_ref.refs_2_), channel_id=1, source_target_pairs={{0,24},{4,28},{8,16},{12,20},{16,8},{20,12},{24,0},{28,4},{1,25},{... | collective-permute-start | bytes 76808 | tf_op jit(solution)/shard_map/ppermute | solution.py:73
  9.7 4.7 %collective-permute-start.2 = (bf16[2,4,1600]{2,1,0:T(4,128)(2,1)S(1)}, bf16[2,4,1600]{2,1,0:T(4,128)(2,1)S(1)}, u32[]{:S(2)}, u32[]{:S(2)}) collective-permute-start(bf16[2,4,1600]{2,1,0:T(4,128)(2,1)S(1)} %shard_map.229.after_ref.refs_2_), channel_id=1, source_target_pairs={{0,16},{4,20},{8,24},{12,28},{16,0},{20,4},{24,8},{28,12},{1,17},{... | collective-permute-start | bytes 76808 | tf_op jit(solution)/shard_map/ppermute | solution.py:73
  9.7 4.7 %collective-permute-start.3 = (bf16[2,4,1600]{2,1,0:T(4,128)(2,1)S(1)}, bf16[2,4,1600]{2,1,0:T(4,128)(2,1)S(1)}, u32[]{:S(2)}, u32[]{:S(2)}) collective-permute-start(bf16[2,4,1600]{2,1,0:T(4,128)(2,1)S(1)} %shard_map.229.after_ref.refs_2_), channel_id=1, source_target_pairs={{0,8},{4,12},{8,0},{12,4},{16,24},{20,28},{24,16},{28,20},{1,9},{5... | collective-permute-start | bytes 76808 | tf_op jit(solution)/shard_map/ppermute | solution.py:73
  14.4 10.3 %copy-start.6 = (f32[16,400]{1,0:T(8,128)S(1)}, f32[16,400]{1,0:T(8,128)}, u32[]{:S(2)}) copy-start(f32[16,400]{1,0:T(8,128)} %refs_9_.1) | copy-start | bytes 76804
  16.1 4.4 %copy-start.2 = (bf16[4,256,320]{1,2,0:T(8,128)(2,1)S(1)}, bf16[4,256,320]{1,2,0:T(8,128)(2,1)}, u32[]{:S(2)}) copy-start(bf16[4,256,320]{1,2,0:T(8,128)(2,1)} %param.24) | copy-start | bytes 1966084
  16.1 4.4 %copy-start.3 = (bf16[4,256,320]{1,2,0:T(8,128)(2,1)S(1)}, bf16[4,256,320]{1,2,0:T(8,128)(2,1)}, u32[]{:S(2)}) copy-start(bf16[4,256,320]{1,2,0:T(8,128)(2,1)} %param.25) | copy-start | bytes 1966084
  16.1 4.4 %copy-start.12 = (s32[4]{0:T(128)S(1)}, s32[4]{0:T(128)}, u32[]{:S(2)}) copy-start(s32[4]{0:T(128)} %refs_2_.1) | copy-start | bytes 52
  16.1 3.5 %collective-permute-start.4 = (f32[4,692]{1,0:T(4,128)S(1)}, f32[4,692]{1,0:T(4,128)S(1)}, u32[]{:S(2)}, u32[]{:S(2)}) collective-permute-start(f32[4,692]{1,0:T(4,128)S(1)} %get-tuple-element.30.refs_3_.refs_1_), channel_id=1, source_target_pairs={{0,1},{1,2},{2,3},{3,0},{4,5},{5,6},{6,7},{7,4},{8,9},{9,10},{10,1... | collective-permute-start | bytes 33224 | tf_op jit(solution)/shard_map/ppermute | solution.py:38
  16.1 3.8 %collective-permute-start.5 = (f32[4,692]{1,0:T(4,128)S(1)}, f32[4,692]{1,0:T(4,128)S(1)}, u32[]{:S(2)}, u32[]{:S(2)}) collective-permute-start(f32[4,692]{1,0:T(4,128)S(1)} %get-tuple-element.30.refs_3_.refs_1_), channel_id=1, source_target_pairs={{0,2},{1,3},{2,0},{3,1},{4,6},{5,7},{6,4},{7,5},{8,10},{9,11},{10,... | collective-permute-start | bytes 33224 | tf_op jit(solution)/shard_map/ppermute | solution.py:38
  17.6 2.8 %collective-permute-start.6 = (f32[4,692]{1,0:T(4,128)S(1)}, f32[4,692]{1,0:T(4,128)S(1)}, u32[]{:S(2)}, u32[]{:S(2)}) collective-permute-start(f32[4,692]{1,0:T(4,128)S(1)} %get-tuple-element.30.refs_3_.refs_1_), channel_id=1, source_target_pairs={{0,3},{1,0},{2,1},{3,2},{4,7},{5,4},{6,5},{7,6},{8,11},{9,8},{10,9... | collective-permute-start | bytes 33224 | tf_op jit(solution)/shard_map/ppermute | solution.py:38
  19.0 5.7 %copy-start.1 = (bf16[400,1600]{1,0:T(8,128)(2,1)S(1)}, bf16[400,1600]{1,0:T(8,128)(2,1)}, u32[]{:S(2)}) copy-start(bf16[400,1600]{1,0:T(8,128)(2,1)} %refs_12_.1) | copy-start | bytes 3840004
  19.0 5.7 %copy-start.4 = (f32[4,16,400]{2,1,0:T(8,128)S(1)}, f32[4,16,400]{2,1,0:T(8,128)}, u32[]{:S(2)}) copy-start(f32[4,16,400]{2,1,0:T(8,128)} %refs_10_.1) | copy-start | bytes 307204
  19.0 5.7 %copy-start.5 = (bf16[100,400]{0,1:T(8,128)(2,1)S(1)}, bf16[100,400]{0,1:T(8,128)(2,1)}, u32[]{:S(2)}) copy-start(bf16[100,400]{0,1:T(8,128)(2,1)} %param.34) | copy-start | bytes 240004
  19.1 5.7 %copy-start.8 = (f32[400]{0:T(512)S(1)}, f32[400]{0:T(512)}, u32[]{:S(2)}) copy-start(f32[400]{0:T(512)} %param.35) | copy-start | bytes 4804
  19.1 5.7 %copy-start.9 = (f32[400]{0:T(512)S(1)}, f32[400]{0:T(512)}, u32[]{:S(2)}) copy-start(f32[400]{0:T(512)} %param.37) | copy-start | bytes 4804
  20.4 6.2 %copy-start = (bf16[1600,400]{0,1:T(8,128)(2,1)S(1)}, bf16[1600,400]{0,1:T(8,128)(2,1)}, u32[]{:S(2)}) copy-start(bf16[1600,400]{0,1:T(8,128)(2,1)} %param.38) | copy-start | bytes 3840004
  22.3 3.4 %collective-permute-start.7 = (bf16[4,1792]{1,0:T(4,128)(2,1)S(1)}, bf16[4,1792]{1,0:T(4,128)(2,1)S(1)}, u32[]{:S(2)}, u32[]{:S(2)}) collective-permute-start(bf16[4,1792]{1,0:T(4,128)(2,1)S(1)} %get-tuple-element.31.refs_0_), channel_id=1, source_target_pairs={{0,1},{1,2},{2,3},{3,0},{4,5},{5,6},{6,7},{7,4},{8,9},{9,10},{10,1... | collective-permute-start | bytes 43016 | tf_op jit(solution)/shard_map/ppermute | solution.py:38
  22.9 3.7 %collective-permute-start.8 = (bf16[4,1792]{1,0:T(4,128)(2,1)S(1)}, bf16[4,1792]{1,0:T(4,128)(2,1)S(1)}, u32[]{:S(2)}, u32[]{:S(2)}) collective-permute-start(bf16[4,1792]{1,0:T(4,128)(2,1)S(1)} %get-tuple-element.31.refs_0_), channel_id=1, source_target_pairs={{0,2},{1,3},{2,0},{3,1},{4,6},{5,7},{6,4},{7,5},{8,10},{9,11},{10,... | collective-permute-start | bytes 43016 | tf_op jit(solution)/shard_map/ppermute | solution.py:38
  24.4 2.2 %collective-permute-start.9 = (bf16[4,1792]{1,0:T(4,128)(2,1)S(1)}, bf16[4,1792]{1,0:T(4,128)(2,1)S(1)}, u32[]{:S(2)}, u32[]{:S(2)}) collective-permute-start(bf16[4,1792]{1,0:T(4,128)(2,1)S(1)} %get-tuple-element.31.refs_0_), channel_id=1, source_target_pairs={{0,3},{1,0},{2,1},{3,2},{4,7},{5,4},{6,5},{7,6},{8,11},{9,8},{10,9... | collective-permute-start | bytes 43016 | tf_op jit(solution)/shard_map/ppermute | solution.py:38
  24.8 7.2 %copy-start.10 = (f32[400]{0:T(512)S(1)}, f32[400]{0:T(512)}, u32[]{:S(2)}) copy-start(f32[400]{0:T(512)} %param.40) | copy-start | bytes 4804
  24.8 7.2 %copy-start.11 = (f32[400]{0:T(512)S(1)}, f32[400]{0:T(512)}, u32[]{:S(2)}) copy-start(f32[400]{0:T(512)} %param.41) | copy-start | bytes 4804
  27.5 3.2 %collective-permute-start.10 = (bf16[4,1664]{1,0:T(4,128)(2,1)S(1)}, bf16[4,1664]{1,0:T(4,128)(2,1)S(1)}, u32[]{:S(2)}, u32[]{:S(2)}) collective-permute-start(bf16[4,1664]{1,0:T(4,128)(2,1)S(1)} %get-tuple-element.34.refs_1_), channel_id=1, source_target_pairs={{0,1},{1,2},{2,3},{3,0},{4,5},{5,6},{6,7},{7,4},{8,9},{9,10},{10,1... | collective-permute-start | bytes 39944 | tf_op jit(solution)/shard_map/ppermute | solution.py:38
  28.2 3.8 %collective-permute-start.11 = (bf16[4,1664]{1,0:T(4,128)(2,1)S(1)}, bf16[4,1664]{1,0:T(4,128)(2,1)S(1)}, u32[]{:S(2)}, u32[]{:S(2)}) collective-permute-start(bf16[4,1664]{1,0:T(4,128)(2,1)S(1)} %get-tuple-element.34.refs_1_), channel_id=1, source_target_pairs={{0,2},{1,3},{2,0},{3,1},{4,6},{5,7},{6,4},{7,5},{8,10},{9,11},{10,... | collective-permute-start | bytes 39944 | tf_op jit(solution)/shard_map/ppermute | solution.py:38
  29.1 2.9 %collective-permute-start.12 = (bf16[4,1664]{1,0:T(4,128)(2,1)S(1)}, bf16[4,1664]{1,0:T(4,128)(2,1)S(1)}, u32[]{:S(2)}, u32[]{:S(2)}) collective-permute-start(bf16[4,1664]{1,0:T(4,128)(2,1)S(1)} %get-tuple-element.34.refs_1_), channel_id=1, source_target_pairs={{0,3},{1,0},{2,1},{3,2},{4,7},{5,4},{6,5},{7,6},{8,11},{9,8},{10,9... | collective-permute-start | bytes 39944 | tf_op jit(solution)/shard_map/ppermute | solution.py:38

commit v5 on v4

--- a/solution.py
+++ b/solution.py
@@ -58,10 +58,11 @@
     return rounds
 
 
-def gather_xor(part, axis, beside):
-    size = lax.axis_size(axis)
+def gather_xor(part, axis, core_axis, beside):
+    size, cores = lax.axis_size(axis), lax.axis_size(core_axis)
     blocks = [part[None]]
-    for place, count in digits_of(size):
+    rounds = digits_of(size)
+    for place, count in rounds:
         held = blocks[0]
         if len(blocks) > 1:
             entries = sum(b.shape[0] for b in blocks)
@@ -69,19 +70,49 @@
                 join, (), blocks, (jax.ShapeDtypeStruct((entries, *part.shape), part.dtype),), after=beside
             )
             beside = ()
-        blocks = [held] + [
-            lax.ppermute(held, axis, [(i, i ^ (step << place)) for i in range(size)])
-            for step in range((1 << count) - 1, 0, -1)
-        ]
+        if count == 2 and place == rounds[-1][0]:
+
+            def fetch(even, odd):
+                moves = [
+                    (i * cores + c, (i ^ (step << place)) * cores + c)
+                    for i in range(size)
+                    for c in range(cores)
+                    for step in [odd if c % 2 else even]
+                    if step
+                ]
+                return lax.ppermute(held, (axis, core_axis), moves)
+
+            far, near = fetch(3, 2), fetch(0, 1)
+            near_swap = lax.ppermute(near, core_axis, [(c, c - 1) for c in range(1, cores, 2)])
+            far_swap = lax.ppermute(far, core_axis, [(c, c ^ 1) for c in range(cores)])
+            blocks = [held, near, near_swap, far, far_swap]
+        else:
+            blocks = [held] + [
+                lax.ppermute(held, axis, [(i, i ^ (step << place)) for i in range(size)])
+                for step in range((1 << count) - 1, 0, -1)
+            ]
     return blocks
 
 
-def entry_of(away, size):
+def entries_of(size):
+    rounds = digits_of(size)
+    return (5 * size) // 4 if rounds[-1][1] == 2 else size
+
+
+def entry_of(away, size, core):
     entry, done = jnp.int32(0), 0
-    for place, count in digits_of(size):
+    rounds = digits_of(size)
+    for place, count in rounds:
         top = (1 << count) - 1
         digit = lax.bitwise_and(lax.shift_right_logical(away, place), top)
-        entry = entry + lax.shift_left(lax.bitwise_and(top + 1 - digit, top), done)
+        if count == 2 and place == rounds[-1][0]:
+            odd = lax.bitwise_and(core, 1)
+            near = 2 - odd
+            far = jnp.where(digit == 3 - odd, 3, 4)
+            block = jnp.where(digit == 0, 0, jnp.where(digit == 1, near, far))
+        else:
+            block = lax.bitwise_and(top + 1 - digit, top)
+        entry = entry + block * (1 << done)
         done += count
     return entry
 
@@ -108,14 +139,28 @@
     return [pltpu.make_async_copy(origin, to, sems.at[i]) for i, (origin, to) in enumerate(copies)]
 
 
+def live_slots(lengths, span, me):
+    row_id = lax.broadcasted_iota(jnp.int32, (8, span), 0)
+    slot = lax.broadcasted_iota(jnp.int32, (8, span), 1) + me * span
+    length = jnp.zeros((8, span), jnp.int32)
+    hole = jnp.zeros((8, span), jnp.int32)
+    for r in range(lengths.shape[0]):
+        count = lengths[r]
+        length = jnp.where(row_id == r, count, length)
+        hole = jnp.where(
+            row_id == r, jnp.where(count >= WINDOW_LENGTH, lax.rem(count, WINDOW_LENGTH), -1), hole
+        )
+    return jnp.where((slot < length) & (slot != hole), 1.0, 0.0)
+
+
 def prepare(
-    place_ref, source_ref, gain_ref, conv_w_ref, conv_b_ref, conv_rows_ref, heads_ref, xproj_ref, xz_ref,
-    chosen_ref, base_ref, new_conv_ref, gain_out, heads_out, xproj_out, in_out,
-    source, gain, conv_w, conv_b, conv_rows, sems,
+    source_ref, lengths_ref, gain_ref, conv_w_ref, conv_b_ref, conv_rows_ref, heads_ref, xproj_ref, xz_ref,
+    chosen_ref, live_ref, base_ref, new_conv_ref, gain_out, heads_out, xproj_out, in_out,
+    source, lengths, gain, conv_w, conv_b, conv_rows, sems, *, size,
 ):
     rows = source.shape[0]
     small = (
-        (source_ref, source), (gain_ref, gain), (conv_w_ref, conv_w), (conv_b_ref, conv_b),
+        (source_ref, source), (lengths_ref, lengths), (gain_ref, gain), (conv_w_ref, conv_w), (conv_b_ref, conv_b),
         (conv_rows_ref, conv_rows),
     )
     copies = copies_of(
@@ -125,15 +170,17 @@
         copy.start()
     for copy in copies[: len(small)]:
         copy.wait()
+    me = lax.axis_index("narrow")
     slots = chosen_ref.shape[1]
     row_id = lax.broadcasted_iota(jnp.int32, (8, slots), 0)
     wanted = jnp.full((8, slots), -1, jnp.int32)
     for r in range(rows):
-        away = lax.bitwise_xor(lax.div(source[r], rows), place_ref[0])
-        entry = entry_of(away, slots // rows)
+        away = lax.bitwise_xor(lax.div(source[r], rows), lax.axis_index("wide"))
+        entry = entry_of(away, size, me)
         wanted = jnp.where(row_id == r, entry * rows + lax.rem(source[r], rows), wanted)
     chosen = lax.broadcasted_iota(jnp.int32, (8, slots), 1) == wanted
     chosen_ref[...] = jnp.where(chosen, 1.0, 0.0)
+    live_ref[...] = live_slots(lengths, live_ref.shape[1], me)
     gain_out[...] = gain[...][None]
     taps = conv_rows.shape[0]
     base = conv_b[...]
@@ -148,18 +195,10 @@
         copy.wait()
 
 
-def bring(after_ref, xz_ref, gate_out, sems):
-    copies = copies_of(((xz_ref.at[1], gate_out),), sems)
-    for copy in copies:
-        copy.start()
-    for copy in copies:
-        copy.wait()
-
-
-def project_in(me_ref, *refs, size):
+def project_in(*refs, size):
     arrived_refs = refs[:size]
-    (chosen_ref, base_ref, old_conv_ref, gain_ref, heads_w_ref, xproj_ref, in_w_ref, part_ref,
-     act_ref, normed_ref, new_conv_ref, cols_ref, blocks) = refs[size:]
+    (chosen_ref, base_ref, gain_ref, heads_w_ref, xproj_ref, in_w_ref, part_ref, act_ref,
+     normed_ref, channel_ref, cols_ref, blocks) = refs[size:]
     rows, cols = cols_ref.shape
     arrived = jnp.concatenate(
         [ref[i].astype(F32) for ref in arrived_refs for i in range(ref.shape[0])], axis=0
@@ -167,32 +206,34 @@
     routed = jnp.dot(chosen_ref[...].astype(BF16), arrived, preferred_element_type=F32)
     for block in range(blocks.shape[0]):
         blocks[block] = routed[:rows, block * cols : (block + 1) * cols]
-    cols_ref[...] = blocks[me_ref[0]]
+    cols_ref[...] = blocks[lax.axis_index("narrow")]
     scale = lax.rsqrt(jnp.mean(routed * routed, axis=1, keepdims=True) + EPSILON)
     normed = (routed * scale * gain_ref[...]).astype(BF16)
     normed_ref[...] = normed
     channel_in = dot_nt(normed, in_w_ref[...])[:rows]
     heads = dot_nt(normed, heads_w_ref[...])[:rows].astype(BF16).astype(F32)
-    taps = old_conv_ref.shape[0]
+    channel_ref[...] = channel_in
     conv_out = base_ref[:rows] + base_ref[rows:] * channel_in
     act = conv_out * sigmoid(conv_out)
-    for tap in range(taps - 1):
-        new_conv_ref[tap] = old_conv_ref[tap]
-    new_conv_ref[taps - 1] = channel_in.astype(BF16)
     act_ref[...] = act
     state = dot_nt(act.astype(BF16), xproj_ref[...])
     part_ref[...] = jnp.concatenate([heads, state], axis=1)
 
 
-def project_gate(normed_ref, gate_w_ref, gate_ref):
-    gate = dot_nt(normed_ref[...], gate_w_ref[...])[: gate_ref.shape[0]]
+def project_gate(normed_ref, gate_w_ref, channel_ref, old_conv_ref, gate_ref, new_conv_ref):
+    taps = new_conv_ref.shape[0]
+    for tap in range(taps - 1):
+        new_conv_ref[tap] = old_conv_ref[tap]
+    new_conv_ref[taps - 1] = channel_ref[...].astype(BF16)
+    gate = dot_nt(normed_ref[...], gate_w_ref[1])[: gate_ref.shape[0]]
     gate_ref[...] = gate * sigmoid(gate)
 
 
-def state_step(me_ref, *refs, size, head_width):
+def state_step(kv_ref, *refs, size, head_width):
     pieces = refs[:size]
     (act_ref, gate_ref, dt_w_ref, dt_b_ref, a_log_ref, ssm_ref, skip_ref, out_w_ref, part_ref,
-     new_ssm_ref) = refs[size:]
+     new_ssm_ref, new_kv_ref) = refs[size:]
+    new_kv_ref[...] = kv_ref[...].astype(BF16)
     state = pieces[0][:, head_width:]
     for piece in pieces[1:]:
         state = state + piece[:, head_width:]
@@ -220,14 +261,14 @@
     part_ref[...] = jnp.dot(ssm_heads, out_w_ref[...], preferred_element_type=F32).astype(BF16)
 
 
-def attend(me_ref, lengths_ref, *refs, size, head_width):
+def attend(*refs, size, head_width):
     pieces = refs[:size]
-    (keys_ref, values_ref, part_ref, new_kv_ref, held) = refs[size:]
-    me = me_ref[0]
+    (live_ref, keys_ref, values_ref, part_ref, new_kv_ref, held) = refs[size:]
+    me = lax.axis_index("narrow")
     stack_pieces(me, pieces, held)
     rows = held.shape[1]
     heads = jnp.concatenate([held[i][:, :head_width] for i in range(size)], axis=1)
-    new_kv_ref[...] = heads[:, QUERY_WIDTH:].astype(BF16)
+    new_kv_ref[...] = heads[:, QUERY_WIDTH:]
     tall = jnp.concatenate([heads, jnp.zeros((8 - rows, heads.shape[1]), F32)], axis=0)
     tall = jnp.concatenate([tall, jnp.zeros((8, -tall.shape[1] % 128), F32)], axis=1)
     lane = lax.broadcasted_iota(jnp.int32, (8, 128), 1)
@@ -272,19 +313,7 @@
         for g in groups
     ]
 
-    span = keys_ref.shape[2]
-    row_id = lax.broadcasted_iota(jnp.int32, (8, span), 0)
-    slot = lax.broadcasted_iota(jnp.int32, (8, span), 1) + me * span
-    length = jnp.zeros((8, span), jnp.int32)
-    hole = jnp.zeros((8, span), jnp.int32)
-    for r in range(rows):
-        count = lengths_ref[r]
-        length = jnp.where(row_id == r, count, length)
-        hole = jnp.where(
-            row_id == r, jnp.where(count >= WINDOW_LENGTH, lax.rem(count, WINDOW_LENGTH), -1), hole
-        )
-    live = jnp.where((slot < length) & (slot != hole), 1.0, 0.0)
-    live = jnp.concatenate([live] * GROUP, axis=0) > 0.0
+    live = jnp.concatenate([live_ref[...]] * GROUP, axis=0) > 0.0
     tops = [
         jnp.maximum(
             jnp.max(jnp.where(live, scores[g], -jnp.inf), axis=1, keepdims=True), own[g]
@@ -375,7 +404,7 @@
     )
 
 
-def finish(me_ref, *refs, size):
+def finish(*refs, size):
     pieces = refs[:size]
     y_ref, cols_ref, gain_attn_ref, gain_ssm_ref, out_ref, blocks = refs[size:]
     cols = out_ref.shape[1]
@@ -388,7 +417,7 @@
         blocks[block] = y_ssm[:, block * cols : (block + 1) * cols]
     mixed = 0.5 * (
         y_ref[...] * attn_scale * gain_attn_ref[...]
-        + blocks[me_ref[0]] * state_scale * gain_ssm_ref[...]
+        + blocks[lax.axis_index("narrow")] * state_scale * gain_ssm_ref[...]
     )
     out_ref[...] = (cols_ref[...] + mixed).astype(BF16)
 
@@ -438,82 +467,84 @@
 ):
     rows = tokens.shape[0]
     narrow = lax.axis_size("narrow")
-    me = lax.axis_index("narrow").astype(jnp.int32).reshape(1)
     cols = MODEL_WIDTH // narrow
     head_width = query_key_value_weight.shape[1]
     shape = jax.ShapeDtypeStruct
 
-    place = lax.axis_index("wide").astype(jnp.int32).reshape(1)
+    wide = lax.axis_size("wide")
     large = (query_key_value_weight.T, w_xproj.T, w_xz.transpose(1, 2, 0))
-    small = (source, norm_gain, conv_weight, conv_bias[None], conv_state.transpose(1, 0, 2))
-    slots = rows * lax.axis_size("wide")
+    small = (source, lengths, norm_gain, conv_weight, conv_bias[None], conv_state.transpose(1, 0, 2))
+    slots = rows * entries_of(wide)
     half = large[2].shape[1:]
     pinned = [pltpu.with_memory_space_constraint(a, pltpu.HBM) for a in small + large]
     anywhere = pl.BlockSpec(memory_space=pl.ANY)
     prepared = pl.pallas_call(
-        prepare,
-        in_specs=[SMEM] + [anywhere] * len(pinned),
-        out_specs=[VMEM] * 7,
+        functools.partial(prepare, size=wide),
+        in_specs=[anywhere] * len(pinned),
+        out_specs=[VMEM] * 8,
         out_shape=[
             pltpu.VMEM((8, slots), F32),
+            pltpu.VMEM((8, cached_key_rows.shape[1]), F32),
             pltpu.VMEM((2 * rows, cols), F32),
-            pltpu.VMEM(small[4].shape, BF16),
+            pltpu.VMEM(small[5].shape, BF16),
             pltpu.VMEM((1, MODEL_WIDTH), F32),
             pltpu.VMEM(large[0].shape, BF16),
             pltpu.VMEM(large[1].shape, BF16),
             pltpu.VMEM(half, BF16),
         ],
-        scratch_shapes=[pltpu.SMEM(source.shape, jnp.int32)]
-        + [pltpu.VMEM(a.shape, a.dtype) for a in small[1:]]
-        + [pltpu.SemaphoreType.DMA((6 + 2 * (PARTS + 1),))],
+        scratch_shapes=[pltpu.SMEM(a.shape, jnp.int32) for a in small[:2]]
+        + [pltpu.VMEM(a.shape, a.dtype) for a in small[2:]]
+        + [pltpu.SemaphoreType.DMA((7 + 2 * (PARTS + 1),))],
         compiler_params=pltpu.CompilerParams(vmem_limit_bytes=4 * 1024 * 1024),
-    )(place, *pinned)
-    arrived = gather_xor(tokens, "wide", prepared[:1])
-    (gate_w,) = pl.pallas_call(
-        bring,
-        in_specs=[anywhere] * 2,
-        out_specs=[VMEM],
-        out_shape=[pltpu.VMEM(half, BF16)],
-        scratch_shapes=[pltpu.SemaphoreType.DMA((PARTS + 1,))],
-        compiler_params=pltpu.CompilerParams(vmem_limit_bytes=4 * 1024 * 1024),
-    )(arrived[0], pinned[-1])
+    )(*pinned)
+    arrived = gather_xor(tokens, "wide", "narrow", prepared[:1])
     part_width = head_width + w_xproj.shape[1]
-    part, act, normed, new_conv, routed_cols = call(
+    chosen, live, base, old_conv, *weights = prepared
+    part, act, normed, channel_in, routed_cols = call(
         functools.partial(project_in, size=len(arrived)),
-        (me,),
-        (*arrived, *prepared),
+        (),
+        (*arrived, chosen, base, *weights),
         (
             shape((rows, part_width), F32),
             shape((rows, cols), F32),
             shape((8, MODEL_WIDTH), BF16),
-            shape((conv_state.shape[1], rows, cols), BF16),
+            shape((rows, cols), F32),
             shape((rows, cols), F32),
         ),
         (pltpu.VMEM((narrow, rows, cols), F32),),
-        after=(gate_w,),
     )
     pieces = exchange(part, "narrow")
-    (gate,) = call(project_gate, (), (normed, gate_w), (shape((rows, cols), F32),))
-    second, new_kv = call(
+    gate, new_conv = call(
+        project_gate,
+        (),
+        (normed, w_xz.transpose(1, 2, 0), channel_in, old_conv),
+        (shape((rows, cols), F32), shape(old_conv.shape, BF16)),
+    )
+    second, key_value = call(
         functools.partial(attend, size=narrow, head_width=head_width),
-        (me, lengths),
-        (*pieces, cached_key_rows.transpose(0, 2, 1), cached_value_rows.transpose(0, 2, 1)),
+        (),
+        (*pieces, live, cached_key_rows.transpose(0, 2, 1), cached_value_rows.transpose(0, 2, 1)),
         (
             shape((rows, QUERY_WIDTH + 3 * HEAD_SIZE), BF16),
-            shape((rows, 2 * KEY_VALUE_WIDTH), BF16),
+            shape((rows, 2 * KEY_VALUE_WIDTH), F32),
         ),
         (pltpu.VMEM((narrow, rows, part_width), F32),),
         after=(gate,),
     )
-    state_part, new_ssm = call(
+    state_part, new_ssm, new_kv = call(
         functools.partial(state_step, size=narrow, head_width=head_width),
-        (me,),
+        (),
         (
-            *pieces, act, gate, w_dt.T, dt_bias[None], a_log, ssm_state, skip_d[None], w_ssm_out,
+            key_value, *pieces, act, gate, w_dt.T, dt_bias[None], a_log, ssm_state, skip_d[None], w_ssm_out,
         ),
-        (shape((rows, MODEL_WIDTH), BF16), shape(ssm_state.shape, F32)),
+        (
+            shape((rows, MODEL_WIDTH), BF16),
+            shape(ssm_state.shape, F32),
+            shape(key_value.shape, BF16),
+        ),
     )
     pieces = exchange(second, "narrow")
+    pieces = [pieces[0]] + [pieces[k] for k in (2, 3, 1)]
     spread = (
         lax.broadcasted_iota(jnp.int32, (QUERY_HEADS, QUERY_WIDTH), 1) // HEAD_SIZE
         == lax.broadcasted_iota(jnp.int32, (QUERY_HEADS, QUERY_WIDTH), 0)
@@ -527,7 +558,7 @@
     pieces = exchange(third, "narrow")
     (out,) = call(
         functools.partial(finish, size=narrow),
-        (me,),
+        (),
         (*pieces, y_attn, routed_cols, gain_attn[None], gain_ssm[None]),
         (shape((rows, cols), BF16),),
         (pltpu.VMEM((narrow, rows, cols), F32),),

time: 33 us -> 31.3 us (0.948)
  starting transfers between devices: 15.9 us -> 18.2 us
  Pallas kernels: 9.92 us -> 7.65 us
  waiting for transfers between devices: 6.07 us -> 4.32 us
    ppermute x0 -> x4, starting transfers between devices: none -> 6.27 us  [the longest x2 4.71 us: fetch(): return lax.ppermute(held, (axis, core_axis), moves)]
    ppermute x4 -> x1, starting transfers between devices: 7.55 us -> 3.03 us  [gather_xor(): lax.ppermute(held, axis, [(i, i ^ step << place) for i in range(size)])]
    ppermute x4 -> x1, waiting for transfers between devices: 2.79 us -> 0.01 us  [gather_xor(): lax.ppermute(held, axis, [(i, i ^ step << place) for i in range(size)])]
    ppermute x0 -> x4, waiting for transfers between devices: none -> 1.83 us  [the longest x2 0.92 us: fetch(): return lax.ppermute(held, (axis, core_axis), moves)]
    pallas_call x2 -> x1, Pallas kernels: 3.39 us -> 2.09 us  [shards(): pl.pallas_call(functools.partial(prepare, size=wide), in_specs=[anywhere]...]
    pallas_call x7, Pallas kernels: 6.52 us -> 5.55 us  [call(): pl.pallas_call(run, in_specs=[pl.BlockSpec(memory_space=pl.ANY)] * len(af...]
    ppermute x9, waiting for transfers between devices: 3.28 us -> 2.49 us  [exchange(): lax.ppermute(part, axis, [(i, (i + step) % size) for i in range(size)])]
    ppermute x9, starting transfers between devices: 8.33 us -> 8.9 us  [exchange(): lax.ppermute(part, axis, [(i, (i + step) % size) for i in range(size)])]
  transfers between devices with their start and end apart: 13 -> 14, of which waited for: 7 -> 6; matrix products, arithmetic and copies ran while one was open for 0% -> 0% of each run, Pallas kernels for 15% -> 13%
where the time goes in v5:
time: 31.3 us; the launch traced here: 31.1 us
  starting transfers between devices  18.2 us (58%)
  Pallas kernels  7.65 us (24%)
  waiting for transfers between devices  4.32 us (14%)
  between operations  0.82 us (3%)
    ppermute x9, starting transfers between devices, exchange(): lax.ppermute(part, axis, [(i, (i + step) % size) for i in range(size)])  8.9 us
    pallas_call x7, Pallas kernels, call(): pl.pallas_call(run, in_specs=[pl.BlockSpec(memory_space=pl.ANY)] * len(af...  5.55 us
    ppermute x2, starting transfers between devices, fetch(): return lax.ppermute(held, (axis, core_axis), moves)  4.71 us
    ppermute x1, starting transfers between devices, gather_xor(): lax.ppermute(held, axis, [(i, i ^ step << place) for i in range(size)])  3.03 us
    ppermute x9, waiting for transfers between devices, exchange(): lax.ppermute(part, axis, [(i, (i + step) % size) for i in range(size)])  2.49 us
    pallas_call x1, Pallas kernels, shards(): pl.pallas_call(functools.partial(prepare, size=wide), in_specs=[anywhere]...  2.09 us
    ppermute x1, starting transfers between devices, gather_xor(): lax.ppermute(near, core_axis, [(c, c - 1) for c in range(1, cores, 2)])  1.28 us
    ppermute x2, waiting for transfers between devices, fetch(): return lax.ppermute(held, (axis, core_axis), moves)  0.92 us
  transfers between devices with their start and end apart: 14, of which 6 were waited for; matrix products, arithmetic and copies ran while one was open for 0% of the time, Pallas kernels for 13%

profile of v5, /device:TPU:0, one launch (start us, length us, event | category | flops | bytes accessed | tf_op | source)
XLA Modules:
  0.0 31.1 jit_solution(16485797219255694080)
XLA Ops:
  0.6 3.0 %collective-permute-start = (bf16[1,4,1600]{2,1,0:T(4,128)(2,1)}, bf16[1,4,1600]{2,1,0:T(4,128)(2,1)S(1)}, u32[]{:S(2)}, u32[]{:S(2)}) collective-permute-start(bf16[1,4,1600]{2,1,0:T(4,128)(2,1)} %bitcast.21), channel_id=1, source_target_pairs={{0,4},{4,0},{8,12},{12,8},{16,20},{20,16},{24,28},{28,24},{1,5},{5... | collective-permute-start | bytes 38408 | tf_op jit(solution)/shard_map/ppermute | solution.py:91
  3.7 2.1 %shard_map.228 = (f32[8,40]{1,0:T(8,128)S(1)}, f32[8,256]{1,0:T(8,128)S(1)}, f32[8,400]{1,0:T(8,128)S(1)}, bf16[3,4,400]{2,1,0:T(4,128)(2,1)S(1)}, f32[1,1600]{1...) custom-call(s32[4]{0:T(128)} %source_ref.1, ...), custom_call_target="tpu_custom_call" | custom-call | tf_op jit(solution)/shard_map/pallas_call | solution.py:481
  5.8 0.0 copy-start
  5.8 0.8 %collective-permute-start.1 = (bf16[2,4,1600]{2,1,0:T(4,128)(2,1)S(1)}, bf16[2,4,1600]{2,1,0:T(4,128)(2,1)S(1)}, u32[]{:S(2)}, u32[]{:S(2)}) collective-permute-start(bf16[2,4,1600]{2,1,0:T(4,128)(2,1)S(1)} %shard_map.229.refs_0_), channel_id=1, source_target_pairs={{1,9},{3,11},{5,13},{7,15},{9,1},{11,3},{13,5},{15,7},{17,25},{19,... | collective-permute-start | bytes 76808 | tf_op jit(solution)/shard_map/ppermute | solution.py:83
  6.6 3.9 %collective-permute-start.3 = (bf16[2,4,1600]{2,1,0:T(4,128)(2,1)S(1)}, bf16[2,4,1600]{2,1,0:T(4,128)(2,1)S(1)}, u32[]{:S(2)}, u32[]{:S(2)}) collective-permute-start(bf16[2,4,1600]{2,1,0:T(4,128)(2,1)S(1)} %shard_map.229.refs_0_), channel_id=1, source_target_pairs={{0,24},{1,17},{2,26},{3,19},{4,28},{5,21},{6,30},{7,23},{8,16},{9,... | collective-permute-start | bytes 76808 | tf_op jit(solution)/shard_map/ppermute | solution.py:83
  10.5 1.3 %collective-permute-start.2 = (bf16[2,4,1600]{2,1,0:T(4,128)(2,1)S(1)}, bf16[2,4,1600]{2,1,0:T(4,128)(2,1)S(1)}, u32[]{:S(2)}, u32[]{:S(2)}) collective-permute-start(bf16[2,4,1600]{2,1,0:T(4,128)(2,1)S(1)} %collective-permute-done.1.refs_1_), channel_id=1, source_target_pairs={{1,0},{3,2},{5,4},{7,6},{9,8},{11,10},{13,12},{15,14},{17,16},{19,... | collective-permute-start | bytes 76808 | tf_op jit(solution)/shard_map/ppermute | solution.py:86
  11.8 0.9 %collective-permute-done.3.refs_3_ = bf16[2,4,1600]{2,1,0:T(4,128)(2,1)S(1)} collective-permute-done((bf16[2,4,1600]{2,1,0:T(4,128)(2,1)S(1)}, bf16[2,4,1600]{2,1,0:T(4,128)(2,1)S(1)}, u32[]{:S(2)}, u32[]{:S(2)}) %collective-permute-start.3) | collective-permute-done | bytes 25632 | tf_op jit(solution)/shard_map/ppermute | solution.py:83
  12.7 0.3 collective-permute-start.4
  13.0 0.6 %collective-permute-done.2.refs_2_ = bf16[2,4,1600]{2,1,0:T(4,128)(2,1)S(1)} collective-permute-done((bf16[2,4,1600]{2,1,0:T(4,128)(2,1)S(1)}, bf16[2,4,1600]{2,1,0:T(4,128)(2,1)S(1)}, u32[]{:S(2)}, u32[]{:S(2)}) %collective-permute-start.2) | collective-permute-done | bytes 25632 | tf_op jit(solution)/shard_map/ppermute | solution.py:86
  13.6 0.3 %collective-permute-done.4.refs_4_ = bf16[2,4,1600]{2,1,0:T(4,128)(2,1)S(1)} collective-permute-done((bf16[2,4,1600]{2,1,0:T(4,128)(2,1)S(1)}, bf16[2,4,1600]{2,1,0:T(4,128)(2,1)S(1)}, u32[]{:S(2)}, u32[]{:S(2)}) %collective-permute-start.4) | collective-permute-done | bytes 25632 | tf_op jit(solution)/shard_map/ppermute | solution.py:87
  13.9 1.2 %shard_map.230 = (f32[4,692]{1,0:T(4,128)S(1)}, f32[4,400]{1,0:T(4,128)S(1)}, bf16[8,1600]{1,0:T(8,128)(2,1)S(1)}, f32[4,400]{1,0:T(4,128)S(1)}, f32[4,400]{1,0:T(4,128)S(1)}) custom-call(bf16[2,4,1600]{2,1,0:T(4,128)(2,1)S(1)} %shard_map.229.refs_0_, bf16[2,4,1600]{2,1,0:T(4,128)(2,1)S(1)} %collective-permute-done.1.refs_1_, ...), custom_call_target="tpu_custom_call" | custom-call | tf_op jit(solution)/shard_map/pallas_call | solution.py:433
  15.2 0.3 %collective-permute-start.5 = (f32[4,692]{1,0:T(4,128)S(1)}, f32[4,692]{1,0:T(4,128)S(1)}, u32[]{:S(2)}, u32[]{:S(2)}) collective-permute-start(f32[4,692]{1,0:T(4,128)S(1)} %get-tuple-element.36.refs_1_), channel_id=1, source_target_pairs={{0,1},{1,2},{2,3},{3,0},{4,5},{5,6},{6,7},{7,4},{8,9},{9,10},{10,1... | collective-permute-start | bytes 33224 | tf_op jit(solution)/shard_map/ppermute | solution.py:38
  15.5 1.6 %collective-permute-start.6 = (f32[4,692]{1,0:T(4,128)S(1)}, f32[4,692]{1,0:T(4,128)S(1)}, u32[]{:S(2)}, u32[]{:S(2)}) collective-permute-start(f32[4,692]{1,0:T(4,128)S(1)} %get-tuple-element.36.refs_1_), channel_id=1, source_target_pairs={{0,2},{1,3},{2,0},{3,1},{4,6},{5,7},{6,4},{7,5},{8,10},{9,11},{10,... | collective-permute-start | bytes 33224 | tf_op jit(solution)/shard_map/ppermute | solution.py:38
  17.1 1.3 %collective-permute-start.7 = (f32[4,692]{1,0:T(4,128)S(1)}, f32[4,692]{1,0:T(4,128)S(1)}, u32[]{:S(2)}, u32[]{:S(2)}) collective-permute-start(f32[4,692]{1,0:T(4,128)S(1)} %get-tuple-element.36.refs_1_), channel_id=1, source_target_pairs={{0,3},{1,0},{2,1},{3,2},{4,7},{5,4},{6,5},{7,6},{8,11},{9,8},{10,9... | collective-permute-start | bytes 33224 | tf_op jit(solution)/shard_map/ppermute | solution.py:38
  18.4 0.0 copy-start.1
  18.4 0.0 copy-start.5
  18.4 0.0 copy-start.6
  18.4 0.0 copy-start.7
  18.5 0.9 %shard_map.231 = (f32[4,400]{1,0:T(4,128)S(1)}, bf16[3,4,400]{2,1,0:T(4,128)(2,1)}) custom-call(bf16[8,1600]{1,0:T(8,128)(2,1)S(1)} %get-tuple-element.32.refs_0_, bf16[2,400,1600]{2,1,0:T(8,128)(2,1)S(1)} %bitcast.16, f32[4,400]{1,0:T(4,128)S(1)} %get-tuple-element.33.refs_2_, bf16[3,4,400]{2,1,0:T(4,128)(2,1)S(1)} %get-tuple-element.34.refs_3_), custom_call_target="tpu_custom_call" | custom-call | tf_op jit(solution)/shard_map/pallas_call | solution.py:433
  19.4 0.4 %collective-permute-done.7.refs_4_ = f32[4,692]{1,0:T(4,128)S(1)} collective-permute-done((f32[4,692]{1,0:T(4,128)S(1)}, f32[4,692]{1,0:T(4,128)S(1)}, u32[]{:S(2)}, u32[]{:S(2)}) %collective-permute-start.7) | collective-permute-done | bytes 11104 | tf_op jit(solution)/shard_map/ppermute | solution.py:38
  19.8 0.8 %shard_map.232 = (bf16[4,1792]{1,0:T(4,128)(2,1)S(1)}, f32[4,640]{1,0:T(4,128)S(1)}) custom-call(f32[4,400]{1,0:T(4,128)S(1)} %get-tuple-element.35.refs_0_.refs_6_, f32[4,692]{1,0:T(4,128)S(1)} %get-tuple-element.36.refs_1_, f32[4,692]{1,0:T(4,128)S(1)} %collective-permute-done.5.refs_2_, f32[4,692]{1,0:T(4,128)S(1)} %collective-permute-done.6.refs_3_, ...), custom_call_target="tpu_custom_call" | custom-call | tf_op jit(solution)/shard_map/pallas_call | solution.py:433
  20.6 0.5 %collective-permute-start.10 = (bf16[4,1792]{1,0:T(4,128)(2,1)S(1)}, bf16[4,1792]{1,0:T(4,128)(2,1)S(1)}, u32[]{:S(2)}, u32[]{:S(2)}) collective-permute-start(bf16[4,1792]{1,0:T(4,128)(2,1)S(1)} %get-tuple-element.38.refs_0_), channel_id=1, source_target_pairs={{0,1},{1,2},{2,3},{3,0},{4,5},{5,6},{6,7},{7,4},{8,9},{9,10},{10,1... | collective-permute-start | bytes 43016 | tf_op jit(solution)/shard_map/ppermute | solution.py:38
  21.0 1.7 %collective-permute-start.8 = (bf16[4,1792]{1,0:T(4,128)(2,1)S(1)}, bf16[4,1792]{1,0:T(4,128)(2,1)S(1)}, u32[]{:S(2)}, u32[]{:S(2)}) collective-permute-start(bf16[4,1792]{1,0:T(4,128)(2,1)S(1)} %get-tuple-element.38.refs_0_), channel_id=1, source_target_pairs={{0,2},{1,3},{2,0},{3,1},{4,6},{5,7},{6,4},{7,5},{8,10},{9,11},{10,... | collective-permute-start | bytes 43016 | tf_op jit(solution)/shard_map/ppermute | solution.py:38
  22.7 0.3 %collective-permute-start.9 = (bf16[4,1792]{1,0:T(4,128)(2,1)S(1)}, bf16[4,1792]{1,0:T(4,128)(2,1)S(1)}, u32[]{:S(2)}, u32[]{:S(2)}) collective-permute-start(bf16[4,1792]{1,0:T(4,128)(2,1)S(1)} %get-tuple-element.38.refs_0_), channel_id=1, source_target_pairs={{0,3},{1,0},{2,1},{3,2},{4,7},{5,4},{6,5},{7,6},{8,11},{9,8},{10,9... | collective-permute-start | bytes 43016 | tf_op jit(solution)/shard_map/ppermute | solution.py:38
  23.2 1.0 %shard_map.233 = (bf16[4,1600]{1,0:T(4,128)(2,1)S(1)}, f32[4,16,400]{2,1,0:T(8,128)}, bf16[4,640]{1,0:T(4,128)(2,1)}) custom-call(f32[4,640]{1,0:T(4,128)S(1)} %get-tuple-element.39.refs_0_, f32[4,692]{1,0:T(4,128)S(1)} %get-tuple-element.36.refs_1_, f32[4,692]{1,0:T(4,128)S(1)} %collective-permute-done.5.refs_2_, ...), custom_call_target="tpu_custom_call" | custom-call | tf_op jit(solution)/shard_map/pallas_call | solution.py:433
  24.2 0.6 %collective-permute-done.8.refs_1_ = bf16[4,1792]{1,0:T(4,128)(2,1)S(1)} collective-permute-done((bf16[4,1792]{1,0:T(4,128)(2,1)S(1)}, bf16[4,1792]{1,0:T(4,128)(2,1)S(1)}, u32[]{:S(2)}, u32[]{:S(2)}) %collective-permute-start.8) | collective-permute-done | bytes 14368 | tf_op jit(solution)/shard_map/ppermute | solution.py:38
  24.8 0.9 %shard_map.234 = (f32[4,400]{1,0:T(4,128)S(1)}, bf16[4,1664]{1,0:T(4,128)(2,1)S(1)}) custom-call(bf16[4,1792]{1,0:T(4,128)(2,1)S(1)} %get-tuple-element.38.refs_0_, bf16[4,1792]{1,0:T(4,128)(2,1)S(1)} %collective-permute-done.8.refs_1_, bf16[4,1792]{1,0:T(4,128)(2,1)S(1)} %collective-permute-done.9.refs_2_, ...), custom_call_target="tpu_custom_call" | custom-call | tf_op jit(solution)/shard_map/pallas_call | solution.py:433
  25.6 0.9 %collective-permute-start.11 = (bf16[4,1664]{1,0:T(4,128)(2,1)S(1)}, bf16[4,1664]{1,0:T(4,128)(2,1)S(1)}, u32[]{:S(2)}, u32[]{:S(2)}) collective-permute-start(bf16[4,1664]{1,0:T(4,128)(2,1)S(1)} %get-tuple-element.42.refs_0_), channel_id=1, source_target_pairs={{0,1},{1,2},{2,3},{3,0},{4,5},{5,6},{6,7},{7,4},{8,9},{9,10},{10,1... | collective-permute-start | bytes 39944 | tf_op jit(solution)/shard_map/ppermute | solution.py:38
  26.6 0.9 %collective-permute-start.12 = (bf16[4,1664]{1,0:T(4,128)(2,1)S(1)}, bf16[4,1664]{1,0:T(4,128)(2,1)S(1)}, u32[]{:S(2)}, u32[]{:S(2)}) collective-permute-start(bf16[4,1664]{1,0:T(4,128)(2,1)S(1)} %get-tuple-element.42.refs_0_), channel_id=1, source_target_pairs={{0,2},{1,3},{2,0},{3,1},{4,6},{5,7},{6,4},{7,5},{8,10},{9,11},{10,... | collective-permute-start | bytes 39944 | tf_op jit(solution)/shard_map/ppermute | solution.py:38
  27.5 1.3 %collective-permute-start.13 = (bf16[4,1664]{1,0:T(4,128)(2,1)S(1)}, bf16[4,1664]{1,0:T(4,128)(2,1)S(1)}, u32[]{:S(2)}, u32[]{:S(2)}) collective-permute-start(bf16[4,1664]{1,0:T(4,128)(2,1)S(1)} %get-tuple-element.42.refs_0_), channel_id=1, source_target_pairs={{0,3},{1,0},{2,1},{3,2},{4,7},{5,4},{6,5},{7,6},{8,11},{9,8},{10,9... | collective-permute-start | bytes 39944 | tf_op jit(solution)/shard_map/ppermute | solution.py:38
  28.8 1.5 %collective-permute-done.12.refs_2_ = bf16[4,1664]{1,0:T(4,128)(2,1)S(1)} collective-permute-done((bf16[4,1664]{1,0:T(4,128)(2,1)S(1)}, bf16[4,1664]{1,0:T(4,128)(2,1)S(1)}, u32[]{:S(2)}, u32[]{:S(2)}) %collective-permute-start.12) | collective-permute-done | bytes 13344 | tf_op jit(solution)/shard_map/ppermute | solution.py:38
  30.3 0.8 %shard_map.235 = bf16[4,400]{1,0:T(4,128)(2,1)} custom-call(bf16[4,1664]{1,0:T(4,128)(2,1)S(1)} %get-tuple-element.42.refs_0_, bf16[4,1664]{1,0:T(4,128)(2,1)S(1)} %collective-permute-done.11.refs_1_, bf16[4,1664]{1,0:T(4,128)(2,1)S(1)} %collective-permute-done.12.refs_2_, bf16[4,1664]{1,0:T(4,128)(2,1)S(1)} %collective-permute-done.13.refs_3_, ...), custom_call_target="tpu_custom_call" | custom-call | tf_op jit(solution)/shard_map/pallas_call | solution.py:433
  (33 shorter events, 0.1 us)
Async XLA Ops:
  0.6 5.2 %collective-permute-start = (bf16[1,4,1600]{2,1,0:T(4,128)(2,1)}, bf16[1,4,1600]{2,1,0:T(4,128)(2,1)S(1)}, u32[]{:S(2)}, u32[]{:S(2)}) collective-permute-start(bf16[1,4,1600]{2,1,0:T(4,128)(2,1)} %bitcast.21), channel_id=1, source_target_pairs={{0,4},{4,0},{8,12},{12,8},{16,20},{20,16},{24,28},{28,24},{1,5},{5... | collective-permute-start | bytes 38408 | tf_op jit(solution)/shard_map/ppermute | solution.py:91
  3.7 2.1 %copy-start.8 = (bf16[4,1600]{1,0:T(4,128)(2,1)S(1)}, bf16[4,1600]{1,0:T(4,128)(2,1)}, u32[]{:S(2)}) copy-start(bf16[4,1600]{1,0:T(4,128)(2,1)} %param.21) | copy-start | bytes 38404
  5.8 12.6 %copy-start = (bf16[1600,2,400]{0,2,1:T(8,128)(2,1)S(1)}, bf16[1600,2,400]{0,2,1:T(8,128)(2,1)}, u32[]{:S(2)}) copy-start(bf16[1600,2,400]{0,2,1:T(8,128)(2,1)} %param.30) | copy-start | bytes 7680004
  5.8 4.7 %collective-permute-start.1 = (bf16[2,4,1600]{2,1,0:T(4,128)(2,1)S(1)}, bf16[2,4,1600]{2,1,0:T(4,128)(2,1)S(1)}, u32[]{:S(2)}, u32[]{:S(2)}) collective-permute-start(bf16[2,4,1600]{2,1,0:T(4,128)(2,1)S(1)} %shard_map.229.refs_0_), channel_id=1, source_target_pairs={{1,9},{3,11},{5,13},{7,15},{9,1},{11,3},{13,5},{15,7},{17,25},{19,... | collective-permute-start | bytes 76808 | tf_op jit(solution)/shard_map/ppermute | solution.py:83
  6.6 6.1 %collective-permute-start.3 = (bf16[2,4,1600]{2,1,0:T(4,128)(2,1)S(1)}, bf16[2,4,1600]{2,1,0:T(4,128)(2,1)S(1)}, u32[]{:S(2)}, u32[]{:S(2)}) collective-permute-start(bf16[2,4,1600]{2,1,0:T(4,128)(2,1)S(1)} %shard_map.229.refs_0_), channel_id=1, source_target_pairs={{0,24},{1,17},{2,26},{3,19},{4,28},{5,21},{6,30},{7,23},{8,16},{9,... | collective-permute-start | bytes 76808 | tf_op jit(solution)/shard_map/ppermute | solution.py:83
  10.5 3.1 %collective-permute-start.2 = (bf16[2,4,1600]{2,1,0:T(4,128)(2,1)S(1)}, bf16[2,4,1600]{2,1,0:T(4,128)(2,1)S(1)}, u32[]{:S(2)}, u32[]{:S(2)}) collective-permute-start(bf16[2,4,1600]{2,1,0:T(4,128)(2,1)S(1)} %collective-permute-done.1.refs_1_), channel_id=1, source_target_pairs={{1,0},{3,2},{5,4},{7,6},{9,8},{11,10},{13,12},{15,14},{17,16},{19,... | collective-permute-start | bytes 76808 | tf_op jit(solution)/shard_map/ppermute | solution.py:86
  12.7 1.2 %collective-permute-start.4 = (bf16[2,4,1600]{2,1,0:T(4,128)(2,1)S(1)}, bf16[2,4,1600]{2,1,0:T(4,128)(2,1)S(1)}, u32[]{:S(2)}, u32[]{:S(2)}) collective-permute-start(bf16[2,4,1600]{2,1,0:T(4,128)(2,1)S(1)} %collective-permute-done.3.refs_3_), channel_id=1, source_target_pairs={{0,1},{1,0},{2,3},{3,2},{4,5},{5,4},{6,7},{7,6},{8,9},{9,8},{10,11... | collective-permute-start | bytes 76808 | tf_op jit(solution)/shard_map/ppermute | solution.py:87
  15.2 4.6 %copy-start.3 = (bf16[4,256,320]{1,2,0:T(8,128)(2,1)S(1)}, bf16[4,256,320]{1,2,0:T(8,128)(2,1)}, u32[]{:S(2)}) copy-start(bf16[4,256,320]{1,2,0:T(8,128)(2,1)} %param.24) | copy-start | bytes 1966084
  15.2 4.6 %copy-start.4 = (bf16[4,256,320]{1,2,0:T(8,128)(2,1)S(1)}, bf16[4,256,320]{1,2,0:T(8,128)(2,1)}, u32[]{:S(2)}) copy-start(bf16[4,256,320]{1,2,0:T(8,128)(2,1)} %param.25) | copy-start | bytes 1966084
  15.2 4.2 %collective-permute-start.5 = (f32[4,692]{1,0:T(4,128)S(1)}, f32[4,692]{1,0:T(4,128)S(1)}, u32[]{:S(2)}, u32[]{:S(2)}) collective-permute-start(f32[4,692]{1,0:T(4,128)S(1)} %get-tuple-element.36.refs_1_), channel_id=1, source_target_pairs={{0,1},{1,2},{2,3},{3,0},{4,5},{5,6},{6,7},{7,4},{8,9},{9,10},{10,1... | collective-permute-start | bytes 33224 | tf_op jit(solution)/shard_map/ppermute | solution.py:38
  15.5 3.9 %collective-permute-start.6 = (f32[4,692]{1,0:T(4,128)S(1)}, f32[4,692]{1,0:T(4,128)S(1)}, u32[]{:S(2)}, u32[]{:S(2)}) collective-permute-start(f32[4,692]{1,0:T(4,128)S(1)} %get-tuple-element.36.refs_1_), channel_id=1, source_target_pairs={{0,2},{1,3},{2,0},{3,1},{4,6},{5,7},{6,4},{7,5},{8,10},{9,11},{10,... | collective-permute-start | bytes 33224 | tf_op jit(solution)/shard_map/ppermute | solution.py:38
  17.1 2.7 %collective-permute-start.7 = (f32[4,692]{1,0:T(4,128)S(1)}, f32[4,692]{1,0:T(4,128)S(1)}, u32[]{:S(2)}, u32[]{:S(2)}) collective-permute-start(f32[4,692]{1,0:T(4,128)S(1)} %get-tuple-element.36.refs_1_), channel_id=1, source_target_pairs={{0,3},{1,0},{2,1},{3,2},{4,7},{5,4},{6,5},{7,6},{8,11},{9,8},{10,9... | collective-permute-start | bytes 33224 | tf_op jit(solution)/shard_map/ppermute | solution.py:38
  18.4 4.7 %copy-start.1 = (bf16[400,1600]{1,0:T(8,128)(2,1)S(1)}, bf16[400,1600]{1,0:T(8,128)(2,1)}, u32[]{:S(2)}) copy-start(bf16[400,1600]{1,0:T(8,128)(2,1)} %refs_12_.1) | copy-start | bytes 3840004
  18.4 4.7 %copy-start.5 = (f32[4,16,400]{2,1,0:T(8,128)S(1)}, f32[4,16,400]{2,1,0:T(8,128)}, u32[]{:S(2)}) copy-start(f32[4,16,400]{2,1,0:T(8,128)} %refs_10_.1) | copy-start | bytes 307204
  18.4 4.7 %copy-start.6 = (bf16[100,400]{0,1:T(8,128)(2,1)S(1)}, bf16[100,400]{0,1:T(8,128)(2,1)}, u32[]{:S(2)}) copy-start(bf16[100,400]{0,1:T(8,128)(2,1)} %param.34) | copy-start | bytes 240004
  18.4 4.7 %copy-start.7 = (f32[16,400]{1,0:T(8,128)S(1)}, f32[16,400]{1,0:T(8,128)}, u32[]{:S(2)}) copy-start(f32[16,400]{1,0:T(8,128)} %refs_9_.1) | copy-start | bytes 76804
  18.4 4.7 %copy-start.9 = (f32[400]{0:T(512)S(1)}, f32[400]{0:T(512)}, u32[]{:S(2)}) copy-start(f32[400]{0:T(512)} %param.35) | copy-start | bytes 4804
  18.5 4.7 %copy-start.10 = (f32[400]{0:T(512)S(1)}, f32[400]{0:T(512)}, u32[]{:S(2)}) copy-start(f32[400]{0:T(512)} %param.37) | copy-start | bytes 4804
  19.4 5.4 %copy-start.2 = (bf16[1600,400]{0,1:T(8,128)(2,1)S(1)}, bf16[1600,400]{0,1:T(8,128)(2,1)}, u32[]{:S(2)}) copy-start(bf16[1600,400]{0,1:T(8,128)(2,1)} %param.38) | copy-start | bytes 3840004
  20.6 9.8 %copy-start.11 = (f32[400]{0:T(512)S(1)}, f32[400]{0:T(512)}, u32[]{:S(2)}) copy-start(f32[400]{0:T(512)} %param.40) | copy-start | bytes 4804
  20.6 9.8 %copy-start.12 = (f32[400]{0:T(512)S(1)}, f32[400]{0:T(512)}, u32[]{:S(2)}) copy-start(f32[400]{0:T(512)} %param.41) | copy-start | bytes 4804
  20.6 3.6 %collective-permute-start.10 = (bf16[4,1792]{1,0:T(4,128)(2,1)S(1)}, bf16[4,1792]{1,0:T(4,128)(2,1)S(1)}, u32[]{:S(2)}, u32[]{:S(2)}) collective-permute-start(bf16[4,1792]{1,0:T(4,128)(2,1)S(1)} %get-tuple-element.38.refs_0_), channel_id=1, source_target_pairs={{0,1},{1,2},{2,3},{3,0},{4,5},{5,6},{6,7},{7,4},{8,9},{9,10},{10,1... | collective-permute-start | bytes 43016 | tf_op jit(solution)/shard_map/ppermute | solution.py:38
  21.0 3.7 %collective-permute-start.8 = (bf16[4,1792]{1,0:T(4,128)(2,1)S(1)}, bf16[4,1792]{1,0:T(4,128)(2,1)S(1)}, u32[]{:S(2)}, u32[]{:S(2)}) collective-permute-start(bf16[4,1792]{1,0:T(4,128)(2,1)S(1)} %get-tuple-element.38.refs_0_), channel_id=1, source_target_pairs={{0,2},{1,3},{2,0},{3,1},{4,6},{5,7},{6,4},{7,5},{8,10},{9,11},{10,... | collective-permute-start | bytes 43016 | tf_op jit(solution)/shard_map/ppermute | solution.py:38
  22.7 2.0 %collective-permute-start.9 = (bf16[4,1792]{1,0:T(4,128)(2,1)S(1)}, bf16[4,1792]{1,0:T(4,128)(2,1)S(1)}, u32[]{:S(2)}, u32[]{:S(2)}) collective-permute-start(bf16[4,1792]{1,0:T(4,128)(2,1)S(1)} %get-tuple-element.38.refs_0_), channel_id=1, source_target_pairs={{0,3},{1,0},{2,1},{3,2},{4,7},{5,4},{6,5},{7,6},{8,11},{9,8},{10,9... | collective-permute-start | bytes 43016 | tf_op jit(solution)/shard_map/ppermute | solution.py:38
  25.6 3.2 %collective-permute-start.11 = (bf16[4,1664]{1,0:T(4,128)(2,1)S(1)}, bf16[4,1664]{1,0:T(4,128)(2,1)S(1)}, u32[]{:S(2)}, u32[]{:S(2)}) collective-permute-start(bf16[4,1664]{1,0:T(4,128)(2,1)S(1)} %get-tuple-element.42.refs_0_), channel_id=1, source_target_pairs={{0,1},{1,2},{2,3},{3,0},{4,5},{5,6},{6,7},{7,4},{8,9},{9,10},{10,1... | collective-permute-start | bytes 39944 | tf_op jit(solution)/shard_map/ppermute | solution.py:38
  26.6 3.8 %collective-permute-start.12 = (bf16[4,1664]{1,0:T(4,128)(2,1)S(1)}, bf16[4,1664]{1,0:T(4,128)(2,1)S(1)}, u32[]{:S(2)}, u32[]{:S(2)}) collective-permute-start(bf16[4,1664]{1,0:T(4,128)(2,1)S(1)} %get-tuple-element.42.refs_0_), channel_id=1, source_target_pairs={{0,2},{1,3},{2,0},{3,1},{4,6},{5,7},{6,4},{7,5},{8,10},{9,11},{10,... | collective-permute-start | bytes 39944 | tf_op jit(solution)/shard_map/ppermute | solution.py:38
  27.5 2.8 %collective-permute-start.13 = (bf16[4,1664]{1,0:T(4,128)(2,1)S(1)}, bf16[4,1664]{1,0:T(4,128)(2,1)S(1)}, u32[]{:S(2)}, u32[]{:S(2)}) collective-permute-start(bf16[4,1664]{1,0:T(4,128)(2,1)S(1)} %get-tuple-element.42.refs_0_), channel_id=1, source_target_pairs={{0,3},{1,0},{2,1},{3,2},{4,7},{5,4},{6,5},{7,6},{8,11},{9,8},{10,9... | collective-permute-start | bytes 39944 | tf_op jit(solution)/shard_map/ppermute | solution.py:38

commit v6 on v5

--- a/solution.py
+++ b/solution.py
@@ -32,12 +32,8 @@
     return 1.0 / (1.0 + jnp.exp(-v))
 
 
-def exchange(part, axis):
-    size = lax.axis_size(axis)
-    return [part] + [
-        lax.ppermute(part, axis, [(i, (i + step) % size) for i in range(size)])
-        for step in range(1, size)
-    ]
+def exchange(part, order):
+    return [part] + [swap(part, step) for step in order]
 
 
 def join(*refs):
@@ -46,6 +42,12 @@
     for ref in given:
         out_ref[at : at + ref.shape[0]] = ref[...]
         at += ref.shape[0]
+
+
+def swap(part, step):
+    size = lax.axis_size("narrow")
+    assert size == 4
+    return lax.ppermute(part, "narrow", [(i, i ^ step) for i in range(size)])
 
 
 def digits_of(size):
@@ -115,12 +117,6 @@
         entry = entry + block * (1 << done)
         done += count
     return entry
-
-
-def stack_pieces(me, pieces, held):
-    size = len(pieces)
-    for step, piece in enumerate(pieces):
-        held[lax.rem(me - step + size, size)] = piece[...]
 
 
 def cut(rows, count):
@@ -197,8 +193,8 @@
 
 def project_in(*refs, size):
     arrived_refs = refs[:size]
-    (chosen_ref, base_ref, gain_ref, heads_w_ref, xproj_ref, in_w_ref, part_ref, act_ref,
-     normed_ref, channel_ref, cols_ref, blocks) = refs[size:]
+    (other_w_ref, chosen_ref, base_ref, gain_ref, heads_w_ref, xproj_ref, in_w_ref, part_ref,
+     state_ref, act_ref, normed_ref, channel_ref, cols_ref, blocks) = refs[size:]
     rows, cols = cols_ref.shape
     arrived = jnp.concatenate(
         [ref[i].astype(F32) for ref in arrived_refs for i in range(ref.shape[0])], axis=0
@@ -211,33 +207,37 @@
     normed = (routed * scale * gain_ref[...]).astype(BF16)
     normed_ref[...] = normed
     channel_in = dot_nt(normed, in_w_ref[...])[:rows]
-    heads = dot_nt(normed, heads_w_ref[...])[:rows].astype(BF16).astype(F32)
+    heads = [
+        dot_nt(normed, w[...])[:rows].astype(BF16).astype(F32) for w in (heads_w_ref, other_w_ref)
+    ]
     channel_ref[...] = channel_in
     conv_out = base_ref[:rows] + base_ref[rows:] * channel_in
     act = conv_out * sigmoid(conv_out)
     act_ref[...] = act
     state = dot_nt(act.astype(BF16), xproj_ref[...])
-    part_ref[...] = jnp.concatenate([heads, state], axis=1)
-
-
-def project_gate(normed_ref, gate_w_ref, channel_ref, old_conv_ref, gate_ref, new_conv_ref):
+    state_ref[...] = state
+    part_ref[...] = jnp.concatenate([*heads, state], axis=1)
+
+
+def keep_conv(channel_ref, old_conv_ref, new_conv_ref):
     taps = new_conv_ref.shape[0]
     for tap in range(taps - 1):
         new_conv_ref[tap] = old_conv_ref[tap]
     new_conv_ref[taps - 1] = channel_ref[...].astype(BF16)
-    gate = dot_nt(normed_ref[...], gate_w_ref[1])[: gate_ref.shape[0]]
-    gate_ref[...] = gate * sigmoid(gate)
-
-
-def state_step(kv_ref, *refs, size, head_width):
-    pieces = refs[:size]
-    (act_ref, gate_ref, dt_w_ref, dt_b_ref, a_log_ref, ssm_ref, skip_ref, out_w_ref, part_ref,
-     new_ssm_ref, new_kv_ref) = refs[size:]
+
+
+def state_step(
+    kv_ref, far_ref, *refs, size,
+):
+    states = refs[: size - 1]
+    (normed_ref, gate_w_ref, act_ref, dt_w_ref, dt_b_ref, a_log_ref, ssm_ref, skip_ref, out_w_ref,
+     part_ref, new_ssm_ref, new_kv_ref) = refs[size - 1 :]
     new_kv_ref[...] = kv_ref[...].astype(BF16)
-    state = pieces[0][:, head_width:]
-    for piece in pieces[1:]:
-        state = state + piece[:, head_width:]
+    state = far_ref[:, far_ref.shape[1] - states[0].shape[1] :]
+    for other in states:
+        state = state + other[...]
     rows = state.shape[0]
+    gate = dot_nt(normed_ref[...], gate_w_ref[1])[:rows]
     rank = dt_w_ref.shape[1]
     depth = a_log_ref.shape[0]
     step = dot_nt(state[:, :rank].astype(BF16), dt_w_ref[...]) + dt_b_ref[...]
@@ -257,17 +257,20 @@
         new_ssm_ref[r] = fresh
         outs.append(jnp.sum(maps[depth : 2 * depth, r : r + 1] * fresh, axis=0, keepdims=True))
     state_out = jnp.concatenate(outs, axis=0) + skip_ref[...] * act
-    ssm_heads = (state_out * gate_ref[...]).astype(BF16)
+    ssm_heads = (state_out * (gate * sigmoid(gate))).astype(BF16)
     part_ref[...] = jnp.dot(ssm_heads, out_w_ref[...], preferred_element_type=F32).astype(BF16)
 
 
-def attend(*refs, size, head_width):
-    pieces = refs[:size]
-    (live_ref, keys_ref, values_ref, part_ref, new_kv_ref, held) = refs[size:]
+def attend(
+    near_ref, far_ref, live_ref, keys_ref, values_ref, part_ref, new_kv_ref, held, *, head_width
+):
     me = lax.axis_index("narrow")
-    stack_pieces(me, pieces, held)
     rows = held.shape[1]
-    heads = jnp.concatenate([held[i][:, :head_width] for i in range(size)], axis=1)
+    for step in range(held.shape[0]):
+        piece = far_ref if step & 2 else near_ref
+        at = (step & 1) * head_width
+        held[lax.bitwise_xor(me, step)] = piece[:, at : at + head_width]
+    heads = jnp.concatenate([held[i] for i in range(held.shape[0])], axis=1)
     new_kv_ref[...] = heads[:, QUERY_WIDTH:]
     tall = jnp.concatenate([heads, jnp.zeros((8 - rows, heads.shape[1]), F32)], axis=0)
     tall = jnp.concatenate([tall, jnp.zeros((8, -tall.shape[1] % 128), F32)], axis=1)
@@ -498,14 +501,16 @@
         compiler_params=pltpu.CompilerParams(vmem_limit_bytes=4 * 1024 * 1024),
     )(*pinned)
     arrived = gather_xor(tokens, "wide", "narrow", prepared[:1])
-    part_width = head_width + w_xproj.shape[1]
+    other_w = swap(large[0], 1)
+    part_width = 2 * head_width + w_xproj.shape[1]
     chosen, live, base, old_conv, *weights = prepared
-    part, act, normed, channel_in, routed_cols = call(
+    part, state, act, normed, channel_in, routed_cols = call(
         functools.partial(project_in, size=len(arrived)),
         (),
-        (*arrived, chosen, base, *weights),
+        (*arrived, other_w, chosen, base, *weights),
         (
             shape((rows, part_width), F32),
+            shape((rows, w_xproj.shape[1]), F32),
             shape((rows, cols), F32),
             shape((8, MODEL_WIDTH), BF16),
             shape((rows, cols), F32),
@@ -513,29 +518,26 @@
         ),
         (pltpu.VMEM((narrow, rows, cols), F32),),
     )
-    pieces = exchange(part, "narrow")
-    gate, new_conv = call(
-        project_gate,
+    far = swap(part, 2)
+    states = [state, swap(state, 1), swap(state, 3)]
+    second, key_value = call(
+        functools.partial(attend, head_width=head_width),
         (),
-        (normed, w_xz.transpose(1, 2, 0), channel_in, old_conv),
-        (shape((rows, cols), F32), shape(old_conv.shape, BF16)),
-    )
-    second, key_value = call(
-        functools.partial(attend, size=narrow, head_width=head_width),
-        (),
-        (*pieces, live, cached_key_rows.transpose(0, 2, 1), cached_value_rows.transpose(0, 2, 1)),
+        (
+            part, far, live, cached_key_rows.transpose(0, 2, 1),
+            cached_value_rows.transpose(0, 2, 1),
+        ),
         (
             shape((rows, QUERY_WIDTH + 3 * HEAD_SIZE), BF16),
             shape((rows, 2 * KEY_VALUE_WIDTH), F32),
         ),
-        (pltpu.VMEM((narrow, rows, part_width), F32),),
-        after=(gate,),
+        (pltpu.VMEM((narrow, rows, head_width), F32),),
     )
     state_part, new_ssm, new_kv = call(
-        functools.partial(state_step, size=narrow, head_width=head_width),
+        functools.partial(state_step, size=narrow),
         (),
         (
-            key_value, *pieces, act, gate, w_dt.T, dt_bias[None], a_log, ssm_state, skip_d[None], w_ssm_out,
+            key_value, far, *states, normed, w_xz.transpose(1, 2, 0), act, w_dt.T, dt_bias[None], a_log, ssm_state, skip_d[None], w_ssm_out,
         ),
         (
             shape((rows, MODEL_WIDTH), BF16),
@@ -543,8 +545,8 @@
             shape(key_value.shape, BF16),
         ),
     )
-    pieces = exchange(second, "narrow")
-    pieces = [pieces[0]] + [pieces[k] for k in (2, 3, 1)]
+    (new_conv,) = call(keep_conv, (), (channel_in, old_conv), (shape(old_conv.shape, BF16),))
+    pieces = exchange(second, (3, 2, 1))
     spread = (
         lax.broadcasted_iota(jnp.int32, (QUERY_HEADS, QUERY_WIDTH), 1) // HEAD_SIZE
         == lax.broadcasted_iota(jnp.int32, (QUERY_HEADS, QUERY_WIDTH), 0)
@@ -555,7 +557,7 @@
         (*pieces, state_part, spread, w_attn_out.T),
         (shape((rows, cols), F32), shape((rows, MODEL_WIDTH + 64), BF16)),
     )
-    pieces = exchange(third, "narrow")
+    pieces = exchange(third, (3, 2, 1))
     (out,) = call(
         functools.partial(finish, size=narrow),
         (),

time: 31.3 us -> 30.7 us (0.981)
  starting transfers between devices: 18.2 us -> 15.9 us
  waiting for transfers between devices: 4.32 us -> 5.49 us
  Pallas kernels: 7.65 us -> 8.2 us
    ppermute x9 -> x10, starting transfers between devices: 8.9 us -> 6.53 us  [swap(): return lax.ppermute(part, 'narrow', [(i, i ^ step) for i in range(size)])]
    ppermute x9 -> x10, waiting for transfers between devices: 2.49 us -> 4.1 us  [swap(): return lax.ppermute(part, 'narrow', [(i, i ^ step) for i in range(size)])]
    ppermute x1, starting transfers between devices: 0.28 us -> 0.9 us  [gather_xor(): far_swap = lax.ppermute(far, core_axis, [(c, c ^ 1) for c in range(cores)])]
    pallas_call x7, Pallas kernels: 5.55 us -> 6.11 us  [call(): pl.pallas_call(run, in_specs=[pl.BlockSpec(memory_space=pl.ANY)] * len(af...]
    ppermute x1, starting transfers between devices: 3.03 us -> 2.59 us  [gather_xor(): lax.ppermute(held, axis, [(i, i ^ step << place) for i in range(size)])]
    ppermute x2, waiting for transfers between devices: 0.92 us -> 0.54 us  [fetch(): return lax.ppermute(held, (axis, core_axis), moves)]
  transfers between devices with their start and end apart: 14 -> 15, of which waited for: 6 -> 7; matrix products, arithmetic and copies ran while one was open for 0% -> 0% of each run, Pallas kernels for 13% -> 16%
where the time goes in v6:
time: 30.7 us; the launch traced here: 30.5 us
  starting transfers between devices  15.9 us (52%)
  Pallas kernels  8.2 us (27%)
  waiting for transfers between devices  5.49 us (18%)
  between operations  0.85 us (3%)
    ppermute x10, starting transfers between devices, swap(): return lax.ppermute(part, 'narrow', [(i, i ^ step) for i in range(size)])  6.53 us
    pallas_call x7, Pallas kernels, call(): pl.pallas_call(run, in_specs=[pl.BlockSpec(memory_space=pl.ANY)] * len(af...  6.11 us
    ppermute x2, starting transfers between devices, fetch(): return lax.ppermute(held, (axis, core_axis), moves)  4.59 us
    ppermute x10, waiting for transfers between devices, swap(): return lax.ppermute(part, 'narrow', [(i, i ^ step) for i in range(size)])  4.1 us
    ppermute x1, starting transfers between devices, gather_xor(): lax.ppermute(held, axis, [(i, i ^ step << place) for i in range(size)])  2.59 us
    pallas_call x1, Pallas kernels, shards(): pl.pallas_call(functools.partial(prepare, size=wide), in_specs=[anywhere]...  2.09 us
    ppermute x1, starting transfers between devices, gather_xor(): lax.ppermute(near, core_axis, [(c, c - 1) for c in range(1, cores, 2)])  1.28 us
    ppermute x1, starting transfers between devices, gather_xor(): far_swap = lax.ppermute(far, core_axis, [(c, c ^ 1) for c in range(cores)])  0.9 us
  transfers between devices with their start and end apart: 15, of which 7 were waited for; matrix products, arithmetic and copies ran while one was open for 0% of the time, Pallas kernels for 16%

profile of v6, /device:TPU:0, one launch (start us, length us, event | category | flops | bytes accessed | tf_op | source)
XLA Modules:
  0.0 30.5 jit_solution(5677984381052183498)
XLA Ops:
  0.6 0.5 %collective-permute-start.5 = (bf16[560,1600]{1,0:T(8,128)(2,1)}, bf16[560,1600]{1,0:T(8,128)(2,1)S(1)}, u32[]{:S(2)}, u32[]{:S(2)}) collective-permute-start(bf16[560,1600]{1,0:T(8,128)(2,1)} %bitcast.27), channel_id=1, source_target_pairs={{0,1},{1,0},{2,3},{3,2},{4,5},{5,4},{6,7},{7,6},{8,9},{9,8},{10,11... | collective-permute-start | bytes 5376008 | tf_op jit(solution)/shard_map/ppermute | solution.py:50
  1.2 2.6 %collective-permute-start = (bf16[1,4,1600]{2,1,0:T(4,128)(2,1)}, bf16[1,4,1600]{2,1,0:T(4,128)(2,1)S(1)}, u32[]{:S(2)}, u32[]{:S(2)}) collective-permute-start(bf16[1,4,1600]{2,1,0:T(4,128)(2,1)} %bitcast.21), channel_id=1, source_target_pairs={{0,4},{4,0},{8,12},{12,8},{16,20},{20,16},{24,28},{28,24},{1,5},{5... | collective-permute-start | bytes 38408 | tf_op jit(solution)/shard_map/ppermute | solution.py:93
  3.7 2.1 %shard_map.228 = (f32[8,40]{1,0:T(8,128)S(1)}, f32[8,256]{1,0:T(8,128)S(1)}, f32[8,400]{1,0:T(8,128)S(1)}, bf16[3,4,400]{2,1,0:T(4,128)(2,1)S(1)}, f32[1,1600]{1...) custom-call(s32[4]{0:T(128)} %source_ref.1, ...), custom_call_target="tpu_custom_call" | custom-call | tf_op jit(solution)/shard_map/pallas_call | solution.py:484
  5.9 0.7 %collective-permute-start.1 = (bf16[2,4,1600]{2,1,0:T(4,128)(2,1)S(1)}, bf16[2,4,1600]{2,1,0:T(4,128)(2,1)S(1)}, u32[]{:S(2)}, u32[]{:S(2)}) collective-permute-start(bf16[2,4,1600]{2,1,0:T(4,128)(2,1)S(1)} %shard_map.229.refs_0_), channel_id=1, source_target_pairs={{1,9},{3,11},{5,13},{7,15},{9,1},{11,3},{13,5},{15,7},{17,25},{19,... | collective-permute-start | bytes 76808 | tf_op jit(solution)/shard_map/ppermute | solution.py:85
  6.6 3.9 %collective-permute-start.3 = (bf16[2,4,1600]{2,1,0:T(4,128)(2,1)S(1)}, bf16[2,4,1600]{2,1,0:T(4,128)(2,1)S(1)}, u32[]{:S(2)}, u32[]{:S(2)}) collective-permute-start(bf16[2,4,1600]{2,1,0:T(4,128)(2,1)S(1)} %shard_map.229.refs_0_), channel_id=1, source_target_pairs={{0,24},{1,17},{2,26},{3,19},{4,28},{5,21},{6,30},{7,23},{8,16},{9,... | collective-permute-start | bytes 76808 | tf_op jit(solution)/shard_map/ppermute | solution.py:85
  10.5 1.3 %collective-permute-start.2 = (bf16[2,4,1600]{2,1,0:T(4,128)(2,1)S(1)}, bf16[2,4,1600]{2,1,0:T(4,128)(2,1)S(1)}, u32[]{:S(2)}, u32[]{:S(2)}) collective-permute-start(bf16[2,4,1600]{2,1,0:T(4,128)(2,1)S(1)} %collective-permute-done.1.refs_1_), channel_id=1, source_target_pairs={{1,0},{3,2},{5,4},{7,6},{9,8},{11,10},{13,12},{15,14},{17,16},{19,... | collective-permute-start | bytes 76808 | tf_op jit(solution)/shard_map/ppermute | solution.py:88
  11.8 0.5 %collective-permute-done.3.refs_3_ = bf16[2,4,1600]{2,1,0:T(4,128)(2,1)S(1)} collective-permute-done((bf16[2,4,1600]{2,1,0:T(4,128)(2,1)S(1)}, bf16[2,4,1600]{2,1,0:T(4,128)(2,1)S(1)}, u32[]{:S(2)}, u32[]{:S(2)}) %collective-permute-start.3) | collective-permute-done | bytes 25632 | tf_op jit(solution)/shard_map/ppermute | solution.py:85
  12.3 0.9 %collective-permute-start.4 = (bf16[2,4,1600]{2,1,0:T(4,128)(2,1)S(1)}, bf16[2,4,1600]{2,1,0:T(4,128)(2,1)S(1)}, u32[]{:S(2)}, u32[]{:S(2)}) collective-permute-start(bf16[2,4,1600]{2,1,0:T(4,128)(2,1)S(1)} %collective-permute-done.3.refs_3_), channel_id=1, source_target_pairs={{0,1},{1,0},{2,3},{3,2},{4,5},{5,4},{6,7},{7,6},{8,9},{9,8},{10,11... | collective-permute-start | bytes 76808 | tf_op jit(solution)/shard_map/ppermute | solution.py:89
  13.2 0.4 %collective-permute-done.2.refs_2_ = bf16[2,4,1600]{2,1,0:T(4,128)(2,1)S(1)} collective-permute-done((bf16[2,4,1600]{2,1,0:T(4,128)(2,1)S(1)}, bf16[2,4,1600]{2,1,0:T(4,128)(2,1)S(1)}, u32[]{:S(2)}, u32[]{:S(2)}) %collective-permute-start.2) | collective-permute-done | bytes 25632 | tf_op jit(solution)/shard_map/ppermute | solution.py:88
  13.6 0.5 %collective-permute-done.4.refs_4_ = bf16[2,4,1600]{2,1,0:T(4,128)(2,1)S(1)} collective-permute-done((bf16[2,4,1600]{2,1,0:T(4,128)(2,1)S(1)}, bf16[2,4,1600]{2,1,0:T(4,128)(2,1)S(1)}, u32[]{:S(2)}, u32[]{:S(2)}) %collective-permute-start.4) | collective-permute-done | bytes 25632 | tf_op jit(solution)/shard_map/ppermute | solution.py:89
  14.1 0.0 copy-start.5
  14.1 0.0 copy-start.6
  14.1 0.0 copy-start.9
  14.1 1.7 %shard_map.230 = (f32[4,1252]{1,0:T(4,128)S(1)}, f32[4,132]{1,0:T(4,128)S(1)}, f32[4,400]{1,0:T(4,128)S(1)}, bf16[8,1600]{1,0:T(8,128)(2,1)S(1)}, f32[4,400]{1,0:T(4,128)S(1)}, /*index=5*/f32[4,400]{1,0:T(4,128)S(1)}) custom-call(bf16[2,4,1600]{2,1,0:T(4,128)(2,1)S(1)} %shard_map.229.refs_0_, bf16[2,4,1600]{2,1,0:T(4,128)(2,1)S(1)} %collective-permute-done.1.refs_1_, ...), custom_call_target="tpu_custom_call" | custom-call | tf_op jit(solution)/shard_map/pallas_call | solution.py:436
  15.8 1.6 %collective-permute-start.6 = (f32[4,1252]{1,0:T(4,128)S(1)}, f32[4,1252]{1,0:T(4,128)S(1)}, u32[]{:S(2)}, u32[]{:S(2)}) collective-permute-start(f32[4,1252]{1,0:T(4,128)S(1)} %get-tuple-element.31.refs_0_), channel_id=1, source_target_pairs={{0,2},{1,3},{2,0},{3,1},{4,6},{5,7},{6,4},{7,5},{8,10},{9,11},{10,... | collective-permute-start | bytes 60104 | tf_op jit(solution)/shard_map/ppermute | solution.py:50
  17.4 0.1 collective-permute-start.10
  17.5 0.6 %collective-permute-start.11 = (f32[4,132]{1,0:T(4,128)S(1)}, f32[4,132]{1,0:T(4,128)S(1)}, u32[]{:S(2)}, u32[]{:S(2)}) collective-permute-start(f32[4,132]{1,0:T(4,128)S(1)} %get-tuple-element.35.refs_2_), channel_id=1, source_target_pairs={{0,3},{1,2},{2,1},{3,0},{4,7},{5,6},{6,5},{7,4},{8,11},{9,10},{10,... | collective-permute-start | bytes 6344 | tf_op jit(solution)/shard_map/ppermute | solution.py:50
  18.1 1.6 %collective-permute-done.6.refs_1_ = f32[4,1252]{1,0:T(4,128)S(1)} collective-permute-done((f32[4,1252]{1,0:T(4,128)S(1)}, f32[4,1252]{1,0:T(4,128)S(1)}, u32[]{:S(2)}, u32[]{:S(2)}) %collective-permute-start.6) | collective-permute-done | bytes 20064 | tf_op jit(solution)/shard_map/ppermute | solution.py:50
  19.7 0.8 %shard_map.231 = (bf16[4,1792]{1,0:T(4,128)(2,1)S(1)}, f32[4,640]{1,0:T(4,128)S(1)}) custom-call(f32[4,1252]{1,0:T(4,128)S(1)} %get-tuple-element.31.refs_0_, f32[4,1252]{1,0:T(4,128)S(1)} %collective-permute-done.6.refs_1_, f32[8,256]{1,0:T(8,128)S(1)} %get-tuple-element.32.refs_2_, bf16[4,320,256]{2,1,0:T(8,128)(2,1)S(1)} %bitcast.18, ...), custom_call_target="tpu_custom_call" | custom-call | tf_op jit(solution)/shard_map/pallas_call | solution.py:436
  20.5 0.3 %collective-permute-start.7 = (bf16[4,1792]{1,0:T(4,128)(2,1)S(1)}, bf16[4,1792]{1,0:T(4,128)(2,1)S(1)}, u32[]{:S(2)}, u32[]{:S(2)}) collective-permute-start(bf16[4,1792]{1,0:T(4,128)(2,1)S(1)} %get-tuple-element.33.refs_0_), channel_id=1, source_target_pairs={{0,3},{1,2},{2,1},{3,0},{4,7},{5,6},{6,5},{7,4},{8,11},{9,10},{10,... | collective-permute-start | bytes 43016 | tf_op jit(solution)/shard_map/ppermute | solution.py:50
  20.9 1.3 %collective-permute-start.8 = (bf16[4,1792]{1,0:T(4,128)(2,1)S(1)}, bf16[4,1792]{1,0:T(4,128)(2,1)S(1)}, u32[]{:S(2)}, u32[]{:S(2)}) collective-permute-start(bf16[4,1792]{1,0:T(4,128)(2,1)S(1)} %get-tuple-element.33.refs_0_), channel_id=1, source_target_pairs={{0,2},{1,3},{2,0},{3,1},{4,6},{5,7},{6,4},{7,5},{8,10},{9,11},{10,... | collective-permute-start | bytes 43016 | tf_op jit(solution)/shard_map/ppermute | solution.py:50
  22.2 0.2 collective-permute-start.9
  22.6 1.4 %shard_map.232 = (bf16[4,1600]{1,0:T(4,128)(2,1)S(1)}, f32[4,16,400]{2,1,0:T(8,128)}, bf16[4,640]{1,0:T(4,128)(2,1)}) custom-call(f32[4,640]{1,0:T(4,128)S(1)} %get-tuple-element.34.refs_0_, f32[4,1252]{1,0:T(4,128)S(1)} %collective-permute-done.6.refs_1_, f32[4,132]{1,0:T(4,128)S(1)} %get-tuple-element.35.refs_2_, ...), custom_call_target="tpu_custom_call" | custom-call | tf_op jit(solution)/shard_map/pallas_call | solution.py:436
  24.0 0.6 %collective-permute-done.8.refs_2_ = bf16[4,1792]{1,0:T(4,128)(2,1)S(1)} collective-permute-done((bf16[4,1792]{1,0:T(4,128)(2,1)S(1)}, bf16[4,1792]{1,0:T(4,128)(2,1)S(1)}, u32[]{:S(2)}, u32[]{:S(2)}) %collective-permute-start.8) | collective-permute-done | bytes 14368 | tf_op jit(solution)/shard_map/ppermute | solution.py:50
  24.6 0.9 %shard_map.233 = (f32[4,400]{1,0:T(4,128)S(1)}, bf16[4,1664]{1,0:T(4,128)(2,1)S(1)}) custom-call(bf16[4,1792]{1,0:T(4,128)(2,1)S(1)} %get-tuple-element.33.refs_0_, bf16[4,1792]{1,0:T(4,128)(2,1)S(1)} %collective-permute-done.7.refs_1_, bf16[4,1792]{1,0:T(4,128)(2,1)S(1)} %collective-permute-done.8.refs_2_, ...), custom_call_target="tpu_custom_call" | custom-call | tf_op jit(solution)/shard_map/pallas_call | solution.py:436
  25.4 0.6 %collective-permute-start.12 = (bf16[4,1664]{1,0:T(4,128)(2,1)S(1)}, bf16[4,1664]{1,0:T(4,128)(2,1)S(1)}, u32[]{:S(2)}, u32[]{:S(2)}) collective-permute-start(bf16[4,1664]{1,0:T(4,128)(2,1)S(1)} %get-tuple-element.39.refs_0_), channel_id=1, source_target_pairs={{0,3},{1,2},{2,1},{3,0},{4,7},{5,6},{6,5},{7,4},{8,11},{9,10},{10,... | collective-permute-start | bytes 39944 | tf_op jit(solution)/shard_map/ppermute | solution.py:50
  26.0 1.3 %collective-permute-start.13 = (bf16[4,1664]{1,0:T(4,128)(2,1)S(1)}, bf16[4,1664]{1,0:T(4,128)(2,1)S(1)}, u32[]{:S(2)}, u32[]{:S(2)}) collective-permute-start(bf16[4,1664]{1,0:T(4,128)(2,1)S(1)} %get-tuple-element.39.refs_0_), channel_id=1, source_target_pairs={{0,2},{1,3},{2,0},{3,1},{4,6},{5,7},{6,4},{7,5},{8,10},{9,11},{10,... | collective-permute-start | bytes 39944 | tf_op jit(solution)/shard_map/ppermute | solution.py:50
  27.3 0.0 collective-permute-start.14
  27.3 0.6 %shard_map.235 = bf16[3,4,400]{2,1,0:T(4,128)(2,1)} custom-call(f32[4,400]{1,0:T(4,128)S(1)} %get-tuple-element.43.refs_0_, bf16[3,4,400]{2,1,0:T(4,128)(2,1)S(1)} %get-tuple-element.44.refs_1_), custom_call_target="tpu_custom_call" | custom-call | tf_op jit(solution)/shard_map/pallas_call | solution.py:436
  27.9 0.7 %collective-permute-done.12.refs_1_ = bf16[4,1664]{1,0:T(4,128)(2,1)S(1)} collective-permute-done((bf16[4,1664]{1,0:T(4,128)(2,1)S(1)}, bf16[4,1664]{1,0:T(4,128)(2,1)S(1)}, u32[]{:S(2)}, u32[]{:S(2)}) %collective-permute-start.12) | collective-permute-done | bytes 13344 | tf_op jit(solution)/shard_map/ppermute | solution.py:50
  28.6 1.2 %collective-permute-done.13.refs_2_ = bf16[4,1664]{1,0:T(4,128)(2,1)S(1)} collective-permute-done((bf16[4,1664]{1,0:T(4,128)(2,1)S(1)}, bf16[4,1664]{1,0:T(4,128)(2,1)S(1)}, u32[]{:S(2)}, u32[]{:S(2)}) %collective-permute-start.13) | collective-permute-done | bytes 13344 | tf_op jit(solution)/shard_map/ppermute | solution.py:50
  29.8 0.8 %shard_map.234 = bf16[4,400]{1,0:T(4,128)(2,1)} custom-call(bf16[4,1664]{1,0:T(4,128)(2,1)S(1)} %get-tuple-element.39.refs_0_, bf16[4,1664]{1,0:T(4,128)(2,1)S(1)} %collective-permute-done.12.refs_1_, bf16[4,1664]{1,0:T(4,128)(2,1)S(1)} %collective-permute-done.13.refs_2_, bf16[4,1664]{1,0:T(4,128)(2,1)S(1)} %collective-permute-done.14.refs_3_, ...), custom_call_target="tpu_custom_call" | custom-call | tf_op jit(solution)/shard_map/pallas_call | solution.py:436
  (35 shorter events, 0.1 us)
Async XLA Ops:
  0.6 13.4 %collective-permute-start.5 = (bf16[560,1600]{1,0:T(8,128)(2,1)}, bf16[560,1600]{1,0:T(8,128)(2,1)S(1)}, u32[]{:S(2)}, u32[]{:S(2)}) collective-permute-start(bf16[560,1600]{1,0:T(8,128)(2,1)} %bitcast.27), channel_id=1, source_target_pairs={{0,1},{1,0},{2,3},{3,2},{4,5},{5,4},{6,7},{7,6},{8,9},{9,8},{10,11... | collective-permute-start | bytes 5376008 | tf_op jit(solution)/shard_map/ppermute | solution.py:50
  1.2 4.7 %collective-permute-start = (bf16[1,4,1600]{2,1,0:T(4,128)(2,1)}, bf16[1,4,1600]{2,1,0:T(4,128)(2,1)S(1)}, u32[]{:S(2)}, u32[]{:S(2)}) collective-permute-start(bf16[1,4,1600]{2,1,0:T(4,128)(2,1)} %bitcast.21), channel_id=1, source_target_pairs={{0,4},{4,0},{8,12},{12,8},{16,20},{20,16},{24,28},{28,24},{1,5},{5... | collective-permute-start | bytes 38408 | tf_op jit(solution)/shard_map/ppermute | solution.py:93
  3.7 2.1 %copy-start.8 = (bf16[4,1600]{1,0:T(4,128)(2,1)S(1)}, bf16[4,1600]{1,0:T(4,128)(2,1)}, u32[]{:S(2)}) copy-start(bf16[4,1600]{1,0:T(4,128)(2,1)} %param.21) | copy-start | bytes 38404
  5.9 4.6 %collective-permute-start.1 = (bf16[2,4,1600]{2,1,0:T(4,128)(2,1)S(1)}, bf16[2,4,1600]{2,1,0:T(4,128)(2,1)S(1)}, u32[]{:S(2)}, u32[]{:S(2)}) collective-permute-start(bf16[2,4,1600]{2,1,0:T(4,128)(2,1)S(1)} %shard_map.229.refs_0_), channel_id=1, source_target_pairs={{1,9},{3,11},{5,13},{7,15},{9,1},{11,3},{13,5},{15,7},{17,25},{19,... | collective-permute-start | bytes 76808 | tf_op jit(solution)/shard_map/ppermute | solution.py:85
  6.6 5.8 %collective-permute-start.3 = (bf16[2,4,1600]{2,1,0:T(4,128)(2,1)S(1)}, bf16[2,4,1600]{2,1,0:T(4,128)(2,1)S(1)}, u32[]{:S(2)}, u32[]{:S(2)}) collective-permute-start(bf16[2,4,1600]{2,1,0:T(4,128)(2,1)S(1)} %shard_map.229.refs_0_), channel_id=1, source_target_pairs={{0,24},{1,17},{2,26},{3,19},{4,28},{5,21},{6,30},{7,23},{8,16},{9,... | collective-permute-start | bytes 76808 | tf_op jit(solution)/shard_map/ppermute | solution.py:85
  10.5 3.1 %collective-permute-start.2 = (bf16[2,4,1600]{2,1,0:T(4,128)(2,1)S(1)}, bf16[2,4,1600]{2,1,0:T(4,128)(2,1)S(1)}, u32[]{:S(2)}, u32[]{:S(2)}) collective-permute-start(bf16[2,4,1600]{2,1,0:T(4,128)(2,1)S(1)} %collective-permute-done.1.refs_1_), channel_id=1, source_target_pairs={{1,0},{3,2},{5,4},{7,6},{9,8},{11,10},{13,12},{15,14},{17,16},{19,... | collective-permute-start | bytes 76808 | tf_op jit(solution)/shard_map/ppermute | solution.py:88
  12.3 1.8 %collective-permute-start.4 = (bf16[2,4,1600]{2,1,0:T(4,128)(2,1)S(1)}, bf16[2,4,1600]{2,1,0:T(4,128)(2,1)S(1)}, u32[]{:S(2)}, u32[]{:S(2)}) collective-permute-start(bf16[2,4,1600]{2,1,0:T(4,128)(2,1)S(1)} %collective-permute-done.3.refs_3_), channel_id=1, source_target_pairs={{0,1},{1,0},{2,3},{3,2},{4,5},{5,4},{6,7},{7,6},{8,9},{9,8},{10,11... | collective-permute-start | bytes 76808 | tf_op jit(solution)/shard_map/ppermute | solution.py:89
  14.1 5.6 %copy-start.3 = (bf16[4,256,320]{1,2,0:T(8,128)(2,1)S(1)}, bf16[4,256,320]{1,2,0:T(8,128)(2,1)}, u32[]{:S(2)}) copy-start(bf16[4,256,320]{1,2,0:T(8,128)(2,1)} %param.24) | copy-start | bytes 1966084
  14.1 5.6 %copy-start.4 = (bf16[4,256,320]{1,2,0:T(8,128)(2,1)S(1)}, bf16[4,256,320]{1,2,0:T(8,128)(2,1)}, u32[]{:S(2)}) copy-start(bf16[4,256,320]{1,2,0:T(8,128)(2,1)} %param.25) | copy-start | bytes 1966084
  14.1 8.4 %copy-start = (bf16[1600,2,400]{0,2,1:T(8,128)(2,1)S(1)}, bf16[1600,2,400]{0,2,1:T(8,128)(2,1)}, u32[]{:S(2)}) copy-start(bf16[1600,2,400]{0,2,1:T(8,128)(2,1)} %param.30) | copy-start | bytes 7680004
  14.1 8.4 %copy-start.5 = (f32[4,16,400]{2,1,0:T(8,128)S(1)}, f32[4,16,400]{2,1,0:T(8,128)}, u32[]{:S(2)}) copy-start(f32[4,16,400]{2,1,0:T(8,128)} %refs_11_.1) | copy-start | bytes 307204
  14.1 8.4 %copy-start.6 = (bf16[100,400]{0,1:T(8,128)(2,1)S(1)}, bf16[100,400]{0,1:T(8,128)(2,1)}, u32[]{:S(2)}) copy-start(bf16[100,400]{0,1:T(8,128)(2,1)} %param.34) | copy-start | bytes 240004
  14.1 8.4 %copy-start.7 = (f32[16,400]{1,0:T(8,128)S(1)}, f32[16,400]{1,0:T(8,128)}, u32[]{:S(2)}) copy-start(f32[16,400]{1,0:T(8,128)} %refs_10_.1) | copy-start | bytes 76804
  14.1 8.4 %copy-start.9 = (f32[400]{0:T(512)S(1)}, f32[400]{0:T(512)}, u32[]{:S(2)}) copy-start(f32[400]{0:T(512)} %param.35) | copy-start | bytes 4804
  14.1 8.4 %copy-start.10 = (f32[400]{0:T(512)S(1)}, f32[400]{0:T(512)}, u32[]{:S(2)}) copy-start(f32[400]{0:T(512)} %param.37) | copy-start | bytes 4804
  15.8 6.7 %copy-start.2 = (bf16[400,1600]{1,0:T(8,128)(2,1)S(1)}, bf16[400,1600]{1,0:T(8,128)(2,1)}, u32[]{:S(2)}) copy-start(bf16[400,1600]{1,0:T(8,128)(2,1)} %refs_13_.1) | copy-start | bytes 3840004
  15.8 3.9 %collective-permute-start.6 = (f32[4,1252]{1,0:T(4,128)S(1)}, f32[4,1252]{1,0:T(4,128)S(1)}, u32[]{:S(2)}, u32[]{:S(2)}) collective-permute-start(f32[4,1252]{1,0:T(4,128)S(1)} %get-tuple-element.31.refs_0_), channel_id=1, source_target_pairs={{0,2},{1,3},{2,0},{3,1},{4,6},{5,7},{6,4},{7,5},{8,10},{9,11},{10,... | collective-permute-start | bytes 60104 | tf_op jit(solution)/shard_map/ppermute | solution.py:50
  17.4 5.1 %collective-permute-start.10 = (f32[4,132]{1,0:T(4,128)S(1)}, f32[4,132]{1,0:T(4,128)S(1)}, u32[]{:S(2)}, u32[]{:S(2)}) collective-permute-start(f32[4,132]{1,0:T(4,128)S(1)} %get-tuple-element.35.refs_2_), channel_id=1, source_target_pairs={{0,1},{1,0},{2,3},{3,2},{4,5},{5,4},{6,7},{7,6},{8,9},{9,8},{10,11... | collective-permute-start | bytes 6344 | tf_op jit(solution)/shard_map/ppermute | solution.py:50
  17.5 5.0 %collective-permute-start.11 = (f32[4,132]{1,0:T(4,128)S(1)}, f32[4,132]{1,0:T(4,128)S(1)}, u32[]{:S(2)}, u32[]{:S(2)}) collective-permute-start(f32[4,132]{1,0:T(4,128)S(1)} %get-tuple-element.35.refs_2_), channel_id=1, source_target_pairs={{0,3},{1,2},{2,1},{3,0},{4,7},{5,6},{6,5},{7,4},{8,11},{9,10},{10,... | collective-permute-start | bytes 6344 | tf_op jit(solution)/shard_map/ppermute | solution.py:50
  20.5 3.5 %collective-permute-start.7 = (bf16[4,1792]{1,0:T(4,128)(2,1)S(1)}, bf16[4,1792]{1,0:T(4,128)(2,1)S(1)}, u32[]{:S(2)}, u32[]{:S(2)}) collective-permute-start(bf16[4,1792]{1,0:T(4,128)(2,1)S(1)} %get-tuple-element.33.refs_0_), channel_id=1, source_target_pairs={{0,3},{1,2},{2,1},{3,0},{4,7},{5,6},{6,5},{7,4},{8,11},{9,10},{10,... | collective-permute-start | bytes 43016 | tf_op jit(solution)/shard_map/ppermute | solution.py:50
  20.9 3.7 %collective-permute-start.8 = (bf16[4,1792]{1,0:T(4,128)(2,1)S(1)}, bf16[4,1792]{1,0:T(4,128)(2,1)S(1)}, u32[]{:S(2)}, u32[]{:S(2)}) collective-permute-start(bf16[4,1792]{1,0:T(4,128)(2,1)S(1)} %get-tuple-element.33.refs_0_), channel_id=1, source_target_pairs={{0,2},{1,3},{2,0},{3,1},{4,6},{5,7},{6,4},{7,5},{8,10},{9,11},{10,... | collective-permute-start | bytes 43016 | tf_op jit(solution)/shard_map/ppermute | solution.py:50
  22.2 2.4 %collective-permute-start.9 = (bf16[4,1792]{1,0:T(4,128)(2,1)S(1)}, bf16[4,1792]{1,0:T(4,128)(2,1)S(1)}, u32[]{:S(2)}, u32[]{:S(2)}) collective-permute-start(bf16[4,1792]{1,0:T(4,128)(2,1)S(1)} %get-tuple-element.33.refs_0_), channel_id=1, source_target_pairs={{0,1},{1,0},{2,3},{3,2},{4,5},{5,4},{6,7},{7,6},{8,9},{9,8},{10,11... | collective-permute-start | bytes 43016 | tf_op jit(solution)/shard_map/ppermute | solution.py:50
  22.5 2.0 %copy-start.1 = (bf16[1600,400]{0,1:T(8,128)(2,1)S(1)}, bf16[1600,400]{0,1:T(8,128)(2,1)}, u32[]{:S(2)}) copy-start(bf16[1600,400]{0,1:T(8,128)(2,1)} %param.38) | copy-start | bytes 3840004
  22.6 7.2 %copy-start.11 = (f32[400]{0:T(512)S(1)}, f32[400]{0:T(512)}, u32[]{:S(2)}) copy-start(f32[400]{0:T(512)} %param.40) | copy-start | bytes 4804
  22.6 7.2 %copy-start.12 = (f32[400]{0:T(512)S(1)}, f32[400]{0:T(512)}, u32[]{:S(2)}) copy-start(f32[400]{0:T(512)} %param.41) | copy-start | bytes 4804
  25.4 3.2 %collective-permute-start.12 = (bf16[4,1664]{1,0:T(4,128)(2,1)S(1)}, bf16[4,1664]{1,0:T(4,128)(2,1)S(1)}, u32[]{:S(2)}, u32[]{:S(2)}) collective-permute-start(bf16[4,1664]{1,0:T(4,128)(2,1)S(1)} %get-tuple-element.39.refs_0_), channel_id=1, source_target_pairs={{0,3},{1,2},{2,1},{3,0},{4,7},{5,6},{6,5},{7,4},{8,11},{9,10},{10,... | collective-permute-start | bytes 39944 | tf_op jit(solution)/shard_map/ppermute | solution.py:50
  26.0 3.8 %collective-permute-start.13 = (bf16[4,1664]{1,0:T(4,128)(2,1)S(1)}, bf16[4,1664]{1,0:T(4,128)(2,1)S(1)}, u32[]{:S(2)}, u32[]{:S(2)}) collective-permute-start(bf16[4,1664]{1,0:T(4,128)(2,1)S(1)} %get-tuple-element.39.refs_0_), channel_id=1, source_target_pairs={{0,2},{1,3},{2,0},{3,1},{4,6},{5,7},{6,4},{7,5},{8,10},{9,11},{10,... | collective-permute-start | bytes 39944 | tf_op jit(solution)/shard_map/ppermute | solution.py:50
  27.3 2.5 %collective-permute-start.14 = (bf16[4,1664]{1,0:T(4,128)(2,1)S(1)}, bf16[4,1664]{1,0:T(4,128)(2,1)S(1)}, u32[]{:S(2)}, u32[]{:S(2)}) collective-permute-start(bf16[4,1664]{1,0:T(4,128)(2,1)S(1)} %get-tuple-element.39.refs_0_), channel_id=1, source_target_pairs={{0,1},{1,0},{2,3},{3,2},{4,5},{5,4},{6,7},{7,6},{8,9},{9,8},{10,11... | collective-permute-start | bytes 39944 | tf_op jit(solution)/shard_map/ppermute | solution.py:50

commit v7 on v6

--- a/solution.py
+++ b/solution.py
@@ -194,15 +194,13 @@
 def project_in(*refs, size):
     arrived_refs = refs[:size]
     (other_w_ref, chosen_ref, base_ref, gain_ref, heads_w_ref, xproj_ref, in_w_ref, part_ref,
-     state_ref, act_ref, normed_ref, channel_ref, cols_ref, blocks) = refs[size:]
-    rows, cols = cols_ref.shape
+     state_ref, act_ref, normed_ref, channel_ref, routed_ref) = refs[size:]
+    rows = act_ref.shape[0]
     arrived = jnp.concatenate(
         [ref[i].astype(F32) for ref in arrived_refs for i in range(ref.shape[0])], axis=0
     ).astype(BF16)
     routed = jnp.dot(chosen_ref[...].astype(BF16), arrived, preferred_element_type=F32)
-    for block in range(blocks.shape[0]):
-        blocks[block] = routed[:rows, block * cols : (block + 1) * cols]
-    cols_ref[...] = blocks[lax.axis_index("narrow")]
+    routed_ref[...] = routed
     scale = lax.rsqrt(jnp.mean(routed * routed, axis=1, keepdims=True) + EPSILON)
     normed = (routed * scale * gain_ref[...]).astype(BF16)
     normed_ref[...] = normed
@@ -219,20 +217,26 @@
     part_ref[...] = jnp.concatenate([*heads, state], axis=1)
 
 
-def keep_conv(channel_ref, old_conv_ref, new_conv_ref):
+def keep(
+    channel_ref, old_conv_ref, kv_ref, ssm_ref, routed_ref, new_conv_ref, new_kv_ref, new_ssm_ref,
+    cols_ref, blocks,
+):
+    rows, cols = cols_ref.shape
+    for block in range(blocks.shape[0]):
+        blocks[block] = routed_ref[:rows, block * cols : (block + 1) * cols]
+    cols_ref[...] = blocks[lax.axis_index("narrow")]
+    new_kv_ref[...] = kv_ref[...].astype(BF16)
+    new_ssm_ref[...] = ssm_ref[...]
     taps = new_conv_ref.shape[0]
     for tap in range(taps - 1):
         new_conv_ref[tap] = old_conv_ref[tap]
     new_conv_ref[taps - 1] = channel_ref[...].astype(BF16)
 
 
-def state_step(
-    kv_ref, far_ref, *refs, size,
-):
+def state_step(far_ref, *refs, size):
     states = refs[: size - 1]
     (normed_ref, gate_w_ref, act_ref, dt_w_ref, dt_b_ref, a_log_ref, ssm_ref, skip_ref, out_w_ref,
-     part_ref, new_ssm_ref, new_kv_ref) = refs[size - 1 :]
-    new_kv_ref[...] = kv_ref[...].astype(BF16)
+     part_ref, new_ssm_ref) = refs[size - 1 :]
     state = far_ref[:, far_ref.shape[1] - states[0].shape[1] :]
     for other in states:
         state = state + other[...]
@@ -387,9 +391,10 @@
     factors = jnp.concatenate([f / total for f in factors], axis=0)
     high = factors.astype(BF16)
     low = (factors - high.astype(F32)).astype(BF16)
-    spread = jnp.dot(high, spread_ref[...], preferred_element_type=F32) + jnp.dot(
-        low, spread_ref[...], preferred_element_type=F32
-    )
+    both = jnp.dot(
+        jnp.concatenate([high, low], axis=0), spread_ref[...], preferred_element_type=F32
+    )
+    spread = both[: high.shape[0]] + both[high.shape[0] :]
     merged = functools.reduce(
         jnp.add,
         [spread[i * rows : (i + 1) * rows] * p[:, :QUERY_WIDTH].astype(F32) for i, p in enumerate(pieces)],
@@ -504,7 +509,7 @@
     other_w = swap(large[0], 1)
     part_width = 2 * head_width + w_xproj.shape[1]
     chosen, live, base, old_conv, *weights = prepared
-    part, state, act, normed, channel_in, routed_cols = call(
+    part, state, act, normed, channel_in, routed = call(
         functools.partial(project_in, size=len(arrived)),
         (),
         (*arrived, other_w, chosen, base, *weights),
@@ -514,9 +519,8 @@
             shape((rows, cols), F32),
             shape((8, MODEL_WIDTH), BF16),
             shape((rows, cols), F32),
-            shape((rows, cols), F32),
+            shape((8, MODEL_WIDTH), F32),
         ),
-        (pltpu.VMEM((narrow, rows, cols), F32),),
     )
     far = swap(part, 2)
     states = [state, swap(state, 1), swap(state, 3)]
@@ -533,19 +537,17 @@
         ),
         (pltpu.VMEM((narrow, rows, head_width), F32),),
     )
-    state_part, new_ssm, new_kv = call(
+    state_part, fresh_ssm = call(
         functools.partial(state_step, size=narrow),
         (),
         (
-            key_value, far, *states, normed, w_xz.transpose(1, 2, 0), act, w_dt.T, dt_bias[None], a_log, ssm_state, skip_d[None], w_ssm_out,
+            far, *states, normed, w_xz.transpose(1, 2, 0), act, w_dt.T, dt_bias[None], a_log, ssm_state, skip_d[None], w_ssm_out,
         ),
         (
             shape((rows, MODEL_WIDTH), BF16),
             shape(ssm_state.shape, F32),
-            shape(key_value.shape, BF16),
         ),
     )
-    (new_conv,) = call(keep_conv, (), (channel_in, old_conv), (shape(old_conv.shape, BF16),))
     pieces = exchange(second, (3, 2, 1))
     spread = (
         lax.broadcasted_iota(jnp.int32, (QUERY_HEADS, QUERY_WIDTH), 1) // HEAD_SIZE
@@ -558,6 +560,19 @@
         (shape((rows, cols), F32), shape((rows, MODEL_WIDTH + 64), BF16)),
     )
     pieces = exchange(third, (3, 2, 1))
+    new_conv, new_kv, new_ssm, routed_cols = call(
+        keep,
+        (),
+        (channel_in, old_conv, key_value, fresh_ssm, routed),
+        (
+            shape(old_conv.shape, BF16),
+            shape(key_value.shape, BF16),
+            shape(ssm_state.shape, F32),
+            shape((rows, cols), F32),
+        ),
+        (pltpu.VMEM((narrow, rows, cols), F32),),
+        after=(third,),
+    )
     (out,) = call(
         functools.partial(finish, size=narrow),
         (),

time: 30.7 us -> 30.7 us (level)
  Pallas kernels: 8.2 us -> 7.81 us
  waiting for transfers between devices: 5.49 us -> 5.86 us
    pallas_call x7, Pallas kernels: 6.11 us -> 5.72 us  [call(): pl.pallas_call(run, in_specs=[pl.BlockSpec(memory_space=pl.ANY)] * len(af...]
    ppermute x10, waiting for transfers between devices: 4.1 us -> 4.47 us  [swap(): return lax.ppermute(part, 'narrow', [(i, i ^ step) for i in range(size)])]
  transfers between devices with their start and end apart: 15 -> 15, of which waited for: 7 -> 8; matrix products, arithmetic and copies ran while one was open for 0% -> 0% of each run, Pallas kernels for 16% -> 15%
where the time goes in v7:
time: 30.7 us; the launch traced here: 30.5 us
  starting transfers between devices  15.9 us (52%)
  Pallas kernels  7.81 us (25%)
  waiting for transfers between devices  5.86 us (19%)
  between operations  0.85 us (3%)
    ppermute x10, starting transfers between devices, swap(): return lax.ppermute(part, 'narrow', [(i, i ^ step) for i in range(size)])  6.5 us
    pallas_call x7, Pallas kernels, call(): pl.pallas_call(run, in_specs=[pl.BlockSpec(memory_space=pl.ANY)] * len(af...  5.72 us
    ppermute x2, starting transfers between devices, fetch(): return lax.ppermute(held, (axis, core_axis), moves)  4.59 us
    ppermute x10, waiting for transfers between devices, swap(): return lax.ppermute(part, 'narrow', [(i, i ^ step) for i in range(size)])  4.47 us
    ppermute x1, starting transfers between devices, gather_xor(): lax.ppermute(held, axis, [(i, i ^ step << place) for i in range(size)])  2.59 us
    pallas_call x1, Pallas kernels, shards(): pl.pallas_call(functools.partial(prepare, size=wide), in_specs=[anywhere]...  2.09 us
    ppermute x1, starting transfers between devices, gather_xor(): lax.ppermute(near, core_axis, [(c, c - 1) for c in range(1, cores, 2)])  1.28 us
    ppermute x1, starting transfers between devices, gather_xor(): far_swap = lax.ppermute(far, core_axis, [(c, c ^ 1) for c in range(cores)])  0.9 us
  transfers between devices with their start and end apart: 15, of which 8 were waited for; matrix products, arithmetic and copies ran while one was open for 0% of the time, Pallas kernels for 15%

profile of v7, /device:TPU:0, one launch (start us, length us, event | category | flops | bytes accessed | tf_op | source)
XLA Modules:
  0.0 30.5 jit_solution(1938556886047041825)
XLA Ops:
  0.6 0.5 %collective-permute-start.5 = (bf16[560,1600]{1,0:T(8,128)(2,1)}, bf16[560,1600]{1,0:T(8,128)(2,1)S(1)}, u32[]{:S(2)}, u32[]{:S(2)}) collective-permute-start(bf16[560,1600]{1,0:T(8,128)(2,1)} %bitcast.27), channel_id=1, source_target_pairs={{0,1},{1,0},{2,3},{3,2},{4,5},{5,4},{6,7},{7,6},{8,9},{9,8},{10,11... | collective-permute-start | bytes 5376008 | tf_op jit(solution)/shard_map/ppermute | solution.py:50
  1.2 2.6 %collective-permute-start = (bf16[1,4,1600]{2,1,0:T(4,128)(2,1)}, bf16[1,4,1600]{2,1,0:T(4,128)(2,1)S(1)}, u32[]{:S(2)}, u32[]{:S(2)}) collective-permute-start(bf16[1,4,1600]{2,1,0:T(4,128)(2,1)} %bitcast.21), channel_id=1, source_target_pairs={{0,4},{4,0},{8,12},{12,8},{16,20},{20,16},{24,28},{28,24},{1,5},{5... | collective-permute-start | bytes 38408 | tf_op jit(solution)/shard_map/ppermute | solution.py:93
  3.7 2.1 %shard_map.228 = (f32[8,40]{1,0:T(8,128)S(1)}, f32[8,256]{1,0:T(8,128)S(1)}, f32[8,400]{1,0:T(8,128)S(1)}, bf16[3,4,400]{2,1,0:T(4,128)(2,1)S(1)}, f32[1,1600]{1...) custom-call(s32[4]{0:T(128)} %source_ref.1, ...), custom_call_target="tpu_custom_call" | custom-call | tf_op jit(solution)/shard_map/pallas_call | solution.py:489
  5.9 0.7 %collective-permute-start.1 = (bf16[2,4,1600]{2,1,0:T(4,128)(2,1)S(1)}, bf16[2,4,1600]{2,1,0:T(4,128)(2,1)S(1)}, u32[]{:S(2)}, u32[]{:S(2)}) collective-permute-start(bf16[2,4,1600]{2,1,0:T(4,128)(2,1)S(1)} %shard_map.229.refs_0_), channel_id=1, source_target_pairs={{1,9},{3,11},{5,13},{7,15},{9,1},{11,3},{13,5},{15,7},{17,25},{19,... | collective-permute-start | bytes 76808 | tf_op jit(solution)/shard_map/ppermute | solution.py:85
  6.6 3.9 %collective-permute-start.3 = (bf16[2,4,1600]{2,1,0:T(4,128)(2,1)S(1)}, bf16[2,4,1600]{2,1,0:T(4,128)(2,1)S(1)}, u32[]{:S(2)}, u32[]{:S(2)}) collective-permute-start(bf16[2,4,1600]{2,1,0:T(4,128)(2,1)S(1)} %shard_map.229.refs_0_), channel_id=1, source_target_pairs={{0,24},{1,17},{2,26},{3,19},{4,28},{5,21},{6,30},{7,23},{8,16},{9,... | collective-permute-start | bytes 76808 | tf_op jit(solution)/shard_map/ppermute | solution.py:85
  10.5 1.3 %collective-permute-start.2 = (bf16[2,4,1600]{2,1,0:T(4,128)(2,1)S(1)}, bf16[2,4,1600]{2,1,0:T(4,128)(2,1)S(1)}, u32[]{:S(2)}, u32[]{:S(2)}) collective-permute-start(bf16[2,4,1600]{2,1,0:T(4,128)(2,1)S(1)} %collective-permute-done.1.refs_1_), channel_id=1, source_target_pairs={{1,0},{3,2},{5,4},{7,6},{9,8},{11,10},{13,12},{15,14},{17,16},{19,... | collective-permute-start | bytes 76808 | tf_op jit(solution)/shard_map/ppermute | solution.py:88
  11.8 0.5 %collective-permute-done.3.refs_3_ = bf16[2,4,1600]{2,1,0:T(4,128)(2,1)S(1)} collective-permute-done((bf16[2,4,1600]{2,1,0:T(4,128)(2,1)S(1)}, bf16[2,4,1600]{2,1,0:T(4,128)(2,1)S(1)}, u32[]{:S(2)}, u32[]{:S(2)}) %collective-permute-start.3) | collective-permute-done | bytes 25632 | tf_op jit(solution)/shard_map/ppermute | solution.py:85
  12.3 0.9 %collective-permute-start.4 = (bf16[2,4,1600]{2,1,0:T(4,128)(2,1)S(1)}, bf16[2,4,1600]{2,1,0:T(4,128)(2,1)S(1)}, u32[]{:S(2)}, u32[]{:S(2)}) collective-permute-start(bf16[2,4,1600]{2,1,0:T(4,128)(2,1)S(1)} %collective-permute-done.3.refs_3_), channel_id=1, source_target_pairs={{0,1},{1,0},{2,3},{3,2},{4,5},{5,4},{6,7},{7,6},{8,9},{9,8},{10,11... | collective-permute-start | bytes 76808 | tf_op jit(solution)/shard_map/ppermute | solution.py:89
  13.2 0.4 %collective-permute-done.2.refs_2_ = bf16[2,4,1600]{2,1,0:T(4,128)(2,1)S(1)} collective-permute-done((bf16[2,4,1600]{2,1,0:T(4,128)(2,1)S(1)}, bf16[2,4,1600]{2,1,0:T(4,128)(2,1)S(1)}, u32[]{:S(2)}, u32[]{:S(2)}) %collective-permute-start.2) | collective-permute-done | bytes 25632 | tf_op jit(solution)/shard_map/ppermute | solution.py:88
  13.6 0.5 %collective-permute-done.4.refs_4_ = bf16[2,4,1600]{2,1,0:T(4,128)(2,1)S(1)} collective-permute-done((bf16[2,4,1600]{2,1,0:T(4,128)(2,1)S(1)}, bf16[2,4,1600]{2,1,0:T(4,128)(2,1)S(1)}, u32[]{:S(2)}, u32[]{:S(2)}) %collective-permute-start.4) | collective-permute-done | bytes 25632 | tf_op jit(solution)/shard_map/ppermute | solution.py:89
  14.1 0.0 copy-start.5
  14.1 0.0 copy-start.7
  14.1 1.7 %shard_map.230 = (f32[4,1252]{1,0:T(4,128)S(1)}, f32[4,132]{1,0:T(4,128)S(1)}, f32[4,400]{1,0:T(4,128)S(1)}, bf16[8,1600]{1,0:T(8,128)(2,1)S(1)}, f32[4,400]{1,0:T(4,128)S(1)}, /*index=5*/f32[8,1600]{1,0:T(8,128)S(1)}) custom-call(bf16[2,4,1600]{2,1,0:T(4,128)(2,1)S(1)} %shard_map.229.refs_0_, bf16[2,4,1600]{2,1,0:T(4,128)(2,1)S(1)} %collective-permute-done.1.refs_1_, ...), custom_call_target="tpu_custom_call" | custom-call | tf_op jit(solution)/shard_map/pallas_call | solution.py:441
  15.9 1.5 %collective-permute-start.6 = (f32[4,1252]{1,0:T(4,128)S(1)}, f32[4,1252]{1,0:T(4,128)S(1)}, u32[]{:S(2)}, u32[]{:S(2)}) collective-permute-start(f32[4,1252]{1,0:T(4,128)S(1)} %get-tuple-element.34.refs_0_), channel_id=1, source_target_pairs={{0,2},{1,3},{2,0},{3,1},{4,6},{5,7},{6,4},{7,5},{8,10},{9,11},{10,... | collective-permute-start | bytes 60104 | tf_op jit(solution)/shard_map/ppermute | solution.py:50
  17.4 0.1 collective-permute-start.10
  17.5 0.6 %collective-permute-start.11 = (f32[4,132]{1,0:T(4,128)S(1)}, f32[4,132]{1,0:T(4,128)S(1)}, u32[]{:S(2)}, u32[]{:S(2)}) collective-permute-start(f32[4,132]{1,0:T(4,128)S(1)} %get-tuple-element.37.refs_1_), channel_id=1, source_target_pairs={{0,3},{1,2},{2,1},{3,0},{4,7},{5,6},{6,5},{7,4},{8,11},{9,10},{10,... | collective-permute-start | bytes 6344 | tf_op jit(solution)/shard_map/ppermute | solution.py:50
  18.1 1.6 %collective-permute-done.6.refs_1_.refs_0_ = f32[4,1252]{1,0:T(4,128)S(1)} collective-permute-done((f32[4,1252]{1,0:T(4,128)S(1)}, f32[4,1252]{1,0:T(4,128)S(1)}, u32[]{:S(2)}, u32[]{:S(2)}) %collective-permute-start.6) | collective-permute-done | bytes 20064 | tf_op jit(solution)/shard_map/ppermute | solution.py:50
  19.7 0.8 %shard_map.231 = (bf16[4,1792]{1,0:T(4,128)(2,1)S(1)}, f32[4,640]{1,0:T(4,128)S(1)}) custom-call(f32[4,1252]{1,0:T(4,128)S(1)} %get-tuple-element.34.refs_0_, f32[4,1252]{1,0:T(4,128)S(1)} %collective-permute-done.6.refs_1_.refs_0_, f32[8,256]{1,0:T(8,128)S(1)} %get-tuple-element.35.refs_2_, bf16[4,320,256]{2,1,0:T(8,128)(2,1)S(1)} %bitcast.18, ...), custom_call_target="tpu_custom_call" | custom-call | tf_op jit(solution)/shard_map/pallas_call | solution.py:441
  20.5 0.3 %collective-permute-start.7 = (bf16[4,1792]{1,0:T(4,128)(2,1)S(1)}, bf16[4,1792]{1,0:T(4,128)(2,1)S(1)}, u32[]{:S(2)}, u32[]{:S(2)}) collective-permute-start(bf16[4,1792]{1,0:T(4,128)(2,1)S(1)} %get-tuple-element.36.refs_0_), channel_id=1, source_target_pairs={{0,3},{1,2},{2,1},{3,0},{4,7},{5,6},{6,5},{7,4},{8,11},{9,10},{10,... | collective-permute-start | bytes 43016 | tf_op jit(solution)/shard_map/ppermute | solution.py:50
  20.9 1.3 %collective-permute-start.8 = (bf16[4,1792]{1,0:T(4,128)(2,1)S(1)}, bf16[4,1792]{1,0:T(4,128)(2,1)S(1)}, u32[]{:S(2)}, u32[]{:S(2)}) collective-permute-start(bf16[4,1792]{1,0:T(4,128)(2,1)S(1)} %get-tuple-element.36.refs_0_), channel_id=1, source_target_pairs={{0,2},{1,3},{2,0},{3,1},{4,6},{5,7},{6,4},{7,5},{8,10},{9,11},{10,... | collective-permute-start | bytes 43016 | tf_op jit(solution)/shard_map/ppermute | solution.py:50
  22.2 0.2 collective-permute-start.9
  22.6 0.9 %shard_map.232 = (bf16[4,1600]{1,0:T(4,128)(2,1)S(1)}, f32[4,16,400]{2,1,0:T(8,128)S(1)}) custom-call(f32[4,1252]{1,0:T(4,128)S(1)} %collective-permute-done.6.refs_1_.refs_0_, f32[4,132]{1,0:T(4,128)S(1)} %get-tuple-element.37.refs_1_, f32[4,132]{1,0:T(4,128)S(1)} %collective-permute-done.10.refs_2_, f32[4,132]{1,0:T(4,128)S(1)} %collective-permute-done.11.refs_3_, ...), custom_call_target="tpu_custom_call" | custom-call | tf_op jit(solution)/shard_map/pallas_call | solution.py:441
  23.5 0.3 collective-permute-done.7.refs_1_
  23.8 0.8 %collective-permute-done.8.refs_2_ = bf16[4,1792]{1,0:T(4,128)(2,1)S(1)} collective-permute-done((bf16[4,1792]{1,0:T(4,128)(2,1)S(1)}, bf16[4,1792]{1,0:T(4,128)(2,1)S(1)}, u32[]{:S(2)}, u32[]{:S(2)}) %collective-permute-start.8) | collective-permute-done | bytes 14368 | tf_op jit(solution)/shard_map/ppermute | solution.py:50
  24.6 0.9 %shard_map.233 = (f32[4,400]{1,0:T(4,128)S(1)}, bf16[4,1664]{1,0:T(4,128)(2,1)S(1)}) custom-call(bf16[4,1792]{1,0:T(4,128)(2,1)S(1)} %get-tuple-element.36.refs_0_, bf16[4,1792]{1,0:T(4,128)(2,1)S(1)} %collective-permute-done.7.refs_1_, bf16[4,1792]{1,0:T(4,128)(2,1)S(1)} %collective-permute-done.8.refs_2_, ...), custom_call_target="tpu_custom_call" | custom-call | tf_op jit(solution)/shard_map/pallas_call | solution.py:441
  25.4 0.5 %collective-permute-start.12 = (bf16[4,1664]{1,0:T(4,128)(2,1)S(1)}, bf16[4,1664]{1,0:T(4,128)(2,1)S(1)}, u32[]{:S(2)}, u32[]{:S(2)}) collective-permute-start(bf16[4,1664]{1,0:T(4,128)(2,1)S(1)} %get-tuple-element.41.refs_0_), channel_id=1, source_target_pairs={{0,3},{1,2},{2,1},{3,0},{4,7},{5,6},{6,5},{7,4},{8,11},{9,10},{10,... | collective-permute-start | bytes 39944 | tf_op jit(solution)/shard_map/ppermute | solution.py:50
  25.9 1.4 %collective-permute-start.13 = (bf16[4,1664]{1,0:T(4,128)(2,1)S(1)}, bf16[4,1664]{1,0:T(4,128)(2,1)S(1)}, u32[]{:S(2)}, u32[]{:S(2)}) collective-permute-start(bf16[4,1664]{1,0:T(4,128)(2,1)S(1)} %get-tuple-element.41.refs_0_), channel_id=1, source_target_pairs={{0,2},{1,3},{2,0},{3,1},{4,6},{5,7},{6,4},{7,5},{8,10},{9,11},{10,... | collective-permute-start | bytes 39944 | tf_op jit(solution)/shard_map/ppermute | solution.py:50
  27.3 0.0 collective-permute-start.14
  27.3 0.7 %shard_map.234 = (bf16[3,4,400]{2,1,0:T(4,128)(2,1)}, bf16[4,640]{1,0:T(4,128)(2,1)}, f32[4,16,400]{2,1,0:T(8,128)}, f32[4,400]{1,0:T(4,128)S(1)}) custom-call(bf16[4,1664]{1,0:T(4,128)(2,1)S(1)} %get-tuple-element.41.refs_0_, f32[4,400]{1,0:T(4,128)S(1)} %get-tuple-element.43.refs_1_, bf16[3,4,400]{2,1,0:T(4,128)(2,1)S(1)} %get-tuple-element.44.refs_2_, ...), custom_call_target="tpu_custom_call" | custom-call | tf_op jit(solution)/shard_map/pallas_call | solution.py:441
  28.0 0.6 %collective-permute-done.12.refs_1_ = bf16[4,1664]{1,0:T(4,128)(2,1)S(1)} collective-permute-done((bf16[4,1664]{1,0:T(4,128)(2,1)S(1)}, bf16[4,1664]{1,0:T(4,128)(2,1)S(1)}, u32[]{:S(2)}, u32[]{:S(2)}) %collective-permute-start.12) | collective-permute-done | bytes 13344 | tf_op jit(solution)/shard_map/ppermute | solution.py:50
  28.6 1.1 %collective-permute-done.13.refs_2_ = bf16[4,1664]{1,0:T(4,128)(2,1)S(1)} collective-permute-done((bf16[4,1664]{1,0:T(4,128)(2,1)S(1)}, bf16[4,1664]{1,0:T(4,128)(2,1)S(1)}, u32[]{:S(2)}, u32[]{:S(2)}) %collective-permute-start.13) | collective-permute-done | bytes 13344 | tf_op jit(solution)/shard_map/ppermute | solution.py:50
  29.7 0.8 %shard_map.235 = bf16[4,400]{1,0:T(4,128)(2,1)} custom-call(bf16[4,1664]{1,0:T(4,128)(2,1)S(1)} %get-tuple-element.41.refs_0_, bf16[4,1664]{1,0:T(4,128)(2,1)S(1)} %collective-permute-done.12.refs_1_, bf16[4,1664]{1,0:T(4,128)(2,1)S(1)} %collective-permute-done.13.refs_2_, bf16[4,1664]{1,0:T(4,128)(2,1)S(1)} %collective-permute-done.14.refs_3_, ...), custom_call_target="tpu_custom_call" | custom-call | tf_op jit(solution)/shard_map/pallas_call | solution.py:441
  (35 shorter events, 0.1 us)
Async XLA Ops:
  0.6 13.4 %collective-permute-start.5 = (bf16[560,1600]{1,0:T(8,128)(2,1)}, bf16[560,1600]{1,0:T(8,128)(2,1)S(1)}, u32[]{:S(2)}, u32[]{:S(2)}) collective-permute-start(bf16[560,1600]{1,0:T(8,128)(2,1)} %bitcast.27), channel_id=1, source_target_pairs={{0,1},{1,0},{2,3},{3,2},{4,5},{5,4},{6,7},{7,6},{8,9},{9,8},{10,11... | collective-permute-start | bytes 5376008 | tf_op jit(solution)/shard_map/ppermute | solution.py:50
  1.2 4.7 %collective-permute-start = (bf16[1,4,1600]{2,1,0:T(4,128)(2,1)}, bf16[1,4,1600]{2,1,0:T(4,128)(2,1)S(1)}, u32[]{:S(2)}, u32[]{:S(2)}) collective-permute-start(bf16[1,4,1600]{2,1,0:T(4,128)(2,1)} %bitcast.21), channel_id=1, source_target_pairs={{0,4},{4,0},{8,12},{12,8},{16,20},{20,16},{24,28},{28,24},{1,5},{5... | collective-permute-start | bytes 38408 | tf_op jit(solution)/shard_map/ppermute | solution.py:93
  3.7 2.1 %copy-start.8 = (bf16[4,1600]{1,0:T(4,128)(2,1)S(1)}, bf16[4,1600]{1,0:T(4,128)(2,1)}, u32[]{:S(2)}) copy-start(bf16[4,1600]{1,0:T(4,128)(2,1)} %param.21) | copy-start | bytes 38404
  5.9 4.6 %collective-permute-start.1 = (bf16[2,4,1600]{2,1,0:T(4,128)(2,1)S(1)}, bf16[2,4,1600]{2,1,0:T(4,128)(2,1)S(1)}, u32[]{:S(2)}, u32[]{:S(2)}) collective-permute-start(bf16[2,4,1600]{2,1,0:T(4,128)(2,1)S(1)} %shard_map.229.refs_0_), channel_id=1, source_target_pairs={{1,9},{3,11},{5,13},{7,15},{9,1},{11,3},{13,5},{15,7},{17,25},{19,... | collective-permute-start | bytes 76808 | tf_op jit(solution)/shard_map/ppermute | solution.py:85
  6.6 5.8 %collective-permute-start.3 = (bf16[2,4,1600]{2,1,0:T(4,128)(2,1)S(1)}, bf16[2,4,1600]{2,1,0:T(4,128)(2,1)S(1)}, u32[]{:S(2)}, u32[]{:S(2)}) collective-permute-start(bf16[2,4,1600]{2,1,0:T(4,128)(2,1)S(1)} %shard_map.229.refs_0_), channel_id=1, source_target_pairs={{0,24},{1,17},{2,26},{3,19},{4,28},{5,21},{6,30},{7,23},{8,16},{9,... | collective-permute-start | bytes 76808 | tf_op jit(solution)/shard_map/ppermute | solution.py:85
  10.5 3.1 %collective-permute-start.2 = (bf16[2,4,1600]{2,1,0:T(4,128)(2,1)S(1)}, bf16[2,4,1600]{2,1,0:T(4,128)(2,1)S(1)}, u32[]{:S(2)}, u32[]{:S(2)}) collective-permute-start(bf16[2,4,1600]{2,1,0:T(4,128)(2,1)S(1)} %collective-permute-done.1.refs_1_), channel_id=1, source_target_pairs={{1,0},{3,2},{5,4},{7,6},{9,8},{11,10},{13,12},{15,14},{17,16},{19,... | collective-permute-start | bytes 76808 | tf_op jit(solution)/shard_map/ppermute | solution.py:88
  12.3 1.8 %collective-permute-start.4 = (bf16[2,4,1600]{2,1,0:T(4,128)(2,1)S(1)}, bf16[2,4,1600]{2,1,0:T(4,128)(2,1)S(1)}, u32[]{:S(2)}, u32[]{:S(2)}) collective-permute-start(bf16[2,4,1600]{2,1,0:T(4,128)(2,1)S(1)} %collective-permute-done.3.refs_3_), channel_id=1, source_target_pairs={{0,1},{1,0},{2,3},{3,2},{4,5},{5,4},{6,7},{7,6},{8,9},{9,8},{10,11... | collective-permute-start | bytes 76808 | tf_op jit(solution)/shard_map/ppermute | solution.py:89
  14.1 5.6 %copy-start.3 = (bf16[4,256,320]{1,2,0:T(8,128)(2,1)S(1)}, bf16[4,256,320]{1,2,0:T(8,128)(2,1)}, u32[]{:S(2)}) copy-start(bf16[4,256,320]{1,2,0:T(8,128)(2,1)} %param.24) | copy-start | bytes 1966084
  14.1 5.6 %copy-start.4 = (bf16[4,256,320]{1,2,0:T(8,128)(2,1)S(1)}, bf16[4,256,320]{1,2,0:T(8,128)(2,1)}, u32[]{:S(2)}) copy-start(bf16[4,256,320]{1,2,0:T(8,128)(2,1)} %param.25) | copy-start | bytes 1966084
  14.1 8.4 %copy-start = (bf16[1600,2,400]{0,2,1:T(8,128)(2,1)S(1)}, bf16[1600,2,400]{0,2,1:T(8,128)(2,1)}, u32[]{:S(2)}) copy-start(bf16[1600,2,400]{0,2,1:T(8,128)(2,1)} %param.30) | copy-start | bytes 7680004
  14.1 8.4 %copy-start.5 = (f32[4,16,400]{2,1,0:T(8,128)S(1)}, f32[4,16,400]{2,1,0:T(8,128)}, u32[]{:S(2)}) copy-start(f32[4,16,400]{2,1,0:T(8,128)} %refs_10_.1) | copy-start | bytes 307204
  14.1 8.4 %copy-start.6 = (bf16[100,400]{0,1:T(8,128)(2,1)S(1)}, bf16[100,400]{0,1:T(8,128)(2,1)}, u32[]{:S(2)}) copy-start(bf16[100,400]{0,1:T(8,128)(2,1)} %param.34) | copy-start | bytes 240004
  14.1 8.4 %copy-start.7 = (f32[16,400]{1,0:T(8,128)S(1)}, f32[16,400]{1,0:T(8,128)}, u32[]{:S(2)}) copy-start(f32[16,400]{1,0:T(8,128)} %refs_9_.1) | copy-start | bytes 76804
  14.1 8.4 %copy-start.9 = (f32[400]{0:T(512)S(1)}, f32[400]{0:T(512)}, u32[]{:S(2)}) copy-start(f32[400]{0:T(512)} %param.35) | copy-start | bytes 4804
  14.1 8.4 %copy-start.10 = (f32[400]{0:T(512)S(1)}, f32[400]{0:T(512)}, u32[]{:S(2)}) copy-start(f32[400]{0:T(512)} %param.37) | copy-start | bytes 4804
  15.9 6.7 %copy-start.2 = (bf16[400,1600]{1,0:T(8,128)(2,1)S(1)}, bf16[400,1600]{1,0:T(8,128)(2,1)}, u32[]{:S(2)}) copy-start(bf16[400,1600]{1,0:T(8,128)(2,1)} %refs_12_.1) | copy-start | bytes 3840004
  15.9 3.8 %collective-permute-start.6 = (f32[4,1252]{1,0:T(4,128)S(1)}, f32[4,1252]{1,0:T(4,128)S(1)}, u32[]{:S(2)}, u32[]{:S(2)}) collective-permute-start(f32[4,1252]{1,0:T(4,128)S(1)} %get-tuple-element.34.refs_0_), channel_id=1, source_target_pairs={{0,2},{1,3},{2,0},{3,1},{4,6},{5,7},{6,4},{7,5},{8,10},{9,11},{10,... | collective-permute-start | bytes 60104 | tf_op jit(solution)/shard_map/ppermute | solution.py:50
  17.4 5.1 %collective-permute-start.10 = (f32[4,132]{1,0:T(4,128)S(1)}, f32[4,132]{1,0:T(4,128)S(1)}, u32[]{:S(2)}, u32[]{:S(2)}) collective-permute-start(f32[4,132]{1,0:T(4,128)S(1)} %get-tuple-element.37.refs_1_), channel_id=1, source_target_pairs={{0,1},{1,0},{2,3},{3,2},{4,5},{5,4},{6,7},{7,6},{8,9},{9,8},{10,11... | collective-permute-start | bytes 6344 | tf_op jit(solution)/shard_map/ppermute | solution.py:50
  17.5 5.0 %collective-permute-start.11 = (f32[4,132]{1,0:T(4,128)S(1)}, f32[4,132]{1,0:T(4,128)S(1)}, u32[]{:S(2)}, u32[]{:S(2)}) collective-permute-start(f32[4,132]{1,0:T(4,128)S(1)} %get-tuple-element.37.refs_1_), channel_id=1, source_target_pairs={{0,3},{1,2},{2,1},{3,0},{4,7},{5,6},{6,5},{7,4},{8,11},{9,10},{10,... | collective-permute-start | bytes 6344 | tf_op jit(solution)/shard_map/ppermute | solution.py:50
  20.5 3.3 %collective-permute-start.7 = (bf16[4,1792]{1,0:T(4,128)(2,1)S(1)}, bf16[4,1792]{1,0:T(4,128)(2,1)S(1)}, u32[]{:S(2)}, u32[]{:S(2)}) collective-permute-start(bf16[4,1792]{1,0:T(4,128)(2,1)S(1)} %get-tuple-element.36.refs_0_), channel_id=1, source_target_pairs={{0,3},{1,2},{2,1},{3,0},{4,7},{5,6},{6,5},{7,4},{8,11},{9,10},{10,... | collective-permute-start | bytes 43016 | tf_op jit(solution)/shard_map/ppermute | solution.py:50
  20.9 3.7 %collective-permute-start.8 = (bf16[4,1792]{1,0:T(4,128)(2,1)S(1)}, bf16[4,1792]{1,0:T(4,128)(2,1)S(1)}, u32[]{:S(2)}, u32[]{:S(2)}) collective-permute-start(bf16[4,1792]{1,0:T(4,128)(2,1)S(1)} %get-tuple-element.36.refs_0_), channel_id=1, source_target_pairs={{0,2},{1,3},{2,0},{3,1},{4,6},{5,7},{6,4},{7,5},{8,10},{9,11},{10,... | collective-permute-start | bytes 43016 | tf_op jit(solution)/shard_map/ppermute | solution.py:50
  22.2 2.4 %collective-permute-start.9 = (bf16[4,1792]{1,0:T(4,128)(2,1)S(1)}, bf16[4,1792]{1,0:T(4,128)(2,1)S(1)}, u32[]{:S(2)}, u32[]{:S(2)}) collective-permute-start(bf16[4,1792]{1,0:T(4,128)(2,1)S(1)} %get-tuple-element.36.refs_0_), channel_id=1, source_target_pairs={{0,1},{1,0},{2,3},{3,2},{4,5},{5,4},{6,7},{7,6},{8,9},{9,8},{10,11... | collective-permute-start | bytes 43016 | tf_op jit(solution)/shard_map/ppermute | solution.py:50
  22.5 2.0 %copy-start.1 = (bf16[1600,400]{0,1:T(8,128)(2,1)S(1)}, bf16[1600,400]{0,1:T(8,128)(2,1)}, u32[]{:S(2)}) copy-start(bf16[1600,400]{0,1:T(8,128)(2,1)} %param.38) | copy-start | bytes 3840004
  22.6 7.2 %copy-start.11 = (f32[400]{0:T(512)S(1)}, f32[400]{0:T(512)}, u32[]{:S(2)}) copy-start(f32[400]{0:T(512)} %param.40) | copy-start | bytes 4804
  22.6 7.2 %copy-start.12 = (f32[400]{0:T(512)S(1)}, f32[400]{0:T(512)}, u32[]{:S(2)}) copy-start(f32[400]{0:T(512)} %param.41) | copy-start | bytes 4804
  25.4 3.2 %collective-permute-start.12 = (bf16[4,1664]{1,0:T(4,128)(2,1)S(1)}, bf16[4,1664]{1,0:T(4,128)(2,1)S(1)}, u32[]{:S(2)}, u32[]{:S(2)}) collective-permute-start(bf16[4,1664]{1,0:T(4,128)(2,1)S(1)} %get-tuple-element.41.refs_0_), channel_id=1, source_target_pairs={{0,3},{1,2},{2,1},{3,0},{4,7},{5,6},{6,5},{7,4},{8,11},{9,10},{10,... | collective-permute-start | bytes 39944 | tf_op jit(solution)/shard_map/ppermute | solution.py:50
  25.9 3.8 %collective-permute-start.13 = (bf16[4,1664]{1,0:T(4,128)(2,1)S(1)}, bf16[4,1664]{1,0:T(4,128)(2,1)S(1)}, u32[]{:S(2)}, u32[]{:S(2)}) collective-permute-start(bf16[4,1664]{1,0:T(4,128)(2,1)S(1)} %get-tuple-element.41.refs_0_), channel_id=1, source_target_pairs={{0,2},{1,3},{2,0},{3,1},{4,6},{5,7},{6,4},{7,5},{8,10},{9,11},{10,... | collective-permute-start | bytes 39944 | tf_op jit(solution)/shard_map/ppermute | solution.py:50
  27.3 2.4 %collective-permute-start.14 = (bf16[4,1664]{1,0:T(4,128)(2,1)S(1)}, bf16[4,1664]{1,0:T(4,128)(2,1)S(1)}, u32[]{:S(2)}, u32[]{:S(2)}) collective-permute-start(bf16[4,1664]{1,0:T(4,128)(2,1)S(1)} %get-tuple-element.41.refs_0_), channel_id=1, source_target_pairs={{0,1},{1,0},{2,3},{3,2},{4,5},{5,4},{6,7},{7,6},{8,9},{9,8},{10,11... | collective-permute-start | bytes 39944 | tf_op jit(solution)/shard_map/ppermute | solution.py:50

commit v8 on v7

--- a/solution.py
+++ b/solution.py
@@ -150,13 +150,13 @@
 
 
 def prepare(
-    source_ref, lengths_ref, gain_ref, conv_w_ref, conv_b_ref, conv_rows_ref, heads_ref, xproj_ref, xz_ref,
-    chosen_ref, live_ref, base_ref, new_conv_ref, gain_out, heads_out, xproj_out, in_out,
-    source, lengths, gain, conv_w, conv_b, conv_rows, sems, *, size,
+    source_ref, gain_ref, conv_w_ref, conv_b_ref, conv_rows_ref, heads_ref, xproj_ref, xz_ref,
+    chosen_ref, base_ref, new_conv_ref, gain_out, heads_out, xproj_out, in_out,
+    source, gain, conv_w, conv_b, conv_rows, sems, *, size,
 ):
     rows = source.shape[0]
     small = (
-        (source_ref, source), (lengths_ref, lengths), (gain_ref, gain), (conv_w_ref, conv_w), (conv_b_ref, conv_b),
+        (source_ref, source), (gain_ref, gain), (conv_w_ref, conv_w), (conv_b_ref, conv_b),
         (conv_rows_ref, conv_rows),
     )
     copies = copies_of(
@@ -176,7 +176,6 @@
         wanted = jnp.where(row_id == r, entry * rows + lax.rem(source[r], rows), wanted)
     chosen = lax.broadcasted_iota(jnp.int32, (8, slots), 1) == wanted
     chosen_ref[...] = jnp.where(chosen, 1.0, 0.0)
-    live_ref[...] = live_slots(lengths, live_ref.shape[1], me)
     gain_out[...] = gain[...][None]
     taps = conv_rows.shape[0]
     base = conv_b[...]
@@ -189,6 +188,13 @@
     new_conv_ref[taps - 1] = jnp.zeros_like(conv_rows[0])
     for copy in copies[len(small) :]:
         copy.wait()
+
+
+def mark_live(lengths_ref, live_ref, lengths, sem):
+    copy = pltpu.make_async_copy(lengths_ref, lengths, sem)
+    copy.start()
+    copy.wait()
+    live_ref[...] = live_slots(lengths, live_ref.shape[1], lax.axis_index("narrow"))
 
 
 def project_in(*refs, size):
@@ -481,7 +487,7 @@
 
     wide = lax.axis_size("wide")
     large = (query_key_value_weight.T, w_xproj.T, w_xz.transpose(1, 2, 0))
-    small = (source, lengths, norm_gain, conv_weight, conv_bias[None], conv_state.transpose(1, 0, 2))
+    small = (source, norm_gain, conv_weight, conv_bias[None], conv_state.transpose(1, 0, 2))
     slots = rows * entries_of(wide)
     half = large[2].shape[1:]
     pinned = [pltpu.with_memory_space_constraint(a, pltpu.HBM) for a in small + large]
@@ -489,26 +495,25 @@
     prepared = pl.pallas_call(
         functools.partial(prepare, size=wide),
         in_specs=[anywhere] * len(pinned),
-        out_specs=[VMEM] * 8,
+        out_specs=[VMEM] * 7,
         out_shape=[
             pltpu.VMEM((8, slots), F32),
-            pltpu.VMEM((8, cached_key_rows.shape[1]), F32),
             pltpu.VMEM((2 * rows, cols), F32),
-            pltpu.VMEM(small[5].shape, BF16),
+            pltpu.VMEM(small[4].shape, BF16),
             pltpu.VMEM((1, MODEL_WIDTH), F32),
             pltpu.VMEM(large[0].shape, BF16),
             pltpu.VMEM(large[1].shape, BF16),
             pltpu.VMEM(half, BF16),
         ],
-        scratch_shapes=[pltpu.SMEM(a.shape, jnp.int32) for a in small[:2]]
-        + [pltpu.VMEM(a.shape, a.dtype) for a in small[2:]]
+        scratch_shapes=[pltpu.SMEM(a.shape, jnp.int32) for a in small[:1]]
+        + [pltpu.VMEM(a.shape, a.dtype) for a in small[1:]]
         + [pltpu.SemaphoreType.DMA((7 + 2 * (PARTS + 1),))],
         compiler_params=pltpu.CompilerParams(vmem_limit_bytes=4 * 1024 * 1024),
     )(*pinned)
     arrived = gather_xor(tokens, "wide", "narrow", prepared[:1])
     other_w = swap(large[0], 1)
     part_width = 2 * head_width + w_xproj.shape[1]
-    chosen, live, base, old_conv, *weights = prepared
+    chosen, base, old_conv, *weights = prepared
     part, state, act, normed, channel_in, routed = call(
         functools.partial(project_in, size=len(arrived)),
         (),
@@ -523,6 +528,18 @@
         ),
     )
     far = swap(part, 2)
+
+    def mark(after_ref, *refs):
+        mark_live(*refs)
+
+    live = pl.pallas_call(
+        mark,
+        in_specs=[anywhere] * 2,
+        out_specs=VMEM,
+        out_shape=pltpu.VMEM((8, cached_key_rows.shape[1]), F32),
+        scratch_shapes=[pltpu.SMEM(lengths.shape, jnp.int32), pltpu.SemaphoreType.DMA(())],
+        compiler_params=pltpu.CompilerParams(vmem_limit_bytes=4 * 1024 * 1024),
+    )(normed, pltpu.with_memory_space_constraint(lengths, pltpu.HBM))
     states = [state, swap(state, 1), swap(state, 3)]
     second, key_value = call(
         functools.partial(attend, head_width=head_width),

time: 30.7 us -> 30.7 us (level)
  waiting for transfers between devices: 5.86 us -> 5.16 us
  Pallas kernels: 7.81 us -> 8.5 us
    ppermute x10, waiting for transfers between devices: 4.47 us -> 3.77 us  [swap(): return lax.ppermute(part, 'narrow', [(i, i ^ step) for i in range(size)])]
    pallas_call x0 -> x1, Pallas kernels: none -> 0.69 us  [shards(): pl.pallas_call(mark, in_specs=[anywhere] * 2, out_specs=VMEM, out_shape=p...]
  transfers between devices with their start and end apart: 15 -> 15, of which waited for: 8 -> 8; matrix products, arithmetic and copies ran while one was open for 0% -> 0% of each run, Pallas kernels for 15% -> 17%
where the time goes in v8:
time: 30.7 us; the launch traced here: 30.5 us
  starting transfers between devices  15.9 us (52%)
  Pallas kernels  8.5 us (28%)
  waiting for transfers between devices  5.16 us (17%)
  between operations  0.85 us (3%)
    ppermute x10, starting transfers between devices, swap(): return lax.ppermute(part, 'narrow', [(i, i ^ step) for i in range(size)])  6.5 us
    pallas_call x7, Pallas kernels, call(): pl.pallas_call(run, in_specs=[pl.BlockSpec(memory_space=pl.ANY)] * len(af...  5.72 us
    ppermute x2, starting transfers between devices, fetch(): return lax.ppermute(held, (axis, core_axis), moves)  4.59 us
    ppermute x10, waiting for transfers between devices, swap(): return lax.ppermute(part, 'narrow', [(i, i ^ step) for i in range(size)])  3.77 us
    ppermute x1, starting transfers between devices, gather_xor(): lax.ppermute(held, axis, [(i, i ^ step << place) for i in range(size)])  2.59 us
    pallas_call x1, Pallas kernels, shards(): pl.pallas_call(functools.partial(prepare, size=wide), in_specs=[anywhere]...  2.09 us
    ppermute x1, starting transfers between devices, gather_xor(): lax.ppermute(near, core_axis, [(c, c - 1) for c in range(1, cores, 2)])  1.28 us
    ppermute x1, starting transfers between devices, gather_xor(): far_swap = lax.ppermute(far, core_axis, [(c, c ^ 1) for c in range(cores)])  0.9 us
  transfers between devices with their start and end apart: 15, of which 8 were waited for; matrix products, arithmetic and copies ran while one was open for 0% of the time, Pallas kernels for 17%

profile of v8, /device:TPU:0, one launch (start us, length us, event | category | flops | bytes accessed | tf_op | source)
XLA Modules:
  0.0 30.5 jit_solution(6535680259006663761)
XLA Ops:
  0.6 0.5 %collective-permute-start.5 = (bf16[560,1600]{1,0:T(8,128)(2,1)}, bf16[560,1600]{1,0:T(8,128)(2,1)S(1)}, u32[]{:S(2)}, u32[]{:S(2)}) collective-permute-start(bf16[560,1600]{1,0:T(8,128)(2,1)} %bitcast.27), channel_id=1, source_target_pairs={{0,1},{1,0},{2,3},{3,2},{4,5},{5,4},{6,7},{7,6},{8,9},{9,8},{10,11... | collective-permute-start | bytes 5376008 | tf_op jit(solution)/shard_map/ppermute | solution.py:50
  1.2 2.6 %collective-permute-start = (bf16[1,4,1600]{2,1,0:T(4,128)(2,1)}, bf16[1,4,1600]{2,1,0:T(4,128)(2,1)S(1)}, u32[]{:S(2)}, u32[]{:S(2)}) collective-permute-start(bf16[1,4,1600]{2,1,0:T(4,128)(2,1)} %bitcast.21), channel_id=1, source_target_pairs={{0,4},{4,0},{8,12},{12,8},{16,20},{20,16},{24,28},{28,24},{1,5},{5... | collective-permute-start | bytes 38408 | tf_op jit(solution)/shard_map/ppermute | solution.py:93
  3.7 2.1 %shard_map.228 = (f32[8,40]{1,0:T(8,128)S(1)}, f32[8,400]{1,0:T(8,128)S(1)}, bf16[3,4,400]{2,1,0:T(4,128)(2,1)S(1)}, f32[1,1600]{1,0:T(1,128)S(1)}, bf16[560,160...) custom-call(s32[4]{0:T(128)} %source_ref.1, f32[1600]{0:T(1024)} %gain_ref.1, ...), custom_call_target="tpu_custom_call" | custom-call | tf_op jit(solution)/shard_map/pallas_call | solution.py:495
  5.9 0.7 %collective-permute-start.1 = (bf16[2,4,1600]{2,1,0:T(4,128)(2,1)S(1)}, bf16[2,4,1600]{2,1,0:T(4,128)(2,1)S(1)}, u32[]{:S(2)}, u32[]{:S(2)}) collective-permute-start(bf16[2,4,1600]{2,1,0:T(4,128)(2,1)S(1)} %shard_map.229.refs_0_), channel_id=1, source_target_pairs={{1,9},{3,11},{5,13},{7,15},{9,1},{11,3},{13,5},{15,7},{17,25},{19,... | collective-permute-start | bytes 76808 | tf_op jit(solution)/shard_map/ppermute | solution.py:85
  6.6 3.9 %collective-permute-start.3 = (bf16[2,4,1600]{2,1,0:T(4,128)(2,1)S(1)}, bf16[2,4,1600]{2,1,0:T(4,128)(2,1)S(1)}, u32[]{:S(2)}, u32[]{:S(2)}) collective-permute-start(bf16[2,4,1600]{2,1,0:T(4,128)(2,1)S(1)} %shard_map.229.refs_0_), channel_id=1, source_target_pairs={{0,24},{1,17},{2,26},{3,19},{4,28},{5,21},{6,30},{7,23},{8,16},{9,... | collective-permute-start | bytes 76808 | tf_op jit(solution)/shard_map/ppermute | solution.py:85
  10.5 1.3 %collective-permute-start.2 = (bf16[2,4,1600]{2,1,0:T(4,128)(2,1)S(1)}, bf16[2,4,1600]{2,1,0:T(4,128)(2,1)S(1)}, u32[]{:S(2)}, u32[]{:S(2)}) collective-permute-start(bf16[2,4,1600]{2,1,0:T(4,128)(2,1)S(1)} %collective-permute-done.1.refs_1_), channel_id=1, source_target_pairs={{1,0},{3,2},{5,4},{7,6},{9,8},{11,10},{13,12},{15,14},{17,16},{19,... | collective-permute-start | bytes 76808 | tf_op jit(solution)/shard_map/ppermute | solution.py:88
  11.8 0.5 %collective-permute-done.3.refs_3_ = bf16[2,4,1600]{2,1,0:T(4,128)(2,1)S(1)} collective-permute-done((bf16[2,4,1600]{2,1,0:T(4,128)(2,1)S(1)}, bf16[2,4,1600]{2,1,0:T(4,128)(2,1)S(1)}, u32[]{:S(2)}, u32[]{:S(2)}) %collective-permute-start.3) | collective-permute-done | bytes 25632 | tf_op jit(solution)/shard_map/ppermute | solution.py:85
  12.3 0.9 %collective-permute-start.4 = (bf16[2,4,1600]{2,1,0:T(4,128)(2,1)S(1)}, bf16[2,4,1600]{2,1,0:T(4,128)(2,1)S(1)}, u32[]{:S(2)}, u32[]{:S(2)}) collective-permute-start(bf16[2,4,1600]{2,1,0:T(4,128)(2,1)S(1)} %collective-permute-done.3.refs_3_), channel_id=1, source_target_pairs={{0,1},{1,0},{2,3},{3,2},{4,5},{5,4},{6,7},{7,6},{8,9},{9,8},{10,11... | collective-permute-start | bytes 76808 | tf_op jit(solution)/shard_map/ppermute | solution.py:89
  13.2 0.4 %collective-permute-done.2.refs_2_ = bf16[2,4,1600]{2,1,0:T(4,128)(2,1)S(1)} collective-permute-done((bf16[2,4,1600]{2,1,0:T(4,128)(2,1)S(1)}, bf16[2,4,1600]{2,1,0:T(4,128)(2,1)S(1)}, u32[]{:S(2)}, u32[]{:S(2)}) %collective-permute-start.2) | collective-permute-done | bytes 25632 | tf_op jit(solution)/shard_map/ppermute | solution.py:88
  13.6 0.5 %collective-permute-done.4.refs_4_ = bf16[2,4,1600]{2,1,0:T(4,128)(2,1)S(1)} collective-permute-done((bf16[2,4,1600]{2,1,0:T(4,128)(2,1)S(1)}, bf16[2,4,1600]{2,1,0:T(4,128)(2,1)S(1)}, u32[]{:S(2)}, u32[]{:S(2)}) %collective-permute-start.4) | collective-permute-done | bytes 25632 | tf_op jit(solution)/shard_map/ppermute | solution.py:89
  14.1 0.0 copy-start.7
  14.1 1.7 %shard_map.230 = (f32[4,1252]{1,0:T(4,128)S(1)}, f32[4,132]{1,0:T(4,128)S(1)}, f32[4,400]{1,0:T(4,128)S(1)}, bf16[8,1600]{1,0:T(8,128)(2,1)S(1)}, f32[4,400]{1,0:T(4,128)S(1)}, /*index=5*/f32[8,1600]{1,0:T(8,128)S(1)}) custom-call(bf16[2,4,1600]{2,1,0:T(4,128)(2,1)S(1)} %shard_map.229.refs_0_, bf16[2,4,1600]{2,1,0:T(4,128)(2,1)S(1)} %collective-permute-done.1.refs_1_, ...), custom_call_target="tpu_custom_call" | custom-call | tf_op jit(solution)/shard_map/pallas_call | solution.py:447
  15.9 1.5 %collective-permute-start.6 = (f32[4,1252]{1,0:T(4,128)S(1)}, f32[4,1252]{1,0:T(4,128)S(1)}, u32[]{:S(2)}, u32[]{:S(2)}) collective-permute-start(f32[4,1252]{1,0:T(4,128)S(1)} %get-tuple-element.33.refs_0_), channel_id=1, source_target_pairs={{0,2},{1,3},{2,0},{3,1},{4,6},{5,7},{6,4},{7,5},{8,10},{9,11},{10,... | collective-permute-start | bytes 60104 | tf_op jit(solution)/shard_map/ppermute | solution.py:50
  17.4 0.1 collective-permute-start.10
  17.5 0.6 %collective-permute-start.11 = (f32[4,132]{1,0:T(4,128)S(1)}, f32[4,132]{1,0:T(4,128)S(1)}, u32[]{:S(2)}, u32[]{:S(2)}) collective-permute-start(f32[4,132]{1,0:T(4,128)S(1)} %get-tuple-element.36.refs_1_), channel_id=1, source_target_pairs={{0,3},{1,2},{2,1},{3,0},{4,7},{5,6},{6,5},{7,4},{8,11},{9,10},{10,... | collective-permute-start | bytes 6344 | tf_op jit(solution)/shard_map/ppermute | solution.py:50
  18.0 0.7 %shard_map.231.refs_2_ = f32[8,256]{1,0:T(8,128)S(1)} custom-call(bf16[8,1600]{1,0:T(8,128)(2,1)S(1)} %get-tuple-element.34.after_ref.refs_4_, s32[4]{0:T(128)} %refs_0_.1), custom_call_target="tpu_custom_call" | custom-call | tf_op jit(solution)/shard_map/pallas_call | solution.py:535
  18.7 0.9 %collective-permute-done.6.refs_1_.refs_0_ = f32[4,1252]{1,0:T(4,128)S(1)} collective-permute-done((f32[4,1252]{1,0:T(4,128)S(1)}, f32[4,1252]{1,0:T(4,128)S(1)}, u32[]{:S(2)}, u32[]{:S(2)}) %collective-permute-start.6) | collective-permute-done | bytes 20064 | tf_op jit(solution)/shard_map/ppermute | solution.py:50
  19.7 0.8 %shard_map.232 = (bf16[4,1792]{1,0:T(4,128)(2,1)S(1)}, f32[4,640]{1,0:T(4,128)S(1)}) custom-call(f32[4,1252]{1,0:T(4,128)S(1)} %get-tuple-element.33.refs_0_, f32[4,1252]{1,0:T(4,128)S(1)} %collective-permute-done.6.refs_1_.refs_0_, f32[8,256]{1,0:T(8,128)S(1)} %shard_map.231.refs_2_, bf16[4,320,256]{2,1,0:T(8,128)(2,1)S(1)} %bitcast.18, ...), custom_call_target="tpu_custom_call" | custom-call | tf_op jit(solution)/shard_map/pallas_call | solution.py:447
  20.5 0.3 %collective-permute-start.7 = (bf16[4,1792]{1,0:T(4,128)(2,1)S(1)}, bf16[4,1792]{1,0:T(4,128)(2,1)S(1)}, u32[]{:S(2)}, u32[]{:S(2)}) collective-permute-start(bf16[4,1792]{1,0:T(4,128)(2,1)S(1)} %get-tuple-element.35.refs_0_), channel_id=1, source_target_pairs={{0,3},{1,2},{2,1},{3,0},{4,7},{5,6},{6,5},{7,4},{8,11},{9,10},{10,... | collective-permute-start | bytes 43016 | tf_op jit(solution)/shard_map/ppermute | solution.py:50
  20.9 1.3 %collective-permute-start.8 = (bf16[4,1792]{1,0:T(4,128)(2,1)S(1)}, bf16[4,1792]{1,0:T(4,128)(2,1)S(1)}, u32[]{:S(2)}, u32[]{:S(2)}) collective-permute-start(bf16[4,1792]{1,0:T(4,128)(2,1)S(1)} %get-tuple-element.35.refs_0_), channel_id=1, source_target_pairs={{0,2},{1,3},{2,0},{3,1},{4,6},{5,7},{6,4},{7,5},{8,10},{9,11},{10,... | collective-permute-start | bytes 43016 | tf_op jit(solution)/shard_map/ppermute | solution.py:50
  22.2 0.2 collective-permute-start.9
  22.6 0.9 %shard_map.233 = (bf16[4,1600]{1,0:T(4,128)(2,1)S(1)}, f32[4,16,400]{2,1,0:T(8,128)S(1)}) custom-call(f32[4,1252]{1,0:T(4,128)S(1)} %collective-permute-done.6.refs_1_.refs_0_, f32[4,132]{1,0:T(4,128)S(1)} %get-tuple-element.36.refs_1_, f32[4,132]{1,0:T(4,128)S(1)} %collective-permute-done.10.refs_2_, f32[4,132]{1,0:T(4,128)S(1)} %collective-permute-done.11.refs_3_, ...), custom_call_target="tpu_custom_call" | custom-call | tf_op jit(solution)/shard_map/pallas_call | solution.py:447
  23.5 0.3 collective-permute-done.7.refs_1_
  23.8 0.8 %collective-permute-done.8.refs_2_ = bf16[4,1792]{1,0:T(4,128)(2,1)S(1)} collective-permute-done((bf16[4,1792]{1,0:T(4,128)(2,1)S(1)}, bf16[4,1792]{1,0:T(4,128)(2,1)S(1)}, u32[]{:S(2)}, u32[]{:S(2)}) %collective-permute-start.8) | collective-permute-done | bytes 14368 | tf_op jit(solution)/shard_map/ppermute | solution.py:50
  24.6 0.9 %shard_map.234 = (f32[4,400]{1,0:T(4,128)S(1)}, bf16[4,1664]{1,0:T(4,128)(2,1)S(1)}) custom-call(bf16[4,1792]{1,0:T(4,128)(2,1)S(1)} %get-tuple-element.35.refs_0_, bf16[4,1792]{1,0:T(4,128)(2,1)S(1)} %collective-permute-done.7.refs_1_, bf16[4,1792]{1,0:T(4,128)(2,1)S(1)} %collective-permute-done.8.refs_2_, ...), custom_call_target="tpu_custom_call" | custom-call | tf_op jit(solution)/shard_map/pallas_call | solution.py:447
  25.4 0.5 %collective-permute-start.12 = (bf16[4,1664]{1,0:T(4,128)(2,1)S(1)}, bf16[4,1664]{1,0:T(4,128)(2,1)S(1)}, u32[]{:S(2)}, u32[]{:S(2)}) collective-permute-start(bf16[4,1664]{1,0:T(4,128)(2,1)S(1)} %get-tuple-element.39.refs_0_), channel_id=1, source_target_pairs={{0,3},{1,2},{2,1},{3,0},{4,7},{5,6},{6,5},{7,4},{8,11},{9,10},{10,... | collective-permute-start | bytes 39944 | tf_op jit(solution)/shard_map/ppermute | solution.py:50
  25.9 1.4 %collective-permute-start.13 = (bf16[4,1664]{1,0:T(4,128)(2,1)S(1)}, bf16[4,1664]{1,0:T(4,128)(2,1)S(1)}, u32[]{:S(2)}, u32[]{:S(2)}) collective-permute-start(bf16[4,1664]{1,0:T(4,128)(2,1)S(1)} %get-tuple-element.39.refs_0_), channel_id=1, source_target_pairs={{0,2},{1,3},{2,0},{3,1},{4,6},{5,7},{6,4},{7,5},{8,10},{9,11},{10,... | collective-permute-start | bytes 39944 | tf_op jit(solution)/shard_map/ppermute | solution.py:50
  27.3 0.0 collective-permute-start.14
  27.3 0.7 %shard_map.235 = (bf16[3,4,400]{2,1,0:T(4,128)(2,1)}, bf16[4,640]{1,0:T(4,128)(2,1)}, f32[4,16,400]{2,1,0:T(8,128)}, f32[4,400]{1,0:T(4,128)S(1)}) custom-call(bf16[4,1664]{1,0:T(4,128)(2,1)S(1)} %get-tuple-element.39.refs_0_, f32[4,400]{1,0:T(4,128)S(1)} %get-tuple-element.41.refs_1_, bf16[3,4,400]{2,1,0:T(4,128)(2,1)S(1)} %get-tuple-element.42.refs_2_, ...), custom_call_target="tpu_custom_call" | custom-call | tf_op jit(solution)/shard_map/pallas_call | solution.py:447
  28.0 0.6 %collective-permute-done.12.refs_1_ = bf16[4,1664]{1,0:T(4,128)(2,1)S(1)} collective-permute-done((bf16[4,1664]{1,0:T(4,128)(2,1)S(1)}, bf16[4,1664]{1,0:T(4,128)(2,1)S(1)}, u32[]{:S(2)}, u32[]{:S(2)}) %collective-permute-start.12) | collective-permute-done | bytes 13344 | tf_op jit(solution)/shard_map/ppermute | solution.py:50
  28.6 1.1 %collective-permute-done.13.refs_2_ = bf16[4,1664]{1,0:T(4,128)(2,1)S(1)} collective-permute-done((bf16[4,1664]{1,0:T(4,128)(2,1)S(1)}, bf16[4,1664]{1,0:T(4,128)(2,1)S(1)}, u32[]{:S(2)}, u32[]{:S(2)}) %collective-permute-start.13) | collective-permute-done | bytes 13344 | tf_op jit(solution)/shard_map/ppermute | solution.py:50
  29.7 0.8 %shard_map.236 = bf16[4,400]{1,0:T(4,128)(2,1)} custom-call(bf16[4,1664]{1,0:T(4,128)(2,1)S(1)} %get-tuple-element.39.refs_0_, bf16[4,1664]{1,0:T(4,128)(2,1)S(1)} %collective-permute-done.12.refs_1_, bf16[4,1664]{1,0:T(4,128)(2,1)S(1)} %collective-permute-done.13.refs_2_, bf16[4,1664]{1,0:T(4,128)(2,1)S(1)} %collective-permute-done.14.refs_3_, ...), custom_call_target="tpu_custom_call" | custom-call | tf_op jit(solution)/shard_map/pallas_call | solution.py:447
  (36 shorter events, 0.1 us)
Async XLA Ops:
  0.6 13.4 %collective-permute-start.5 = (bf16[560,1600]{1,0:T(8,128)(2,1)}, bf16[560,1600]{1,0:T(8,128)(2,1)S(1)}, u32[]{:S(2)}, u32[]{:S(2)}) collective-permute-start(bf16[560,1600]{1,0:T(8,128)(2,1)} %bitcast.27), channel_id=1, source_target_pairs={{0,1},{1,0},{2,3},{3,2},{4,5},{5,4},{6,7},{7,6},{8,9},{9,8},{10,11... | collective-permute-start | bytes 5376008 | tf_op jit(solution)/shard_map/ppermute | solution.py:50
  1.2 4.7 %collective-permute-start = (bf16[1,4,1600]{2,1,0:T(4,128)(2,1)}, bf16[1,4,1600]{2,1,0:T(4,128)(2,1)S(1)}, u32[]{:S(2)}, u32[]{:S(2)}) collective-permute-start(bf16[1,4,1600]{2,1,0:T(4,128)(2,1)} %bitcast.21), channel_id=1, source_target_pairs={{0,4},{4,0},{8,12},{12,8},{16,20},{20,16},{24,28},{28,24},{1,5},{5... | collective-permute-start | bytes 38408 | tf_op jit(solution)/shard_map/ppermute | solution.py:93
  3.7 2.1 %copy-start.8 = (bf16[4,1600]{1,0:T(4,128)(2,1)S(1)}, bf16[4,1600]{1,0:T(4,128)(2,1)}, u32[]{:S(2)}) copy-start(bf16[4,1600]{1,0:T(4,128)(2,1)} %param.21) | copy-start | bytes 38404
  5.9 4.6 %collective-permute-start.1 = (bf16[2,4,1600]{2,1,0:T(4,128)(2,1)S(1)}, bf16[2,4,1600]{2,1,0:T(4,128)(2,1)S(1)}, u32[]{:S(2)}, u32[]{:S(2)}) collective-permute-start(bf16[2,4,1600]{2,1,0:T(4,128)(2,1)S(1)} %shard_map.229.refs_0_), channel_id=1, source_target_pairs={{1,9},{3,11},{5,13},{7,15},{9,1},{11,3},{13,5},{15,7},{17,25},{19,... | collective-permute-start | bytes 76808 | tf_op jit(solution)/shard_map/ppermute | solution.py:85
  6.6 5.8 %collective-permute-start.3 = (bf16[2,4,1600]{2,1,0:T(4,128)(2,1)S(1)}, bf16[2,4,1600]{2,1,0:T(4,128)(2,1)S(1)}, u32[]{:S(2)}, u32[]{:S(2)}) collective-permute-start(bf16[2,4,1600]{2,1,0:T(4,128)(2,1)S(1)} %shard_map.229.refs_0_), channel_id=1, source_target_pairs={{0,24},{1,17},{2,26},{3,19},{4,28},{5,21},{6,30},{7,23},{8,16},{9,... | collective-permute-start | bytes 76808 | tf_op jit(solution)/shard_map/ppermute | solution.py:85
  10.5 3.1 %collective-permute-start.2 = (bf16[2,4,1600]{2,1,0:T(4,128)(2,1)S(1)}, bf16[2,4,1600]{2,1,0:T(4,128)(2,1)S(1)}, u32[]{:S(2)}, u32[]{:S(2)}) collective-permute-start(bf16[2,4,1600]{2,1,0:T(4,128)(2,1)S(1)} %collective-permute-done.1.refs_1_), channel_id=1, source_target_pairs={{1,0},{3,2},{5,4},{7,6},{9,8},{11,10},{13,12},{15,14},{17,16},{19,... | collective-permute-start | bytes 76808 | tf_op jit(solution)/shard_map/ppermute | solution.py:88
  12.3 1.8 %collective-permute-start.4 = (bf16[2,4,1600]{2,1,0:T(4,128)(2,1)S(1)}, bf16[2,4,1600]{2,1,0:T(4,128)(2,1)S(1)}, u32[]{:S(2)}, u32[]{:S(2)}) collective-permute-start(bf16[2,4,1600]{2,1,0:T(4,128)(2,1)S(1)} %collective-permute-done.3.refs_3_), channel_id=1, source_target_pairs={{0,1},{1,0},{2,3},{3,2},{4,5},{5,4},{6,7},{7,6},{8,9},{9,8},{10,11... | collective-permute-start | bytes 76808 | tf_op jit(solution)/shard_map/ppermute | solution.py:89
  14.1 5.6 %copy-start.3 = (bf16[4,256,320]{1,2,0:T(8,128)(2,1)S(1)}, bf16[4,256,320]{1,2,0:T(8,128)(2,1)}, u32[]{:S(2)}) copy-start(bf16[4,256,320]{1,2,0:T(8,128)(2,1)} %param.24) | copy-start | bytes 1966084
  14.1 5.6 %copy-start.4 = (bf16[4,256,320]{1,2,0:T(8,128)(2,1)S(1)}, bf16[4,256,320]{1,2,0:T(8,128)(2,1)}, u32[]{:S(2)}) copy-start(bf16[4,256,320]{1,2,0:T(8,128)(2,1)} %param.25) | copy-start | bytes 1966084
  14.1 8.4 %copy-start = (bf16[1600,2,400]{0,2,1:T(8,128)(2,1)S(1)}, bf16[1600,2,400]{0,2,1:T(8,128)(2,1)}, u32[]{:S(2)}) copy-start(bf16[1600,2,400]{0,2,1:T(8,128)(2,1)} %param.30) | copy-start | bytes 7680004
  14.1 8.4 %copy-start.5 = (f32[4,16,400]{2,1,0:T(8,128)S(1)}, f32[4,16,400]{2,1,0:T(8,128)}, u32[]{:S(2)}) copy-start(f32[4,16,400]{2,1,0:T(8,128)} %refs_10_.1) | copy-start | bytes 307204
  14.1 8.4 %copy-start.6 = (bf16[100,400]{0,1:T(8,128)(2,1)S(1)}, bf16[100,400]{0,1:T(8,128)(2,1)}, u32[]{:S(2)}) copy-start(bf16[100,400]{0,1:T(8,128)(2,1)} %param.34) | copy-start | bytes 240004
  14.1 8.4 %copy-start.7 = (f32[16,400]{1,0:T(8,128)S(1)}, f32[16,400]{1,0:T(8,128)}, u32[]{:S(2)}) copy-start(f32[16,400]{1,0:T(8,128)} %refs_9_.1) | copy-start | bytes 76804
  14.1 8.4 %copy-start.9 = (f32[400]{0:T(512)S(1)}, f32[400]{0:T(512)}, u32[]{:S(2)}) copy-start(f32[400]{0:T(512)} %param.35) | copy-start | bytes 4804
  14.1 8.4 %copy-start.10 = (f32[400]{0:T(512)S(1)}, f32[400]{0:T(512)}, u32[]{:S(2)}) copy-start(f32[400]{0:T(512)} %param.37) | copy-start | bytes 4804
  15.9 6.7 %copy-start.2 = (bf16[400,1600]{1,0:T(8,128)(2,1)S(1)}, bf16[400,1600]{1,0:T(8,128)(2,1)}, u32[]{:S(2)}) copy-start(bf16[400,1600]{1,0:T(8,128)(2,1)} %refs_12_.1) | copy-start | bytes 3840004
  15.9 3.8 %collective-permute-start.6 = (f32[4,1252]{1,0:T(4,128)S(1)}, f32[4,1252]{1,0:T(4,128)S(1)}, u32[]{:S(2)}, u32[]{:S(2)}) collective-permute-start(f32[4,1252]{1,0:T(4,128)S(1)} %get-tuple-element.33.refs_0_), channel_id=1, source_target_pairs={{0,2},{1,3},{2,0},{3,1},{4,6},{5,7},{6,4},{7,5},{8,10},{9,11},{10,... | collective-permute-start | bytes 60104 | tf_op jit(solution)/shard_map/ppermute | solution.py:50
  17.4 5.1 %collective-permute-start.10 = (f32[4,132]{1,0:T(4,128)S(1)}, f32[4,132]{1,0:T(4,128)S(1)}, u32[]{:S(2)}, u32[]{:S(2)}) collective-permute-start(f32[4,132]{1,0:T(4,128)S(1)} %get-tuple-element.36.refs_1_), channel_id=1, source_target_pairs={{0,1},{1,0},{2,3},{3,2},{4,5},{5,4},{6,7},{7,6},{8,9},{9,8},{10,11... | collective-permute-start | bytes 6344 | tf_op jit(solution)/shard_map/ppermute | solution.py:50
  17.5 5.0 %collective-permute-start.11 = (f32[4,132]{1,0:T(4,128)S(1)}, f32[4,132]{1,0:T(4,128)S(1)}, u32[]{:S(2)}, u32[]{:S(2)}) collective-permute-start(f32[4,132]{1,0:T(4,128)S(1)} %get-tuple-element.36.refs_1_), channel_id=1, source_target_pairs={{0,3},{1,2},{2,1},{3,0},{4,7},{5,6},{6,5},{7,4},{8,11},{9,10},{10,... | collective-permute-start | bytes 6344 | tf_op jit(solution)/shard_map/ppermute | solution.py:50
  20.5 3.3 %collective-permute-start.7 = (bf16[4,1792]{1,0:T(4,128)(2,1)S(1)}, bf16[4,1792]{1,0:T(4,128)(2,1)S(1)}, u32[]{:S(2)}, u32[]{:S(2)}) collective-permute-start(bf16[4,1792]{1,0:T(4,128)(2,1)S(1)} %get-tuple-element.35.refs_0_), channel_id=1, source_target_pairs={{0,3},{1,2},{2,1},{3,0},{4,7},{5,6},{6,5},{7,4},{8,11},{9,10},{10,... | collective-permute-start | bytes 43016 | tf_op jit(solution)/shard_map/ppermute | solution.py:50
  20.9 3.7 %collective-permute-start.8 = (bf16[4,1792]{1,0:T(4,128)(2,1)S(1)}, bf16[4,1792]{1,0:T(4,128)(2,1)S(1)}, u32[]{:S(2)}, u32[]{:S(2)}) collective-permute-start(bf16[4,1792]{1,0:T(4,128)(2,1)S(1)} %get-tuple-element.35.refs_0_), channel_id=1, source_target_pairs={{0,2},{1,3},{2,0},{3,1},{4,6},{5,7},{6,4},{7,5},{8,10},{9,11},{10,... | collective-permute-start | bytes 43016 | tf_op jit(solution)/shard_map/ppermute | solution.py:50
  22.2 2.4 %collective-permute-start.9 = (bf16[4,1792]{1,0:T(4,128)(2,1)S(1)}, bf16[4,1792]{1,0:T(4,128)(2,1)S(1)}, u32[]{:S(2)}, u32[]{:S(2)}) collective-permute-start(bf16[4,1792]{1,0:T(4,128)(2,1)S(1)} %get-tuple-element.35.refs_0_), channel_id=1, source_target_pairs={{0,1},{1,0},{2,3},{3,2},{4,5},{5,4},{6,7},{7,6},{8,9},{9,8},{10,11... | collective-permute-start | bytes 43016 | tf_op jit(solution)/shard_map/ppermute | solution.py:50
  22.5 2.0 %copy-start.1 = (bf16[1600,400]{0,1:T(8,128)(2,1)S(1)}, bf16[1600,400]{0,1:T(8,128)(2,1)}, u32[]{:S(2)}) copy-start(bf16[1600,400]{0,1:T(8,128)(2,1)} %param.38) | copy-start | bytes 3840004
  22.6 7.2 %copy-start.11 = (f32[400]{0:T(512)S(1)}, f32[400]{0:T(512)}, u32[]{:S(2)}) copy-start(f32[400]{0:T(512)} %param.40) | copy-start | bytes 4804
  22.6 7.2 %copy-start.12 = (f32[400]{0:T(512)S(1)}, f32[400]{0:T(512)}, u32[]{:S(2)}) copy-start(f32[400]{0:T(512)} %param.41) | copy-start | bytes 4804
  25.4 3.2 %collective-permute-start.12 = (bf16[4,1664]{1,0:T(4,128)(2,1)S(1)}, bf16[4,1664]{1,0:T(4,128)(2,1)S(1)}, u32[]{:S(2)}, u32[]{:S(2)}) collective-permute-start(bf16[4,1664]{1,0:T(4,128)(2,1)S(1)} %get-tuple-element.39.refs_0_), channel_id=1, source_target_pairs={{0,3},{1,2},{2,1},{3,0},{4,7},{5,6},{6,5},{7,4},{8,11},{9,10},{10,... | collective-permute-start | bytes 39944 | tf_op jit(solution)/shard_map/ppermute | solution.py:50
  25.9 3.8 %collective-permute-start.13 = (bf16[4,1664]{1,0:T(4,128)(2,1)S(1)}, bf16[4,1664]{1,0:T(4,128)(2,1)S(1)}, u32[]{:S(2)}, u32[]{:S(2)}) collective-permute-start(bf16[4,1664]{1,0:T(4,128)(2,1)S(1)} %get-tuple-element.39.refs_0_), channel_id=1, source_target_pairs={{0,2},{1,3},{2,0},{3,1},{4,6},{5,7},{6,4},{7,5},{8,10},{9,11},{10,... | collective-permute-start | bytes 39944 | tf_op jit(solution)/shard_map/ppermute | solution.py:50
  27.3 2.4 %collective-permute-start.14 = (bf16[4,1664]{1,0:T(4,128)(2,1)S(1)}, bf16[4,1664]{1,0:T(4,128)(2,1)S(1)}, u32[]{:S(2)}, u32[]{:S(2)}) collective-permute-start(bf16[4,1664]{1,0:T(4,128)(2,1)S(1)} %get-tuple-element.39.refs_0_), channel_id=1, source_target_pairs={{0,1},{1,0},{2,3},{3,2},{4,5},{5,4},{6,7},{7,6},{8,9},{9,8},{10,11... | collective-permute-start | bytes 39944 | tf_op jit(solution)/shard_map/ppermute | solution.py:50
